TPU v7x, 256 devices: a whole 4x4x8 slice. The times are simulated.
256 devices in a mesh: leaf: 32 (over z, x), grp: 8 (over y, core).
Axes of the slice: x: 4, y: 4, z: 8, core: 2. Of those that a mesh axis runs over, the one named last changes fastest.
Arguments:
- hidden_states: bfloat16 [8, 4096, 2560], P('grp', 'leaf'), may hold values from -6 to 6
- query_rows: bfloat16 [8, 4096, 5120], P('grp', 'leaf'), may hold values from -170 to 170
- key_rows: bfloat16 [8, 4096, 512], P('grp', 'leaf'), may hold values from -7 to 7
- value_weight: bfloat16 [2560, 512], P(('leaf', 'grp')), may hold values from -0.125 to 0.125
- parent_links: int32 [8, 32], P('grp', 'leaf'), may hold values from -1 to 30, as said below
- out_grad: bfloat16 [8, 4096, 5120], P('grp', 'leaf'), may hold values from -6 to 6
Outputs:
- attended: bfloat16 [8, 4096, 5120], P('grp', 'leaf')
- query_grad: bfloat16 [8, 4096, 5120], P('grp', 'leaf')
- key_grad: bfloat16 [8, 4096, 512], P('grp', 'leaf')
- hidden_grad: bfloat16 [8, 4096, 2560], P('grp', 'leaf')
- weight_grad: float32 [2560, 512], P(('leaf', 'grp'))
Inputs may be any that keep to these rules, and one draw needn't show every extreme that they name: `parent_links`: entry 0 of each tree is -1 and every other entry names a lower index; no segment has more than 4 children, every segment is at most 3 steps from segment 0, and in every tree some segment is exactly 3 steps from it and segment 0 has exactly 4 children.
All inputs are finite; a program needn't handle non-finite values.
Results may differ from a plain program's by a relative error of at most 0.028.
Values may be sent and summed in bfloat16 or wider, within the bound.
No kernel may reach another device: no remote copies, remote signals or barrier semaphores. Data moves between devices by JAX's collectives and lax.ppermute only.
A program may use at most 128 MiB of HBM per device.

v0:
```python
import jax
import jax.numpy as jnp
from jax import lax
from jax.sharding import PartitionSpec as P

HQ = 40
HK = 4
DH = 128


def chain_slots(parent_list, own_index):
    total = parent_list.shape[0]

    def parent_of(node_index):
        hit = jnp.arange(total, dtype=jnp.int32) == node_index
        found = jnp.sum(jnp.where(hit, parent_list, 0))
        return jnp.where(node_index >= 0, found, -1)

    first = parent_of(own_index)
    second = parent_of(first)
    third = parent_of(second)
    return jnp.stack([first, second, third])


def key_mask(ancestors, segment_len):
    valid = jnp.concatenate([ancestors >= 0, jnp.ones((1,), bool)])
    block_ok = jnp.repeat(valid, segment_len)[None, :]
    row_ids = jnp.arange(segment_len, dtype=jnp.int32)[:, None]
    col_ids = jnp.arange(4 * segment_len, dtype=jnp.int32)[None, :]
    causal = (col_ids < 3 * segment_len) | (col_ids - 3 * segment_len <= row_ids)
    return block_ok & causal


def segment_pass(query_seg, key_all, value_all, grad_seg, visible):
    segment_len = query_seg.shape[0]
    groups = HQ // HK
    scale_factor = 1.0 / DH**0.5
    query_heads = query_seg.reshape(segment_len, HK, groups, DH)
    key_heads = key_all.reshape(-1, HK, DH)
    value_heads = value_all.reshape(-1, HK, DH)
    grad_heads = grad_seg.reshape(segment_len, HK, groups, DH)
    scores = (
        jnp.einsum("rhgd,khd->hgrk", query_heads, key_heads, preferred_element_type=jnp.float32)
        * scale_factor
    )
    scores = jnp.where(visible, scores, -1e30)
    row_max = jnp.max(scores, axis=-1, keepdims=True)
    weights_exp = jnp.where(visible, jnp.exp(scores - row_max), 0.0)
    probs = weights_exp / jnp.sum(weights_exp, axis=-1, keepdims=True)
    probs_low = probs.astype(jnp.bfloat16)
    output = jnp.einsum(
        "hgrk,khd->rhgd", probs_low, value_heads, preferred_element_type=jnp.float32
    )
    output = output.reshape(segment_len, HQ * DH).astype(jnp.bfloat16)
    dprobs = jnp.einsum(
        "rhgd,khd->hgrk", grad_heads, value_heads, preferred_element_type=jnp.float32
    )
    delta = jnp.sum(probs * dprobs, axis=-1, keepdims=True)
    dscores = (probs * (dprobs - delta)).astype(jnp.bfloat16)
    query_grad = (
        jnp.einsum("hgrk,khd->rhgd", dscores, key_heads, preferred_element_type=jnp.float32)
        * scale_factor
    )
    query_grad = query_grad.reshape(segment_len, HQ * DH).astype(jnp.bfloat16)
    key_part = (
        jnp.einsum("hgrk,rhgd->khd", dscores, query_heads, preferred_element_type=jnp.float32)
        * scale_factor
    )
    value_part = jnp.einsum(
        "hgrk,rhgd->khd", probs_low, grad_heads, preferred_element_type=jnp.float32
    )
    grad_term = jnp.concatenate(
        [key_part.reshape(-1, HK * DH), value_part.reshape(-1, HK * DH)], axis=1
    )
    return (output, query_grad, grad_term)


def shards(hidden_states, query_rows, key_rows, value_weight, parent_links, out_grad):
    hidden_local = hidden_states[0]
    query_local = query_rows[0]
    key_local = key_rows[0]
    grad_local = out_grad[0]
    segment_len = hidden_local.shape[0]
    key_width = key_local.shape[1]
    parent_list = lax.all_gather(parent_links, "leaf", axis=1, tiled=True)[0]
    own_index = lax.axis_index("leaf")
    ancestors = chain_slots(parent_list, own_index)
    columns = hidden_local
    values = jnp.dot(
        columns,
        lax.all_gather(value_weight, ("leaf", "grp"), axis=0, tiled=True),
        preferred_element_type=jnp.float32,
    )
    values = values.astype(jnp.bfloat16)
    key_value = jnp.concatenate([key_local, values], axis=1)
    every_segment = lax.all_gather(key_value, "leaf", axis=0, tiled=True)
    fetched = jnp.concatenate(
        [
            lax.dynamic_slice_in_dim(
                every_segment, jnp.maximum(ancestors[i], 0) * segment_len, segment_len, 0
            )
            for i in range(3)
        ],
        axis=0,
    )
    gathered = jnp.concatenate([fetched, key_value], axis=0)
    output, query_grad, grad_term = segment_pass(
        query_local,
        gathered[:, :key_width],
        gathered[:, key_width:],
        grad_local,
        key_mask(ancestors, segment_len),
    )
    grad_low = grad_term.astype(jnp.bfloat16)
    owners = jnp.concatenate([ancestors, own_index[None]])
    grad_wide = grad_low.astype(jnp.float32)
    targets = (
        owners[:, None] * segment_len + jnp.arange(segment_len, dtype=jnp.int32)[None, :]
    ).reshape(-1)
    keep_rows = (
        jnp.repeat(owners >= 0, segment_len)
        & (targets >= 0)
        & (targets < segment_len * lax.axis_size("leaf"))
    )
    targets = jnp.where(keep_rows, targets, segment_len * lax.axis_size("leaf"))
    sums = lax.psum_scatter(
        jnp.zeros((segment_len * lax.axis_size("leaf"), grad_wide.shape[1]), grad_wide.dtype)
        .at[targets]
        .add(grad_wide, mode="drop")
        .astype(jnp.bfloat16),
        "leaf",
        scatter_dimension=0,
        tiled=True,
    ).astype(jnp.float32)
    key_grad = sums[:, :key_width].astype(jnp.bfloat16)
    value_grad = sums[:, key_width:].astype(jnp.bfloat16)
    columns = hidden_local
    weight_grad = lax.psum_scatter(
        lax.dot_general(
            columns, value_grad, (((0,), (0,)), ((), ())), preferred_element_type=jnp.float32
        ),
        ("leaf", "grp"),
        scatter_dimension=0,
        tiled=True,
    )
    hidden_grad = lax.dot_general(
        value_grad,
        lax.all_gather(value_weight, ("leaf", "grp"), axis=0, tiled=True),
        (((1,), (1,)), ((), ())),
        preferred_element_type=jnp.float32,
    )
    hidden_grad = hidden_grad.astype(jnp.bfloat16)
    return (output[None], query_grad[None], key_grad[None], hidden_grad[None], weight_grad)


def solution(mesh):
    placed = (
        P("grp", "leaf", None),
        P("grp", "leaf", None),
        P("grp", "leaf", None),
        P(("leaf", "grp"), None),
        P("grp", "leaf"),
        P("grp", "leaf", None),
    )
    return jax.shard_map(
        shards,
        mesh=mesh,
        in_specs=placed,
        out_specs=(
            P("grp", "leaf", None),
            P("grp", "leaf", None),
            P("grp", "leaf", None),
            P("grp", "leaf", None),
            P(("leaf", "grp"), None),
        ),
        check_vma=False,
    )
```

profile of v0, /device:TPU:32, one launch (start us, length us, event | category | flops | bytes accessed | tf_op | source)
XLA Modules:
  0.0 806.2 jit_solution(11821311922020491470)
XLA Ops:
  7.2 0.7 all-gather.6.cloned.1.call-update
  8.0 120.3 %all-gather.6.cloned.1.call-done = bf16[256,10,512]{2,1,0:T(8,128)(2,1)} async-done(((bf16[1,10,512]{2,1,0:T(8,128)(2,1)}), bf16[256,10,512]{2,1,0:T(8,128)(2,1)}) %all-gather.6.cloned.1.call-update) | async-done | bytes 2621456 | tf_op jit(solution)/shard_map/all_gather | solution.py:91
  128.3 4.8 reshape.168
  133.1 0.5 convolution_convert_fusion.1
  133.7 0.7 pad_maximum_fusion
  135.1 0.6 dynamic-slice
  135.7 0.7 bitcast_dynamic-update-slice_fusion
  136.4 19.6 %all-reduce = s32[32]{0:T(128)S(1)} all-reduce(s32[32]{0:T(128)S(1)} %bitcast_dynamic-update-slice_fusion), channel_id=1, replica_groups=mesh['leaf'=32,'grp'=8] {'leaf'}, use_global_device_ids=true, to_apply=%add | all-reduce | flops 32 | bytes 256 | tf_op jit(solution)/shard_map/squeeze | solution.py:85
  156.0 0.6 fusion.43
  157.3 0.6 fusion.44
  158.6 0.6 fusion.45
  159.9 2.4 copy.45
  162.3 2.4 copy.50
  164.8 0.1 add_compare_fusion
  164.8 0.1 pad_add_fusion
  164.9 0.1 broadcast_compare_fusion
  165.1 0.1 iota_add_fusion
  165.2 0.9 fusion.38
  166.1 63.4 %all-gather.4.cloned.1.call-done = bf16[4096,1024]{1,0:T(8,128)(2,1)} async-done(((bf16[128,1024]{1,0:T(8,128)(2,1)}), bf16[4096,1024]{1,0:T(8,128)(2,1)}) %all-gather.4.cloned.1.call-update) | async-done | bytes 8388624 | tf_op jit(solution)/shard_map/all_gather | solution.py:96
  229.5 1.2 constant_dynamic-slice_fusion.2
  230.7 0.1 maximum_maximum_fusion
  230.8 1.0 fusion.48
  231.9 2.0 reshape.152
  233.8 2.1 copy.68
  236.0 2.0 reshape.151
  237.9 9.5 %fusion.49 = (f32[4,10,128]{2,1,0:T(8,128)S(1)}, f32[4,10,128,512]{2,3,1,0:T(8,128)}) fusion(pred[128,512]{0,1:T(8,128)(4,1)S(1)} %copy-done.5, bf16[512,4,128,1]{0,2,3,1:T(8,128)(2,1)} %copy.68, bf16[128,4,10,128]{0,3,2,1:T(8,128)(2,1)} %bitcast.104), kind=kOutput, calls=%fused_computation.77 | convolution fusion | flops 684196352 | bytes 12406784 | tf_op jit(solution)/shard_map/sub | solution.py:48
  247.4 6.9 fusion.24
  254.3 2.1 copy.58
  256.4 6.2 fusion.1
  262.6 0.8 slice-done.1
  263.4 0.6 slice-done.2
  264.0 3.2 fusion.3
  267.3 2.3 copy-done.1
  269.6 2.6 fusion.23
  272.2 2.0 copy.57
  274.2 12.4 %scatter_custom_fusion = f32[4096,1024]{1,0:T(8,128)} fusion(s32[512]{0:T(512)S(1)} %bitcast.117, f32[]{:T(128)} %constant.8.clone.1, bf16[512,512]{1,0:T(8,128)(2,1)} %copy.58, bf16[]{:T(256)} %constant.51, bf16[512,512]{1,0:T(8,128)(2,1)} %copy.57), kind=kCustom, calls=%fused_computation.9 | custom fusion | flops 2621440 | bytes 17825798 | tf_op jit(solution)/shard_map/scatter-add | solution.py:129
  286.6 9.1 %convert_element_type.64 = bf16[4096,1024]{1,0:T(8,128)(2,1)} convert(f32[4096,1024]{1,0:T(8,128)} %scatter_custom_fusion) | non-fusion elementwise | flops 4194304 | bytes 25165824 | tf_op jit(solution)/shard_map/convert_element_type | solution.py:130
  295.7 227.0 %reduce-scatter.3.cloned.1.call-done = bf16[128,1024]{1,0:T(8,128)(2,1)} async-done(((bf16[4096,1024]{1,0:T(8,128)(2,1)}), bf16[128,1024]{1,0:T(8,128)(2,1)}) %reduce-scatter.3.cloned.1.call-update) | async-done | bytes 262160 | tf_op jit(solution)/shard_map/reduce_scatter | solution.py:126
  522.7 4.1 convolution_bitcast_fusion
  526.8 6.3 fusion.16
  533.1 2.4 copy.59
  535.5 4.7 multiply_convert_fusion
  540.2 2.4 copy.60
  542.6 0.7 slice_bitcast_fusion
  543.3 1.8 fusion.10
  545.1 252.7 %all-reduce.4.cloned.1.call-done = f32[2560,512]{0,1:T(8,128)} async-done(((f32[2560,512]{0,1:T(8,128)}), f32[2560,512]{0,1:T(8,128)}) %all-reduce.4.cloned.1.call-update) | async-done | bytes 5242896
  797.8 1.2 constant_dynamic-slice_fusion.3
  799.0 0.7 copy.61
  (32 shorter events, 0.4 us)
Async XLA Ops:
  7.2 126.0 %copy-start = (bf16[1,128,2560]{2,1,0:T(8,128)(2,1)S(1)}, bf16[1,128,2560]{2,1,0:T(8,128)(2,1)}, u32[]{:S(2)}) copy-start(bf16[1,128,2560]{2,1,0:T(8,128)(2,1)} %param.6) | copy-start | bytes 1966084
  7.2 126.5 %copy-start.4 = (bf16[1,128,512]{2,1,0:T(8,128)(2,1)S(1)}, bf16[1,128,512]{2,1,0:T(8,128)(2,1)}, u32[]{:S(2)}) copy-start(bf16[1,128,512]{2,1,0:T(8,128)(2,1)} %param.8) | copy-start | bytes 393220
  7.2 121.1 %all-gather.6.cloned.1.call-start = ((), (), s32[]{:S(2)}) async-start(), calls=%async_computation.3 | async-start | bytes 4210688 | tf_op jit(solution)/shard_map/all_gather | solution.py:91
  7.9 127.2 %copy-start.6 = (u32[256]{0:T(256)S(1)}, u32[256]{0:T(256)}, u32[]{:S(2)}) copy-start(u32[256]{0:T(256)} %constant.44) | copy-start | bytes 3076
  7.9 221.6 %all-gather.4.cloned.1.call-start = ((), (), s32[]{:S(2)}) async-start(), calls=%async_computation.1 | async-start | bytes 8650752 | tf_op jit(solution)/shard_map/all_gather | solution.py:96
  134.4 388.3 %reduce-scatter.3.cloned.1.call-start = ((), (), s32[]{:S(2)}) async-start(), calls=%async_computation.2 | async-start | bytes 8650752 | tf_op jit(solution)/shard_map/reduce_scatter | solution.py:126
  230.8 7.1 copy-start.5
  256.4 6.2 slice-start
  256.4 7.0 slice-start.1
  256.4 7.6 slice-start.2
  264.0 5.6 copy-start.2
  267.3 2.3 copy-start.1
  295.7 502.1 %all-reduce.4.cloned.1.call-start = ((), (), s32[]{:S(2)}) async-start(), calls=%async_computation.4 | async-start | bytes 10485760
  535.5 7.1 copy-start.3
Sparse Core Ops, SparseCore 0:
  11.7 116.5 all-gather.5
  134.5 94.9 all-gather.3
  295.8 226.8 reduce-scatter.2
  528.9 268.8 all-reduce.3
where the time goes:
time: 810 us; the launch traced here: 806 us
  waiting for transfers between devices  664 us (82%)
  matrix products  42.6 us (5%)
  local copies, waits for them, and re-layouts  34.5 us (4%)
  other arithmetic  28.6 us (4%)
  blocking collectives  19.6 us (2%)
  between operations  16.6 us (2%)
    unnamed x5, waiting for transfers between devices  253 us
    reduce_scatter x1, waiting for transfers between devices, shards(): lax.psum_scatter(jnp.zeros((segment_len * lax.axis_size('leaf'), grad_wid...  227 us
    all_gather x1, waiting for transfers between devices, shards(): lax.all_gather(value_weight, ('leaf', 'grp'), axis=0, tiled=True)  120 us
    all_gather x1, waiting for transfers between devices, shards(): every_segment = lax.all_gather(key_value, 'leaf', axis=0, tiled=True)  63.4 us
    unnamed x31, local copies, waits for them, and re-layouts  21.4 us
    squeeze x1, blocking collectives, shards(): parent_list = lax.all_gather(parent_links, 'leaf', axis=1, tiled=True)[0]  19.6 us
  transfers between devices with their start and end apart: 4, of which 4 were waited for; matrix products, arithmetic and copies ran while one was open for 3% of the time, Pallas kernels for 0%

commit v1 on v0

v1 whole, which is shorter than its diff:
```python
import functools

import jax
import jax.numpy as jnp
from jax import lax
from jax.experimental import pallas as pl
from jax.experimental.pallas import tpu as pltpu
from jax.sharding import PartitionSpec as P

HQ = 40
HK = 4
DH = 128
GROUPS = HQ // HK
SLOTS = 3
TILE = 16
LOG2E = 1.4426950408889634
BF = jnp.bfloat16
F32 = jnp.float32
VMEM_LIMIT = 56 * 1024 * 1024


def ancestors_of(parents, node):
    first = parents[node]
    second = jnp.where(first >= 0, parents[jnp.maximum(first, 0)], -1)
    third = jnp.where(second >= 0, parents[jnp.maximum(second, 0)], -1)
    return (first, second, third)


def fetch_kernel(parents, held, sent):
    for node in range(sent.shape[0]):
        for slot, owner in enumerate(ancestors_of(parents, node)):
            sent[node, slot * TILE : (slot + 1) * TILE, :] = held[jnp.maximum(owner, 0), 0:TILE, :]


def add_up(parents, held, total):
    nodes = held.shape[0]
    total[...] = jnp.zeros_like(total)
    for node in range(nodes):
        for slot, owner in enumerate(ancestors_of(parents, node)):
            target = jnp.where(owner >= 0, owner, nodes)
            total[target] += held[node, slot * TILE : (slot + 1) * TILE, :].astype(F32)


def value_kernel(parents, held, sent, total):
    add_up(parents, held, total)
    for node in range(held.shape[0]):
        for slot, owner in enumerate(ancestors_of(parents, node)):
            sent[node, slot * TILE : (slot + 1) * TILE, :] = held[
                jnp.maximum(owner, 0), SLOTS * TILE : (SLOTS + 1) * TILE, :
            ]
        sent[node, SLOTS * TILE : (SLOTS + 1) * TILE, :] = total[node].astype(BF)


def key_kernel(parents, held, sent, total):
    add_up(parents, held, total)
    for node in range(held.shape[0]):
        sent[node] = total[node].astype(BF)


def whole(shape):
    return pl.BlockSpec(shape, lambda *_: (0,) * len(shape))


def route(kernel, parents, held, rows, with_total):
    nodes = held.shape[0]
    return pl.pallas_call(
        kernel,
        out_shape=jax.ShapeDtypeStruct((nodes, rows, DH), BF),
        in_specs=[
            pl.BlockSpec(memory_space=pltpu.SMEM),
            pl.BlockSpec(memory_space=pltpu.VMEM),
        ],
        out_specs=pl.BlockSpec(memory_space=pltpu.VMEM),
        scratch_shapes=[pltpu.VMEM((nodes + 1, TILE, DH), F32)] if with_total else [],
        compiler_params=pltpu.CompilerParams(vmem_limit_bytes=VMEM_LIMIT),
        cost_estimate=pl.CostEstimate(flops=0, bytes_accessed=2 * held.size * 2, transcendentals=0),
    )(parents, held)


def rows_of(pieces, own):
    parts = [
        pieces[:, 0, slot * TILE : (slot + 1) * TILE, :].reshape(-1, DH) for slot in range(SLOTS)
    ]
    return jnp.concatenate(parts + [own[...]], axis=0)


def put_rows(pieces, own, rows):
    seg = own.shape[0]
    for slot in range(SLOTS):
        block = rows[slot * seg : (slot + 1) * seg, :]
        pieces[:, 0, slot * TILE : (slot + 1) * TILE, :] = block.reshape(-1, TILE, DH).astype(BF)
    own[...] = rows[SLOTS * seg :, :].astype(BF)


def pair(block, index):
    return jnp.concatenate(
        [block[:, (2 * index + i) * DH : (2 * index + i + 1) * DH] for i in range(2)], axis=0
    )


def put_pair(block, index, rows):
    seg = block.shape[0]
    for i in range(2):
        block[:, (2 * index + i) * DH : (2 * index + i + 1) * DH] = rows[
            i * seg : (i + 1) * seg, :
        ].astype(BF)


def dot(lhs, rhs, left, right):
    return lax.dot_general(lhs, rhs, (((left,), (right,)), ((), ())), preferred_element_type=F32)


def probs_kernel(valid, query, grad, key_pieces, key_own, probs, value_pieces, value_own, bias):
    seg = query.shape[0]

    @pl.when(pl.program_id(0) == 0)
    def _():
        key_ids = lax.broadcasted_iota(jnp.int32, (seg, 2 * seg), 0)
        query_ids = lax.broadcasted_iota(jnp.int32, (seg, 2 * seg), 1) % seg
        for slot in range(SLOTS):
            level = jnp.where(valid[slot] >= 0, 0.0, -1e30).astype(F32)
            bias[slot * seg : (slot + 1) * seg, :] = jnp.full((seg, 2 * seg), level, F32)
        bias[SLOTS * seg :, :] = jnp.where(key_ids <= query_ids, 0.0, -1e30)

    keys = rows_of(key_pieces, key_own)
    total = jnp.zeros((keys.shape[0], DH), F32)
    for index in range(GROUPS // 2):
        scores = dot(keys, pair(query, index), 1, 1) * (LOG2E / DH**0.5) + bias[...]
        weight = jnp.exp2(scores - jnp.max(scores, axis=0, keepdims=True))
        prob = weight * (1.0 / jnp.sum(weight, axis=0, keepdims=True))
        probs[0, :, index * 2 * seg : (index + 1) * 2 * seg] = prob
        total += dot(prob.astype(BF), pair(grad, index), 1, 0)
    put_rows(value_pieces, value_own, total)


def grads_kernel(
    query, grad, probs, key_pieces, key_own, value_pieces, value_own,
    output, query_grad, grad_pieces, grad_own,
):
    seg = query.shape[0]
    keys = rows_of(key_pieces, key_own)
    values = rows_of(value_pieces, value_own)
    total = jnp.zeros((keys.shape[0], DH), F32)
    for index in range(GROUPS // 2):
        prob = probs[0, :, index * 2 * seg : (index + 1) * 2 * seg]
        dprob = dot(values, pair(grad, index), 1, 1)
        delta = jnp.sum(prob * dprob, axis=0, keepdims=True)
        dscore = (prob * (dprob - delta)).astype(BF)
        total += dot(dscore, pair(query, index), 1, 0)
        put_pair(output, index, dot(prob.astype(BF), values, 0, 0))
        put_pair(query_grad, index, dot(dscore, keys, 0, 0) * (1.0 / DH**0.5))
    put_rows(grad_pieces, grad_own, total * (1.0 / DH**0.5))


def attention(kernel, valid, arrays, outs, scratch, flops, transcendentals):
    def spec(shape):
        if len(shape) == 4:
            return pl.BlockSpec((shape[0], 1) + shape[2:], lambda h: (0, h, 0, 0))
        if len(shape) == 3:
            return pl.BlockSpec((1,) + shape[1:], lambda h: (h, 0, 0))
        return pl.BlockSpec((shape[0], shape[1] // HK), lambda h: (0, h))

    lead = [] if valid is None else [valid]
    moved = sum(a.size * a.dtype.itemsize for a in arrays) + sum(
        o.size * o.dtype.itemsize for o in outs
    )
    return pl.pallas_call(
        kernel,
        grid=(HK,),
        out_shape=outs,
        in_specs=[pl.BlockSpec(memory_space=pltpu.SMEM)] * len(lead)
        + [spec(a.shape) for a in arrays],
        out_specs=[spec(o.shape) for o in outs],
        scratch_shapes=scratch,
        compiler_params=pltpu.CompilerParams(vmem_limit_bytes=VMEM_LIMIT),
        cost_estimate=pl.CostEstimate(
            flops=flops, bytes_accessed=moved, transcendentals=transcendentals
        ),
    )(*lead, *arrays)


def to_pieces(rows):
    seg, width = rows.shape
    split = rows.reshape(seg // TILE, TILE, width // DH, DH).transpose(0, 2, 1, 3)
    return split.reshape(-1, TILE, DH)


def from_pieces(pieces):
    split = pieces.reshape(-1, HK, TILE, DH).transpose(0, 2, 1, 3)
    return split.reshape(-1, HK * DH)


def swap(array):
    return lax.all_to_all(array, "leaf", 0, 0, tiled=True)


def shards(n_leaf, n_grp, hidden_states, query_rows, key_rows, value_weight, parent_links, out_grad):
    hidden, query, keys, grad = hidden_states[0], query_rows[0], key_rows[0], out_grad[0]
    seg, width = keys.shape
    depth = hidden.shape[1]
    own_rows = value_weight.shape[0]
    blocks = seg // TILE
    shape = jax.ShapeDtypeStruct
    flops = 2 * seg * 4 * seg * DH * HQ

    columns = hidden.reshape(seg, n_leaf, n_grp, own_rows).transpose(0, 2, 1, 3).reshape(seg, depth)

    weight_rows = own_rows * width // DH
    pad = (-weight_rows) % TILE or TILE
    first = jnp.concatenate(
        [
            to_pieces(keys),
            jnp.broadcast_to(value_weight.reshape(1, weight_rows, DH), (n_leaf, weight_rows, DH)),
            jnp.broadcast_to(parent_links.astype(BF)[:, :, None], (n_leaf, pad, DH)),
        ],
        axis=1,
    )
    first = swap(first)
    parents = first[:, TILE + weight_rows, 0].astype(jnp.int32)
    weight = first[:, TILE : TILE + weight_rows, :].reshape(n_leaf * own_rows, width)
    weight = lax.all_gather(weight, "grp", axis=0, tiled=True)

    key_pieces = swap(route(fetch_kernel, parents, first[:, :TILE, :], SLOTS * TILE, False))
    key_pieces = key_pieces.reshape(blocks, HK, SLOTS * TILE, DH)
    valid = jnp.stack(ancestors_of(parents, lax.axis_index("leaf")))
    probs, value_terms, value_term_own = attention(
        probs_kernel,
        valid,
        [query, grad, key_pieces, keys],
        [
            shape((HK, 4 * seg, GROUPS * seg), F32),
            shape((blocks, HK, SLOTS * TILE, DH), BF),
            shape((seg, width), BF),
        ],
        [pltpu.VMEM((4 * seg, 2 * seg), F32)],
        2 * flops,
        HQ * seg * 4 * seg,
    )

    values = jnp.dot(columns, weight, preferred_element_type=F32).astype(BF)
    third = jnp.concatenate(
        [value_terms.reshape(-1, SLOTS * TILE, DH), to_pieces(values)], axis=1
    )
    third = swap(third)

    fourth = swap(route(value_kernel, parents, third, (SLOTS + 1) * TILE, True))
    value_grad = (
        from_pieces(fourth[:, SLOTS * TILE :, :]).astype(F32) + value_term_own.astype(F32)
    ).astype(BF)
    weight_part = dot(columns, value_grad, 0, 0).astype(BF)
    weight_part = lax.psum_scatter(weight_part, "grp", scatter_dimension=0, tiled=True)
    output, query_grad, key_terms, key_term_own = attention(
        grads_kernel,
        None,
        [
            query, grad, probs, key_pieces, keys,
            fourth.reshape(blocks, HK, (SLOTS + 1) * TILE, DH), values,
        ],
        [
            shape((seg, HQ * DH), BF),
            shape((seg, HQ * DH), BF),
            shape((blocks, HK, SLOTS * TILE, DH), BF),
            shape((seg, width), BF),
        ],
        [],
        4 * flops,
        0,
    )
    hidden_grad = dot(value_grad, weight, 1, 1).astype(BF)
    hidden_grad = hidden_grad.reshape(seg, n_grp, n_leaf, own_rows).transpose(0, 2, 1, 3)
    hidden_grad = hidden_grad.reshape(seg, depth)

    fifth = swap(key_terms.reshape(-1, SLOTS * TILE, DH))

    sixth = jnp.concatenate(
        [
            route(key_kernel, parents, fifth, TILE, True),
            weight_part.reshape(n_leaf, weight_rows, DH).astype(BF),
        ],
        axis=1,
    )
    sixth = swap(sixth)
    key_grad = (
        from_pieces(sixth[:, :TILE, :]).astype(F32) + key_term_own.astype(F32)
    ).astype(BF)
    weight_grad = jnp.sum(sixth[:, TILE:, :].astype(F32), axis=0).reshape(own_rows, width)
    return (output[None], query_grad[None], key_grad[None], hidden_grad[None], weight_grad)


def solution(mesh):
    rows = P("grp", "leaf", None)
    spread = P(("leaf", "grp"), None)
    return jax.shard_map(
        functools.partial(shards, mesh.shape["leaf"], mesh.shape["grp"]),
        mesh=mesh,
        in_specs=(rows, rows, rows, spread, P("grp", "leaf"), rows),
        out_specs=(rows, rows, rows, rows, spread),
        check_vma=False,
    )
```

time: 810 us -> 194 us (0.24)
  waiting for transfers between devices: 664 us -> 17.1 us
  blocking collectives: 19.6 us -> 89 us
  matrix products: 42.6 us -> 5.12 us
  Pallas kernels: 0 us -> 27.6 us
  other arithmetic: 28.6 us -> 6.24 us
  local copies, waits for them, and re-layouts: 34.5 us -> 14.7 us
  starting transfers between devices: 0.16 us -> 15.4 us
    unnamed x5 -> x2, waiting for transfers between devices: 253 us -> 0.03 us
    reduce_scatter x1, waiting for transfers between devices: 227 us -> 0.82 us  [shards(): lax.psum_scatter(weight_part, 'grp', scatter_dimension=0, tiled=True)]
    all_gather x2 -> x1, waiting for transfers between devices: 184 us -> 0.02 us  [shards(): weight = lax.all_gather(weight, 'grp', axis=0, tiled=True)]
    all_to_all x0 -> x4, blocking collectives: none -> 89 us  [swap(): return lax.all_to_all(array, 'leaf', 0, 0, tiled=True)]
    dot_general x8 -> x3, matrix products: 33.1 us -> 5.12 us  [the longest x2 2.76 us: dot(): lax.dot_general(lhs, rhs, (((left,), (right,)), ((), ())), preferred_elem...]
    pallas_call x0 -> x5, Pallas kernels: none -> 27.6 us  [the longest x2 21.3 us: attention(): pl.pallas_call(kernel, grid=(HK,), out_shape=outs, in_specs=[pl.BlockSpec...]
    squeeze x1 -> x0, blocking collectives: 19.6 us -> none  [shards(): parent_list = lax.all_gather(parent_links, 'leaf', axis=1, tiled=True)[0]]
    unnamed x31 -> x23, local copies, waits for them, and re-layouts: 21.4 us -> 4.85 us
  transfers between devices with their start and end apart: 4 -> 4, of which waited for: 4 -> 3; matrix products, arithmetic and copies ran while one was open for 3% -> 5% of each run, Pallas kernels for 0% -> 13%
where the time goes in v1:
time: 194 us; the launch traced here: 193 us
  blocking collectives  89 us (46%)
  Pallas kernels  27.6 us (14%)
  between operations  17.6 us (9%)
  waiting for transfers between devices  17.1 us (9%)
  starting transfers between devices  15.4 us (8%)
  local copies, waits for them, and re-layouts  14.7 us (8%)
  other arithmetic  6.24 us (3%)
  matrix products  5.12 us (3%)
    all_to_all x4, blocking collectives, swap(): return lax.all_to_all(array, 'leaf', 0, 0, tiled=True)  89 us
    pallas_call x2, Pallas kernels, attention(): pl.pallas_call(kernel, grid=(HK,), out_shape=outs, in_specs=[pl.BlockSpec...  21.3 us
    all_to_all x2, waiting for transfers between devices, swap(): return lax.all_to_all(array, 'leaf', 0, 0, tiled=True)  16.2 us
    all_to_all x2, starting transfers between devices, swap(): return lax.all_to_all(array, 'leaf', 0, 0, tiled=True)  15.3 us
    pallas_call x3, Pallas kernels, route(): pl.pallas_call(kernel, out_shape=jax.ShapeDtypeStruct((nodes, rows, DH),...  6.33 us
    unnamed x23, local copies, waits for them, and re-layouts  4.85 us
  transfers between devices with their start and end apart: 4, of which 3 were waited for; matrix products, arithmetic and copies ran while one was open for 5% of the time, Pallas kernels for 13%

profile of v1, /device:TPU:32, one launch (start us, length us, event | category | flops | bytes accessed | tf_op | source)
XLA Modules:
  0.0 192.7 jit_solution(12716524175419605807)
XLA Ops:
  7.2 0.7 broadcast_in_dim.24
  7.9 0.9 reshape_squeeze.6
  9.6 0.1 pad.9.clone
  9.7 0.2 maximum_maximum_fusion
  9.9 28.2 %all_to_all.30 = bf16[32,64,128]{2,1,0:T(8,128)(2,1)S(1)} all-to-all(bf16[32,64,128]{2,1,0:T(8,128)(2,1)S(1)} %maximum_maximum_fusion), channel_id=1, replica_groups=mesh['leaf'=32,'grp'=8] {'leaf'}, dimensions={0} | all-to-all | bytes 1048576 | tf_op jit(solution)/shard_map/all_to_all | solution.py:194
  38.2 0.9 reshape.74
  39.1 0.7 slice.25.held
  39.8 1.2 fusion.5.parents
  41.0 1.8 shard_map.101
  42.8 5.2 %all-to-all-start.1 = ((bf16[32,48,128]{2,1,0:T(8,128)(2,1)}), bf16[32,48,128]{2,1,0:T(8,128)(2,1)S(1)}, u32[]{:S(2)}, u32[]{:S(2)}) async-start(bf16[32,48,128]{2,1,0:T(8,128)(2,1)} %shard_map.101), calls=%async_computation.1 | async-start | bytes 786432 | tf_op jit(solution)/shard_map/all_to_all | solution.py:194
  48.1 0.3 copy.28
  48.4 0.2 reshape_squeeze.7
  48.6 0.2 copy.29
  48.8 0.2 reshape.75
  49.1 0.6 constant_dynamic-slice_fusion.2
  51.0 0.6 constant_dynamic-slice_fusion.1
  52.2 0.5 constant_dynamic-slice_fusion
  53.4 1.3 pad_add_fusion.valid
  54.7 7.1 %all-to-all-done.1 = bf16[32,48,128]{2,1,0:T(8,128)(2,1)S(1)} async-done(((bf16[32,48,128]{2,1,0:T(8,128)(2,1)}), bf16[32,48,128]{2,1,0:T(8,128)(2,1)S(1)}, u32[]{:S(2)}, u32[]{:S(2)}) %all-to-all-start.1) | async-done | bytes 393248 | tf_op jit(solution)/shard_map/all_to_all | solution.py:194
  61.8 0.8 copy-done.4
  62.6 8.7 %shard_map.102 = (f32[4,512,1280]{2,1,0:T(8,128)}, bf16[8,4,48,128]{3,2,1,0:T(8,128)(2,1)}, bf16[128,512]{1,0:T(8,128)(2,1)}) custom-call(s32[3]{0:T(128)} %pad_add_fusion.valid, bf16[128,5120]{1,0:T(8,128)(2,1)} %bitcast.74, bf16[128,5120]{1,0:T(8,128)(2,1)} %bitcast.76, bf16[8,4,48,128]{3,2,1,0:T(8,128)(2,1)} %bitcast.72, bf16[128,512]{1,0:T(8,128)(2,1)} %bitcast.79), custom_call_target="tpu_custom_call" | custom-call | flops 1342177280 | bytes 14155776 | tf_op jit(solution)/shard_map/pallas_call | solution.py:167
  71.3 2.4 %fusion.1.value_own = bf16[128,512]{1,0:T(8,128)(2,1)S(1)} fusion(bf16[2560,512]{1,0:T(8,128)(2,1)} %all-gather.2.cloned.1.call-done, bf16[128,2560]{0,1:T(8,128)(2,1)S(1)} %reshape.75), kind=kOutput, calls=%fused_computation.4 | convolution fusion | flops 335609856 | bytes 3407872 | tf_op jit(solution)/shard_map/dot_general | solution.py:240
  73.8 0.1 pad_maximum_fusion
  73.9 21.0 %all_to_all.31.held = bf16[32,64,128]{2,1,0:T(8,128)(2,1)} all-to-all(bf16[32,64,128]{2,1,0:T(8,128)(2,1)S(1)} %pad_maximum_fusion), channel_id=1, replica_groups=mesh['leaf'=32,'grp'=8] {'leaf'}, dimensions={0} | all-to-all | bytes 1048576 | tf_op jit(solution)/shard_map/all_to_all | solution.py:194
  94.9 2.4 %shard_map.103 = bf16[32,64,128]{2,1,0:T(8,128)(2,1)} custom-call(s32[32]{0:T(128)} %fusion.5.parents, bf16[32,64,128]{2,1,0:T(8,128)(2,1)} %all_to_all.31.held), custom_call_target="tpu_custom_call" | custom-call | bytes 1048576 | tf_op jit(solution)/shard_map/pallas_call | solution.py:66
  97.3 21.1 %all_to_all.32 = bf16[32,64,128]{2,1,0:T(8,128)(2,1)S(1)} all-to-all(bf16[32,64,128]{2,1,0:T(8,128)(2,1)} %shard_map.103), channel_id=1, replica_groups=mesh['leaf'=32,'grp'=8] {'leaf'}, dimensions={0} | all-to-all | bytes 1048576 | tf_op jit(solution)/shard_map/all_to_all | solution.py:194
  118.4 0.1 copy.32
  118.6 0.9 fusion
  119.5 2.6 %copy.39 = bf16[2560,512]{1,0:T(8,128)(2,1)} copy(bf16[2560,512]{0,1:T(8,128)(2,1)S(1)} %fusion) | data formatting | bytes 5242880
  122.1 12.5 %shard_map.104 = (bf16[128,5120]{1,0:T(8,128)(2,1)}, bf16[128,5120]{1,0:T(8,128)(2,1)}, bf16[8,4,48,128]{3,2,1,0:T(8,128)(2,1)}, bf16[128,512]{1,0:T(8,128)(2,1)}) custom-call(bf16[128,5120]{1,0:T(8,128)(2,1)} %bitcast.75, bf16[128,5120]{1,0:T(8,128)(2,1)} %bitcast.77, f32[4,512,1280]{2,1,0:T(8,128)} %get-tuple-element.12.probs, ...), custom_call_target="tpu_custom_call" | custom-call | flops 2684354560 | bytes 17432576 | tf_op jit(solution)/shard_map/pallas_call | solution.py:167
  134.7 18.7 %all_to_all.33.held = bf16[32,48,128]{2,1,0:T(8,128)(2,1)} all-to-all(bf16[32,48,128]{2,1,0:T(8,128)(2,1)} %bitcast.86), channel_id=1, replica_groups=mesh['leaf'=32,'grp'=8] {'leaf'}, dimensions={0} | all-to-all | bytes 786432 | tf_op jit(solution)/shard_map/all_to_all | solution.py:194
  153.3 2.1 %shard_map.105 = bf16[32,16,128]{2,1,0:T(8,128)(2,1)} custom-call(s32[32]{0:T(128)} %fusion.5.parents, bf16[32,48,128]{2,1,0:T(8,128)(2,1)} %all_to_all.33.held), custom_call_target="tpu_custom_call" | custom-call | bytes 786432 | tf_op jit(solution)/shard_map/pallas_call | solution.py:66
  155.4 0.8 reduce-scatter.4.cloned.1.call-done
  156.3 1.2 reshape.80
  157.4 1.7 pad_maximum_fusion.1
  159.1 10.1 %all-to-all-start.5 = ((bf16[32,56,128]{2,1,0:T(8,128)(2,1)}), bf16[32,56,128]{2,1,0:T(8,128)(2,1)}, u32[]{:S(2)}, u32[]{:S(2)}) async-start(bf16[32,56,128]{2,1,0:T(8,128)(2,1)} %pad_maximum_fusion.1), calls=%async_computation.5 | async-start | bytes 917504 | tf_op jit(solution)/shard_map/all_to_all | solution.py:194
  169.3 1.9 convolution_convert_fusion.1
  171.2 0.3 copy.35
  171.5 0.2 reshape.81
  171.7 0.3 copy.36
  172.0 0.2 broadcast_in_dim_reshape.3
  172.2 1.1 copy.37
  173.3 9.1 %all-to-all-done.5 = bf16[32,56,128]{2,1,0:T(8,128)(2,1)} async-done(((bf16[32,56,128]{2,1,0:T(8,128)(2,1)}), bf16[32,56,128]{2,1,0:T(8,128)(2,1)}, u32[]{:S(2)}, u32[]{:S(2)}) %all-to-all-start.5) | async-done | bytes 458784 | tf_op jit(solution)/shard_map/all_to_all | solution.py:194
  182.4 0.9 slice.28
  183.4 0.1 copy.34
  183.5 1.0 convert_reduce_fusion
  184.5 0.6 reshape.82
  185.2 0.7 fusion.4
  (34 shorter events, 0.4 us)
Async XLA Ops:
  7.2 64.1 %all-gather.2.cloned.1.call-start = ((), (), s32[]{:S(2)}) async-start(), calls=%async_computation.7 | async-start | bytes 2949120 | tf_op jit(solution)/shard_map/all_gather | solution.py:221
  9.7 38.4 %copy-start.5 = (bf16[1,128,2560]{2,1,0:T(8,128)(2,1)S(1)}, bf16[1,128,2560]{2,1,0:T(8,128)(2,1)}, u32[]{:S(2)}) copy-start(bf16[1,128,2560]{2,1,0:T(8,128)(2,1)} %param.6) | copy-start | bytes 1966084
  42.8 19.0 %all-to-all-start.1 = ((bf16[32,48,128]{2,1,0:T(8,128)(2,1)}), bf16[32,48,128]{2,1,0:T(8,128)(2,1)S(1)}, u32[]{:S(2)}, u32[]{:S(2)}) async-start(bf16[32,48,128]{2,1,0:T(8,128)(2,1)} %shard_map.101), calls=%async_computation.1 | async-start | bytes 786432 | tf_op jit(solution)/shard_map/all_to_all | solution.py:194
  48.0 108.2 %reduce-scatter.4.cloned.1.call-start = ((), (), s32[]{:S(2)}) async-start(), calls=%async_computation.8 | async-start | bytes 2949120 | tf_op jit(solution)/shard_map/reduce_scatter | solution.py:251
  49.0 24.6 %copy-start.2 = (bf16[128,2560]{0,1:T(8,128)(2,1)}, bf16[128,2560]{0,1:T(8,128)(2,1)S(1)}, u32[]{:S(2)}) copy-start(bf16[128,2560]{0,1:T(8,128)(2,1)S(1)} %reshape.75) | copy-start | bytes 1966084
  61.8 0.8 copy-start.4
  71.3 2.5 %copy-start.8 = (bf16[8,4,48,128]{3,2,1,0:T(8,128)(2,1)S(1)}, bf16[8,4,48,128]{3,2,1,0:T(8,128)(2,1)}, u32[]{:S(2)}) copy-start(bf16[8,4,48,128]{3,2,1,0:T(8,128)(2,1)} %get-tuple-element.13) | copy-start | bytes 1179652
  73.7 44.7 %copy-start.6 = (bf16[128,512]{1,0:T(8,128)(2,1)}, bf16[128,512]{1,0:T(8,128)(2,1)S(1)}, u32[]{:S(2)}) copy-start(bf16[128,512]{1,0:T(8,128)(2,1)S(1)} %fusion.1.value_own) | copy-start | bytes 393220
  73.8 44.8 %copy-start.3 = (bf16[128,2560]{0,1:T(8,128)(2,1)S(1)}, bf16[128,2560]{0,1:T(8,128)(2,1)}, u32[]{:S(2)}) copy-start(bf16[128,2560]{0,1:T(8,128)(2,1)} %copy-done.2) | copy-start | bytes 1966084
  73.8 44.8 %copy-start.7 = (bf16[128,512]{1,0:T(8,128)(2,1)S(1)}, bf16[128,512]{1,0:T(8,128)(2,1)}, u32[]{:S(2)}) copy-start(bf16[128,512]{1,0:T(8,128)(2,1)} %get-tuple-element.17) | copy-start | bytes 393220
  118.4 3.7 %copy-start = (bf16[32,64,128]{2,1,0:T(8,128)(2,1)}, bf16[32,64,128]{2,1,0:T(8,128)(2,1)S(1)}, u32[]{:S(2)}) copy-start(bf16[32,64,128]{2,1,0:T(8,128)(2,1)S(1)} %all_to_all.32) | copy-start | bytes 1572868
  134.7 34.6 %copy-start.1 = (bf16[2560,512]{1,0:T(8,128)(2,1)S(1)}, bf16[2560,512]{1,0:T(8,128)(2,1)}, u32[]{:S(2)}) copy-start(bf16[2560,512]{1,0:T(8,128)(2,1)} %all-gather.2.cloned.1.call-done) | copy-start | bytes 7864324
  159.1 23.3 %all-to-all-start.5 = ((bf16[32,56,128]{2,1,0:T(8,128)(2,1)}), bf16[32,56,128]{2,1,0:T(8,128)(2,1)}, u32[]{:S(2)}, u32[]{:S(2)}) async-start(bf16[32,56,128]{2,1,0:T(8,128)(2,1)} %pad_maximum_fusion.1), calls=%async_computation.5 | async-start | bytes 917504 | tf_op jit(solution)/shard_map/all_to_all | solution.py:194
  172.0 13.2 %copy-start.9 = (bf16[128,512]{1,0:T(8,128)(2,1)S(1)}, bf16[128,512]{1,0:T(8,128)(2,1)}, u32[]{:S(2)}) copy-start(bf16[128,512]{1,0:T(8,128)(2,1)} %get-tuple-element.18) | copy-start | bytes 393220
Sparse Core Ops, SparseCore 0:
  39.2 25.3 all-gather.1
  122.3 33.9 reduce-scatter.3

commit v2 on v1

v2 whole, which is shorter than its diff:
```python
import functools

import jax
import jax.numpy as jnp
import numpy as np
from jax import lax
from jax.experimental import pallas as pl
from jax.experimental.pallas import tpu as pltpu
from jax.sharding import PartitionSpec as P

HQ = 40
HK = 4
DH = 128
GROUPS = HQ // HK
SLOTS = 3
TILE = 16
LOG2E = 1.4426950408889634
BF = jnp.bfloat16
F32 = jnp.float32
VMEM_LIMIT = 56 * 1024 * 1024


def spread_rows(n_leaf, own_rows):
    leaf, head, row = (x.ravel() for x in np.indices((8, HK, own_rows)))
    source = (head * 8 + leaf) * own_rows + row
    return (source[:, None] == np.arange(source.size)[None, :]).astype(np.float32)


def pack_kernel(own_rows, parent, keys, weight, sent, rows):
    count = HK * own_rows
    rows[...] = jnp.full(rows.shape, parent[0, 0].astype(F32), F32)
    for head in range(HK):
        rows[head * own_rows : (head + 1) * own_rows, :] = weight[
            :, head * DH : (head + 1) * DH
        ].astype(F32)
    common = rows[...].astype(BF)
    for piece in range(sent.shape[0]):
        block, head = piece // HK, piece % HK
        sent[piece, 0:TILE, :] = keys[block * TILE : (block + 1) * TILE, head * DH : (head + 1) * DH]
        sent[piece, TILE:, :] = common


def fetch_kernel(own_rows, held, select, sent, weight, table, wide, parents, arrived):
    nodes = held.shape[0]
    count = HK * own_rows
    tail = held[:, held.shape[1] - TILE :, :].astype(F32)
    wide[...] = jnp.max(tail[:, TILE // 2 :, :], axis=1).astype(jnp.int32)
    copy = pltpu.make_async_copy(wide, parents, arrived)
    copy.start()
    for group in range(nodes // 8):
        part = held[group * 8 : (group + 1) * 8, TILE:, :].astype(F32)[:, :count, :]
        part = part.reshape(8 * count, DH).astype(BF)
        moved = dot(select[...], part, 0, 0).astype(BF)
        for head in range(HK):
            weight[
                group * 8 * own_rows : (group + 1) * 8 * own_rows, head * DH : (head + 1) * DH
            ] = moved[head * 8 * own_rows : (head + 1) * 8 * own_rows, :]
    copy.wait()
    for node in range(nodes):
        parent = parents[node, 0]
        above = table[jnp.maximum(parent, 0)] if node > 0 else -1
        deep = jnp.logical_and(parent > 0, above >= 0)
        table[node] = jnp.where(deep, above, jnp.where(parent > 0, parent, -1))
        table[nodes + node] = jnp.where(deep, parent, -1)
    for node in range(nodes):
        sent[node, 0:TILE, :] = held[0, 0:TILE, :]
        for slot in range(1, SLOTS):
            owner = jnp.maximum(table[(slot - 1) * nodes + node], 0)
            sent[node, slot * TILE : (slot + 1) * TILE, :] = held[owner, 0:TILE, :]


def add_up(table, held, totals):
    nodes = held.shape[0]
    for total in totals:
        total[...] = jnp.zeros_like(total)
    root = jnp.zeros((TILE, DH), F32)
    for node in range(nodes):
        root = root + held[node, 0:TILE, :].astype(F32)
        for slot in range(1, SLOTS):
            owner = jnp.maximum(table[(slot - 1) * nodes + node], 0)
            totals[slot - 1][owner] += held[node, slot * TILE : (slot + 1) * TILE, :].astype(F32)
    totals[0][0] += root


def value_kernel(table, held, sent, *totals):
    nodes = held.shape[0]
    values = slice(SLOTS * TILE, (SLOTS + 1) * TILE)
    add_up(table, held, totals)
    for node in range(nodes):
        sent[node, 0:TILE, :] = held[0, values, :]
        for slot in range(1, SLOTS):
            owner = jnp.maximum(table[(slot - 1) * nodes + node], 0)
            sent[node, slot * TILE : (slot + 1) * TILE, :] = held[owner, values, :]
        sent[node, values, :] = (totals[0][node] + totals[1][node]).astype(BF)


def key_kernel(own_rows, table, held, part, select, sent, *totals):
    nodes = held.shape[0]
    count = HK * own_rows
    add_up(table, held, totals)
    for node in range(nodes):
        sent[node, 0:TILE, :] = (totals[0][node] + totals[1][node]).astype(BF)
    for group in range(nodes // 8):
        rows = part[group * 8 * own_rows : (group + 1) * 8 * own_rows, :]
        rows = jnp.concatenate([rows[:, h * DH : (h + 1) * DH] for h in range(HK)], axis=0)
        moved = dot(select[...], rows, 1, 0).reshape(8, count, DH)
        fill = jnp.zeros((8, sent.shape[1] - TILE - count, DH), F32)
        sent[group * 8 : (group + 1) * 8, TILE:, :] = jnp.concatenate(
            [moved, fill], axis=1
        ).astype(BF)


def last_kernel(own_rows, held, key_own, key_grad, weight_grad, rows):
    for piece in range(held.shape[0]):
        block, head = piece // HK, piece % HK
        at = (slice(block * TILE, (block + 1) * TILE), slice(head * DH, (head + 1) * DH))
        key_grad[at] = (held[piece, 0:TILE, :].astype(F32) + key_own[at].astype(F32)).astype(BF)
    rows[...] = jnp.sum(held[:, TILE:, :].astype(F32), axis=0)
    for head in range(HK):
        weight_grad[:, head * DH : (head + 1) * DH] = rows[
            head * own_rows : (head + 1) * own_rows, :
        ]


def project_kernel(pieces, own, columns, value_grad, part):
    @pl.when(pl.program_id(0) == 0)
    def _():
        for block in range(pieces.shape[0]):
            for head in range(HK):
                at = (slice(block * TILE, (block + 1) * TILE), slice(head * DH, (head + 1) * DH))
                value_grad[at] = (
                    pieces[block, head].astype(F32) + own[at].astype(F32)
                ).astype(BF)

    part[...] = dot(columns[...], value_grad[...], 1, 0).astype(BF)


def plain(kernel, arrays, outs, scratch=(), scalars=0, scalar_outs=0, flops=0):
    smem, vmem = pl.BlockSpec(memory_space=pltpu.SMEM), pl.BlockSpec(memory_space=pltpu.VMEM)
    moved = sum(a.size * a.dtype.itemsize for a in list(arrays) + list(outs))
    return pl.pallas_call(
        kernel,
        out_shape=outs,
        in_specs=[smem] * scalars + [vmem] * (len(arrays) - scalars),
        out_specs=[vmem] * (len(outs) - scalar_outs) + [smem] * scalar_outs,
        scratch_shapes=list(scratch),
        compiler_params=pltpu.CompilerParams(vmem_limit_bytes=VMEM_LIMIT),
        cost_estimate=pl.CostEstimate(flops=flops, bytes_accessed=moved, transcendentals=0),
    )(*arrays)


def rows_of(pieces, own):
    parts = [
        pieces[:, 0, slot * TILE : (slot + 1) * TILE, :].reshape(-1, DH) for slot in range(SLOTS)
    ]
    return jnp.concatenate(parts + [own[...]], axis=0)


def put_rows(pieces, own, rows):
    seg = own.shape[0]
    for slot in range(SLOTS):
        block = rows[slot * seg : (slot + 1) * seg, :]
        pieces[:, 0, slot * TILE : (slot + 1) * TILE, :] = block.reshape(-1, TILE, DH).astype(BF)
    own[...] = rows[SLOTS * seg :, :].astype(BF)


def pair(block, index):
    return jnp.concatenate(
        [block[:, (2 * index + i) * DH : (2 * index + i + 1) * DH] for i in range(2)], axis=0
    )


def put_pair(block, index, rows):
    seg = block.shape[0]
    for i in range(2):
        block[:, (2 * index + i) * DH : (2 * index + i + 1) * DH] = rows[
            i * seg : (i + 1) * seg, :
        ].astype(BF)


def dot(lhs, rhs, left, right):
    return lax.dot_general(lhs, rhs, (((left,), (right,)), ((), ())), preferred_element_type=F32)


def probs_kernel(table, own, query, grad, key_pieces, key_own, probs, value_pieces, value_own, bias):
    seg = query.shape[0]

    @pl.when(pl.program_id(0) == 0)
    def _():
        key_ids = lax.broadcasted_iota(jnp.int32, (seg, 2 * seg), 0)
        query_ids = lax.broadcasted_iota(jnp.int32, (seg, 2 * seg), 1) % seg
        bias[...] = jnp.where(key_ids <= query_ids, 0.0, -1e30)

    nodes = table.shape[0] // (SLOTS - 1)
    present = [own[0] > 0] + [table[slot * nodes + own[0]] >= 0 for slot in range(SLOTS - 1)]
    levels = [jnp.where(here, 0.0, -1e30).astype(F32) for here in present]
    keys = rows_of(key_pieces, key_own)
    total = jnp.zeros((keys.shape[0], DH), F32)
    for index in range(GROUPS // 2):
        scores = dot(keys, pair(query, index), 1, 1) * (LOG2E / DH**0.5)
        scores = jnp.concatenate(
            [scores[slot * seg : (slot + 1) * seg, :] + levels[slot] for slot in range(SLOTS)]
            + [scores[SLOTS * seg :, :] + bias[...]],
            axis=0,
        )
        weight = jnp.exp2(scores - jnp.max(scores, axis=0, keepdims=True))
        prob = weight * (1.0 / jnp.sum(weight, axis=0, keepdims=True))
        probs[0, :, index * 2 * seg : (index + 1) * 2 * seg] = prob
        total += dot(prob.astype(BF), pair(grad, index), 1, 0)
    put_rows(value_pieces, value_own, total)


def grads_kernel(
    query, grad, probs, key_pieces, key_own, value_pieces, value_own,
    output, query_grad, grad_pieces, grad_own,
):
    seg = query.shape[0]
    keys = rows_of(key_pieces, key_own)
    values = rows_of(value_pieces, value_own)
    keys_t, values_t = keys.T, values.T
    total = jnp.zeros((keys.shape[0], DH), F32)
    for index in range(GROUPS // 2):
        prob = probs[0, :, index * 2 * seg : (index + 1) * 2 * seg]
        dprob = dot(values, pair(grad, index), 1, 1)
        delta = jnp.sum(prob * dprob, axis=0, keepdims=True)
        dscore = (prob * (dprob - delta)).astype(BF)
        total += dot(dscore, pair(query, index), 1, 0)
        put_pair(output, index, dot(values_t, prob.astype(BF), 1, 0).astype(BF).T)
        put_pair(query_grad, index, (dot(keys_t, dscore, 1, 0) * (1.0 / DH**0.5)).astype(BF).T)
    put_rows(grad_pieces, grad_own, total * (1.0 / DH**0.5))


def attention(kernel, lead, arrays, outs, scratch, flops, transcendentals):
    def spec(shape):
        if len(shape) == 4:
            return pl.BlockSpec((shape[0], 1) + shape[2:], lambda h: (0, h, 0, 0))
        if len(shape) == 3:
            return pl.BlockSpec((1,) + shape[1:], lambda h: (h, 0, 0))
        return pl.BlockSpec((shape[0], shape[1] // HK), lambda h: (0, h))

    moved = sum(a.size * a.dtype.itemsize for a in arrays) + sum(
        o.size * o.dtype.itemsize for o in outs
    )
    return pl.pallas_call(
        kernel,
        grid=(HK,),
        out_shape=outs,
        in_specs=[pl.BlockSpec(memory_space=pltpu.SMEM)] * len(lead)
        + [spec(a.shape) for a in arrays],
        out_specs=[spec(o.shape) for o in outs],
        scratch_shapes=scratch,
        compiler_params=pltpu.CompilerParams(vmem_limit_bytes=VMEM_LIMIT),
        cost_estimate=pl.CostEstimate(
            flops=flops, bytes_accessed=moved, transcendentals=transcendentals
        ),
    )(*lead, *arrays)


def project(pieces, own, columns, steps=2):
    blocks = pieces.shape[0]
    seg, width = own.shape
    depth = columns.shape[0]
    return pl.pallas_call(
        project_kernel,
        grid=(steps,),
        out_shape=[
            jax.ShapeDtypeStruct((seg, width), BF),
            jax.ShapeDtypeStruct((depth, width), BF),
        ],
        in_specs=[
            pl.BlockSpec((blocks, HK, TILE, DH), lambda i: (0, 0, SLOTS, 0)),
            pl.BlockSpec((seg, width), lambda i: (0, 0)),
            pl.BlockSpec((depth // steps, seg), lambda i: (i, 0)),
        ],
        out_specs=[
            pl.BlockSpec((seg, width), lambda i: (0, 0)),
            pl.BlockSpec((depth // steps, width), lambda i: (i, 0)),
        ],
        compiler_params=pltpu.CompilerParams(vmem_limit_bytes=VMEM_LIMIT),
        cost_estimate=pl.CostEstimate(
            flops=2 * seg * width * depth,
            bytes_accessed=2 * depth * (width + seg),
            transcendentals=0,
        ),
    )(pieces, own, columns)


def to_pieces(rows):
    seg, width = rows.shape
    split = rows.reshape(seg // TILE, TILE, width // DH, DH).transpose(0, 2, 1, 3)
    return split.reshape(-1, TILE, DH)


def swap(array):
    return lax.all_to_all(array, "leaf", 0, 0, tiled=True)


def shards(n_leaf, n_grp, hidden_states, query_rows, key_rows, value_weight, parent_links, out_grad):
    hidden, query, keys, grad = hidden_states[0], query_rows[0], key_rows[0], out_grad[0]
    seg, width = keys.shape
    depth = hidden.shape[1]
    own_rows = value_weight.shape[0]
    blocks = seg // TILE
    tail = -(-(HK * own_rows + TILE // 2) // TILE) * TILE
    shape = jax.ShapeDtypeStruct
    flops = 2 * seg * 4 * seg * DH * HQ
    select = jnp.asarray(spread_rows(n_leaf, own_rows), BF)
    totals = [pltpu.VMEM((n_leaf, TILE, DH), F32)] * (SLOTS - 1)
    slots = SLOTS * TILE

    columns = hidden.T.reshape(n_leaf, n_grp, own_rows, seg).transpose(1, 0, 2, 3)
    columns = columns.reshape(depth, seg)

    (first,) = plain(
        functools.partial(pack_kernel, own_rows),
        [parent_links, keys, value_weight],
        [shape((n_leaf, TILE + tail, DH), BF)],
        [pltpu.VMEM((tail, DH), F32)],
        scalars=1,
    )
    first = swap(first)

    second, weight, table = plain(
        functools.partial(fetch_kernel, own_rows),
        [first, select],
        [
            shape((n_leaf, slots, DH), BF),
            shape((n_leaf * own_rows, width), BF),
            shape(((SLOTS - 1) * n_leaf,), jnp.int32),
        ],
        [
            pltpu.VMEM((n_leaf, DH), jnp.int32),
            pltpu.SMEM((n_leaf, DH), jnp.int32),
            pltpu.SemaphoreType.DMA,
        ],
        scalar_outs=1,
    )
    weight = lax.all_gather(weight, "grp", axis=0, tiled=True)
    key_pieces = swap(second).reshape(blocks, HK, slots, DH)
    probs, value_terms, value_term_own = attention(
        probs_kernel,
        [table, lax.axis_index("leaf").astype(jnp.int32).reshape(1)],
        [query, grad, key_pieces, keys],
        [
            shape((HK, 4 * seg, GROUPS * seg), F32),
            shape((blocks, HK, slots, DH), BF),
            shape((seg, width), BF),
        ],
        [pltpu.VMEM((seg, 2 * seg), F32)],
        2 * flops,
        HQ * seg * 4 * seg,
    )

    values = dot(columns, weight, 0, 0).astype(BF)
    third = jnp.concatenate([value_terms.reshape(-1, slots, DH), to_pieces(values)], axis=1)
    third = swap(third)

    (fourth,) = plain(
        value_kernel, [table, third], [shape((n_leaf, slots + TILE, DH), BF)], totals, scalars=1
    )
    fourth = swap(fourth).reshape(blocks, HK, slots + TILE, DH)
    value_grad, weight_part = project(fourth, value_term_own, columns)
    weight_part = lax.psum_scatter(weight_part, "grp", scatter_dimension=0, tiled=True)
    output, query_grad, key_terms, key_term_own = attention(
        grads_kernel,
        [],
        [query, grad, probs, key_pieces, keys, fourth, values],
        [
            shape((seg, HQ * DH), BF),
            shape((seg, HQ * DH), BF),
            shape((blocks, HK, slots, DH), BF),
            shape((seg, width), BF),
        ],
        [],
        4 * flops,
        0,
    )
    hidden_grad = dot(value_grad, weight, 1, 1).astype(BF)
    hidden_grad = hidden_grad.reshape(seg, n_grp, n_leaf, own_rows).transpose(0, 2, 1, 3)
    hidden_grad = hidden_grad.reshape(seg, depth)

    fifth = swap(key_terms.reshape(-1, slots, DH))

    (sixth,) = plain(
        functools.partial(key_kernel, own_rows),
        [table, fifth, weight_part, select],
        [shape((n_leaf, TILE + tail, DH), BF)],
        totals,
        scalars=1,
    )
    sixth = swap(sixth)
    key_grad, weight_grad = plain(
        functools.partial(last_kernel, own_rows),
        [sixth, key_term_own],
        [shape((seg, width), BF), shape((own_rows, width), F32)],
        [pltpu.VMEM((tail, DH), F32)],
    )
    return (output[None], query_grad[None], key_grad[None], hidden_grad[None], weight_grad)


def solution(mesh):
    rows = P("grp", "leaf", None)
    spread = P(("leaf", "grp"), None)
    return jax.shard_map(
        functools.partial(shards, mesh.shape["leaf"], mesh.shape["grp"]),
        mesh=mesh,
        in_specs=(rows, rows, rows, spread, P("grp", "leaf"), rows),
        out_specs=(rows, rows, rows, rows, spread),
        check_vma=False,
    )
```

time: 194 us -> 195 us (level)
  waiting for transfers between devices: 17.1 us -> 28.1 us
  local copies, waits for them, and re-layouts: 14.7 us -> 3.92 us
  Pallas kernels: 27.6 us -> 33.8 us
  other arithmetic: 6.24 us -> 0.05 us
  blocking collectives: 89 us -> 93.7 us
  between operations: 17.6 us -> 15 us
    pallas_call x3 -> x6, Pallas kernels: 6.33 us -> 14.6 us  [the longest x5 11.4 us: plain(): pl.pallas_call(kernel, out_shape=outs, in_specs=[smem] * scalars + [vmem]...]
    all_to_all x2, waiting for transfers between devices: 16.2 us -> 24 us  [swap(): return lax.all_to_all(array, 'leaf', 0, 0, tiled=True)]
    all_to_all x4, blocking collectives: 89 us -> 93.7 us  [swap(): return lax.all_to_all(array, 'leaf', 0, 0, tiled=True)]
    reduce_scatter x1, waiting for transfers between devices: 0.82 us -> 4 us  [shards(): lax.psum_scatter(weight_part, 'grp', scatter_dimension=0, tiled=True)]
    unnamed x23 -> x15, local copies, waits for them, and re-layouts: 4.85 us -> 1.87 us
    reshape x4 -> x2, local copies, waits for them, and re-layouts: 2.95 us -> 0.44 us  [the longest x1 0.23 us: shards(): columns = columns.reshape(depth, seg)]
    dot_general x1 -> x0, matrix products: 2.36 us -> none  [shards(): values = jnp.dot(columns, weight, preferred_element_type=F32).astype(BF)]
    pallas_call x2, Pallas kernels: 21.3 us -> 19.2 us  [attention(): pl.pallas_call(kernel, grid=(HK,), out_shape=outs, in_specs=[pl.BlockSpec...]
  transfers between devices with their start and end apart: 4 -> 4, of which waited for: 3 -> 3; matrix products, arithmetic and copies ran while one was open for 5% -> 2% of each run, Pallas kernels for 13% -> 10%
where the time goes in v2:
time: 195 us; the launch traced here: 193 us
  blocking collectives  93.7 us (48%)
  Pallas kernels  33.8 us (17%)
  waiting for transfers between devices  28.1 us (14%)
  starting transfers between devices  15.1 us (8%)
  between operations  15 us (8%)
  local copies, waits for them, and re-layouts  3.92 us (2%)
  matrix products  3.33 us (2%)
    all_to_all x4, blocking collectives, swap(): return lax.all_to_all(array, 'leaf', 0, 0, tiled=True)  93.7 us
    all_to_all x2, waiting for transfers between devices, swap(): return lax.all_to_all(array, 'leaf', 0, 0, tiled=True)  24 us
    pallas_call x2, Pallas kernels, attention(): pl.pallas_call(kernel, grid=(HK,), out_shape=outs, in_specs=[pl.BlockSpec...  19.2 us
    all_to_all x2, starting transfers between devices, swap(): return lax.all_to_all(array, 'leaf', 0, 0, tiled=True)  15 us
    pallas_call x5, Pallas kernels, plain(): pl.pallas_call(kernel, out_shape=outs, in_specs=[smem] * scalars + [vmem]...  11.4 us
    reduce_scatter x1, waiting for transfers between devices, shards(): lax.psum_scatter(weight_part, 'grp', scatter_dimension=0, tiled=True)  4 us
  transfers between devices with their start and end apart: 4, of which 3 were waited for; matrix products, arithmetic and copies ran while one was open for 2% of the time, Pallas kernels for 10%

profile of v2, /device:TPU:32, one launch (start us, length us, event | category | flops | bytes accessed | tf_op | source)
XLA Modules:
  0.0 193.0 jit_solution(14955377216874387640)
XLA Ops:
  7.2 0.0 copy-start.3
  7.2 0.0 all-gather.2.cloned.1.call-start
  7.9 1.8 shard_map.110
  9.7 28.5 %all_to_all.30.held = bf16[32,64,128]{2,1,0:T(8,128)(2,1)} all-to-all(bf16[32,64,128]{2,1,0:T(8,128)(2,1)} %shard_map.110), channel_id=1, replica_groups=mesh['leaf'=32,'grp'=8] {'leaf'}, dimensions={0} | all-to-all | bytes 1048576 | tf_op jit(solution)/shard_map/all_to_all | solution.py:295
  38.2 3.4 %shard_map.111 = (bf16[32,48,128]{2,1,0:T(8,128)(2,1)}, bf16[320,512]{1,0:T(8,128)(2,1)}, s32[64]{0:T(128)}) custom-call(bf16[32,64,128]{2,1,0:T(8,128)(2,1)} %all_to_all.30.held, bf16[320,320]{1,0:T(8,128)(2,1)} %constant.8.clone.select), custom_call_target="tpu_custom_call" | custom-call | bytes 1450240 | tf_op jit(solution)/shard_map/pallas_call | solution.py:141
  41.6 0.0 all-gather.2.cloned.1.call-update
  41.6 5.2 %all-to-all-start.1 = ((bf16[32,48,128]{2,1,0:T(8,128)(2,1)}), bf16[32,48,128]{2,1,0:T(8,128)(2,1)S(1)}, u32[]{:S(2)}, u32[]{:S(2)}) async-start(bf16[32,48,128]{2,1,0:T(8,128)(2,1)} %get-tuple-element.20), calls=%async_computation.1 | async-start | bytes 786432 | tf_op jit(solution)/shard_map/all_to_all | solution.py:295
  46.8 0.0 reduce-scatter.2.cloned.1.call-start
  46.9 0.0 copy-done.3
  46.9 0.3 copy.16
  47.2 0.2 reshape.43
  47.4 0.2 copy.17
  47.6 0.2 reshape.44.columns
  47.9 0.0 copy-start
  47.9 12.7 %all-to-all-done.1 = bf16[32,48,128]{2,1,0:T(8,128)(2,1)S(1)} async-done(((bf16[32,48,128]{2,1,0:T(8,128)(2,1)}), bf16[32,48,128]{2,1,0:T(8,128)(2,1)S(1)}, u32[]{:S(2)}, u32[]{:S(2)}) %all-to-all-start.1) | async-done | bytes 393248 | tf_op jit(solution)/shard_map/all_to_all | solution.py:295
  60.6 0.0 copy-start.2
  60.6 0.8 copy-done.2
  61.4 8.7 %shard_map.112 = (f32[4,512,1280]{2,1,0:T(8,128)}, bf16[8,4,48,128]{3,2,1,0:T(8,128)(2,1)}, bf16[128,512]{1,0:T(8,128)(2,1)}) custom-call(s32[64]{0:T(128)} %get-tuple-element.19.table, s32[1]{0:T(128)} %bitcast.3.own, bf16[128,5120]{1,0:T(8,128)(2,1)} %bitcast.34, bf16[128,5120]{1,0:T(8,128)(2,1)} %bitcast.36, bf16[8,4,48,128]{3,2,1,0:T(8,128)(2,1)} %bitcast.32, ...), custom_call_target="tpu_custom_call" | custom-call | flops 1342177280 | bytes 14155776 | tf_op jit(solution)/shard_map/pallas_call | solution.py:244
  70.1 0.0 copy-start.5
  70.1 0.0 all-gather.2.cloned.1.call-done
  70.1 2.4 %fusion.value_own = bf16[128,512]{1,0:T(8,128)(2,1)S(1)} fusion(bf16[2560,512]{1,0:T(8,128)(2,1)} %all-gather.2.cloned.1.call-done, bf16[2560,128]{1,0:T(8,128)(2,1)S(1)} %reshape.44.columns), kind=kOutput, calls=%fused_computation.2 | convolution fusion | flops 335609856 | bytes 3407872 | tf_op jit(solution)/shard_map/dot_general | solution.py:182
  72.5 0.0 copy-done
  72.5 0.0 copy-start.4
  72.6 0.0 copy-done.5
  72.6 0.1 pad_maximum_fusion
  72.6 24.5 %all_to_all.31.held = bf16[32,64,128]{2,1,0:T(8,128)(2,1)} all-to-all(bf16[32,64,128]{2,1,0:T(8,128)(2,1)S(1)} %pad_maximum_fusion), channel_id=1, replica_groups=mesh['leaf'=32,'grp'=8] {'leaf'}, dimensions={0} | all-to-all | bytes 1048576 | tf_op jit(solution)/shard_map/all_to_all | solution.py:295
  97.1 2.1 %shard_map.113 = bf16[32,64,128]{2,1,0:T(8,128)(2,1)} custom-call(s32[64]{0:T(128)} %get-tuple-element.19.table, bf16[32,64,128]{2,1,0:T(8,128)(2,1)} %all_to_all.31.held), custom_call_target="tpu_custom_call" | custom-call | bytes 1048832 | tf_op jit(solution)/shard_map/pallas_call | solution.py:141
  99.2 21.7 %all_to_all.32 = bf16[32,64,128]{2,1,0:T(8,128)(2,1)} all-to-all(bf16[32,64,128]{2,1,0:T(8,128)(2,1)} %shard_map.113), channel_id=1, replica_groups=mesh['leaf'=32,'grp'=8] {'leaf'}, dimensions={0} | all-to-all | bytes 1048576 | tf_op jit(solution)/shard_map/all_to_all | solution.py:295
  121.0 3.2 %shard_map.115 = (bf16[128,512]{1,0:T(8,128)(2,1)}, bf16[2560,512]{1,0:T(8,128)(2,1)}) custom-call(bf16[8,4,64,128]{3,2,1,0:T(8,128)(2,1)} %bitcast.28, bf16[128,512]{1,0:T(8,128)(2,1)} %get-tuple-element.27.own, bf16[2560,128]{1,0:T(8,128)(2,1)} %copy-done), custom_call_target="tpu_custom_call" | custom-call | flops 335544320 | bytes 3276800 | tf_op jit(solution)/shard_map/pallas_call | solution.py:263
  124.2 0.0 copy-done.4
  124.2 0.0 reduce-scatter.2.cloned.1.call-update
  124.2 10.5 %shard_map.114 = (bf16[128,5120]{1,0:T(8,128)(2,1)}, bf16[128,5120]{1,0:T(8,128)(2,1)}, bf16[8,4,48,128]{3,2,1,0:T(8,128)(2,1)}, bf16[128,512]{1,0:T(8,128)(2,1)}) custom-call(bf16[128,5120]{1,0:T(8,128)(2,1)} %bitcast.35, bf16[128,5120]{1,0:T(8,128)(2,1)} %bitcast.37, f32[4,512,1280]{2,1,0:T(8,128)} %get-tuple-element.21.probs, ...), custom_call_target="tpu_custom_call" | custom-call | flops 2684354560 | bytes 17432576 | tf_op jit(solution)/shard_map/pallas_call | solution.py:244
  134.7 0.0 copy-start.1
  134.7 0.0 copy-start.6
  134.7 19.0 %all_to_all.33.held = bf16[32,48,128]{2,1,0:T(8,128)(2,1)} all-to-all(bf16[32,48,128]{2,1,0:T(8,128)(2,1)} %bitcast.44), channel_id=1, replica_groups=mesh['leaf'=32,'grp'=8] {'leaf'}, dimensions={0} | all-to-all | bytes 786432 | tf_op jit(solution)/shard_map/all_to_all | solution.py:295
  153.8 4.0 %reduce-scatter.2.cloned.1.call-done.part = bf16[320,512]{1,0:T(8,128)(2,1)} async-done(((bf16[2560,512]{1,0:T(8,128)(2,1)}), bf16[320,512]{1,0:T(8,128)(2,1)}) %reduce-scatter.2.cloned.1.call-update) | async-done | bytes 327696 | tf_op jit(solution)/shard_map/reduce_scatter | solution.py:363
  157.8 2.4 %shard_map.116 = bf16[32,64,128]{2,1,0:T(8,128)(2,1)} custom-call(s32[64]{0:T(128)} %get-tuple-element.19.table, bf16[32,48,128]{2,1,0:T(8,128)(2,1)} %all_to_all.33.held, bf16[320,512]{1,0:T(8,128)(2,1)} %reduce-scatter.2.cloned.1.call-done.part, bf16[320,320]{1,0:T(8,128)(2,1)} %constant.8.clone.select), custom_call_target="tpu_custom_call" | custom-call | bytes 1450240 | tf_op jit(solution)/shard_map/pallas_call | solution.py:141
  160.2 9.8 %all-to-all-start.5 = ((bf16[32,64,128]{2,1,0:T(8,128)(2,1)}), bf16[32,64,128]{2,1,0:T(8,128)(2,1)}, u32[]{:S(2)}, u32[]{:S(2)}) async-start(bf16[32,64,128]{2,1,0:T(8,128)(2,1)} %shard_map.116), calls=%async_computation.6 | async-start | bytes 1048576 | tf_op jit(solution)/shard_map/all_to_all | solution.py:295
  170.0 0.0 copy-done.1
  170.0 0.0 copy-done.6
  170.0 1.0 convolution_convert_fusion
  171.0 0.3 copy.20
  171.3 0.2 reshape.49
  171.5 0.3 copy.21
  171.8 0.2 broadcast_in_dim_reshape.3
  172.0 1.1 copy.22
  173.1 11.3 %all-to-all-done.5.held = bf16[32,64,128]{2,1,0:T(8,128)(2,1)} async-done(((bf16[32,64,128]{2,1,0:T(8,128)(2,1)}), bf16[32,64,128]{2,1,0:T(8,128)(2,1)}, u32[]{:S(2)}, u32[]{:S(2)}) %all-to-all-start.5) | async-done | bytes 524320 | tf_op jit(solution)/shard_map/all_to_all | solution.py:295
  184.4 1.8 shard_map.117
  (2 shorter events, 0.1 us)
Async XLA Ops:
  7.2 39.7 %copy-start.3 = (bf16[1,128,2560]{2,1,0:T(8,128)(2,1)S(1)}, bf16[1,128,2560]{2,1,0:T(8,128)(2,1)}, u32[]{:S(2)}) copy-start(bf16[1,128,2560]{2,1,0:T(8,128)(2,1)} %param.7) | copy-start | bytes 1966084
  7.2 62.9 %all-gather.2.cloned.1.call-start = ((), (), s32[]{:S(2)}) async-start(), calls=%async_computation.7 | async-start | bytes 2949120 | tf_op jit(solution)/shard_map/all_gather | solution.py:338
  41.6 19.0 %all-to-all-start.1 = ((bf16[32,48,128]{2,1,0:T(8,128)(2,1)}), bf16[32,48,128]{2,1,0:T(8,128)(2,1)S(1)}, u32[]{:S(2)}, u32[]{:S(2)}) async-start(bf16[32,48,128]{2,1,0:T(8,128)(2,1)} %get-tuple-element.20), calls=%async_computation.1 | async-start | bytes 786432 | tf_op jit(solution)/shard_map/all_to_all | solution.py:295
  46.8 110.9 %reduce-scatter.2.cloned.1.call-start = ((), (), s32[]{:S(2)}) async-start(), calls=%async_computation.8 | async-start | bytes 2949120 | tf_op jit(solution)/shard_map/reduce_scatter | solution.py:363
  47.9 24.6 %copy-start = (bf16[2560,128]{1,0:T(8,128)(2,1)}, bf16[2560,128]{1,0:T(8,128)(2,1)S(1)}, u32[]{:S(2)}) copy-start(bf16[2560,128]{1,0:T(8,128)(2,1)S(1)} %reshape.44.columns) | copy-start | bytes 1966084
  60.6 0.8 copy-start.2
  70.1 2.5 %copy-start.5 = (bf16[8,4,48,128]{3,2,1,0:T(8,128)(2,1)S(1)}, bf16[8,4,48,128]{3,2,1,0:T(8,128)(2,1)}, u32[]{:S(2)}) copy-start(bf16[8,4,48,128]{3,2,1,0:T(8,128)(2,1)} %get-tuple-element.22) | copy-start | bytes 1179652
  72.5 51.7 %copy-start.4 = (bf16[128,512]{1,0:T(8,128)(2,1)}, bf16[128,512]{1,0:T(8,128)(2,1)S(1)}, u32[]{:S(2)}) copy-start(bf16[128,512]{1,0:T(8,128)(2,1)S(1)} %fusion.value_own) | copy-start | bytes 393220
  134.7 35.2 %copy-start.1 = (bf16[2560,512]{1,0:T(8,128)(2,1)S(1)}, bf16[2560,512]{1,0:T(8,128)(2,1)}, u32[]{:S(2)}) copy-start(bf16[2560,512]{1,0:T(8,128)(2,1)} %all-gather.2.cloned.1.call-done) | copy-start | bytes 7864324
  134.7 35.3 %copy-start.6 = (bf16[128,512]{1,0:T(8,128)(2,1)S(1)}, bf16[128,512]{1,0:T(8,128)(2,1)}, u32[]{:S(2)}) copy-start(bf16[128,512]{1,0:T(8,128)(2,1)} %get-tuple-element.31) | copy-start | bytes 393220
  160.2 24.2 %all-to-all-start.5 = ((bf16[32,64,128]{2,1,0:T(8,128)(2,1)}), bf16[32,64,128]{2,1,0:T(8,128)(2,1)}, u32[]{:S(2)}, u32[]{:S(2)}) async-start(bf16[32,64,128]{2,1,0:T(8,128)(2,1)} %shard_map.116), calls=%async_computation.6 | async-start | bytes 1048576 | tf_op jit(solution)/shard_map/all_to_all | solution.py:295
Sparse Core Ops, SparseCore 0:
  41.7 25.3 all-gather.1
  124.3 33.4 reduce-scatter.1

commit v3 on v2

--- a/solution.py
+++ b/solution.py
@@ -17,7 +17,7 @@
 LOG2E = 1.4426950408889634
 BF = jnp.bfloat16
 F32 = jnp.float32
-VMEM_LIMIT = 56 * 1024 * 1024
+VMEM_LIMIT = 28 * 1024 * 1024
 
 
 def spread_rows(n_leaf, own_rows):
@@ -40,14 +40,9 @@
         sent[piece, TILE:, :] = common
 
 
-def fetch_kernel(own_rows, held, select, sent, weight, table, wide, parents, arrived):
-    nodes = held.shape[0]
+def weight_kernel(own_rows, held, select, weight):
     count = HK * own_rows
-    tail = held[:, held.shape[1] - TILE :, :].astype(F32)
-    wide[...] = jnp.max(tail[:, TILE // 2 :, :], axis=1).astype(jnp.int32)
-    copy = pltpu.make_async_copy(wide, parents, arrived)
-    copy.start()
-    for group in range(nodes // 8):
+    for group in range(held.shape[0] // 8):
         part = held[group * 8 : (group + 1) * 8, TILE:, :].astype(F32)[:, :count, :]
         part = part.reshape(8 * count, DH).astype(BF)
         moved = dot(select[...], part, 0, 0).astype(BF)
@@ -55,6 +50,16 @@
             weight[
                 group * 8 * own_rows : (group + 1) * 8 * own_rows, head * DH : (head + 1) * DH
             ] = moved[head * 8 * own_rows : (head + 1) * 8 * own_rows, :]
+
+
+def fetch_kernel(held, sent, table, wide, parents, arrived):
+    nodes = held.shape[0]
+    tail = held[:, held.shape[1] - TILE :, :].astype(F32)
+    wide[...] = jnp.max(tail[:, TILE // 2 :, :], axis=1).astype(jnp.int32)
+    copy = pltpu.make_async_copy(wide, parents, arrived)
+    copy.start()
+    for node in range(nodes):
+        sent[node, 0:TILE, :] = held[0, 0:TILE, :]
     copy.wait()
     for node in range(nodes):
         parent = parents[node, 0]
@@ -63,7 +68,6 @@
         table[node] = jnp.where(deep, above, jnp.where(parent > 0, parent, -1))
         table[nodes + node] = jnp.where(deep, parent, -1)
     for node in range(nodes):
-        sent[node, 0:TILE, :] = held[0, 0:TILE, :]
         for slot in range(1, SLOTS):
             owner = jnp.maximum(table[(slot - 1) * nodes + node], 0)
             sent[node, slot * TILE : (slot + 1) * TILE, :] = held[owner, 0:TILE, :]
@@ -94,13 +98,16 @@
         sent[node, values, :] = (totals[0][node] + totals[1][node]).astype(BF)
 
 
-def key_kernel(own_rows, table, held, part, select, sent, *totals):
-    nodes = held.shape[0]
+def key_kernel(table, held, sums, *totals):
+    add_up(table, held, totals)
+    for node in range(held.shape[0]):
+        sums[node] = (totals[0][node] + totals[1][node]).astype(BF)
+
+
+def join_kernel(own_rows, sums, part, select, sent):
     count = HK * own_rows
-    add_up(table, held, totals)
-    for node in range(nodes):
-        sent[node, 0:TILE, :] = (totals[0][node] + totals[1][node]).astype(BF)
-    for group in range(nodes // 8):
+    sent[:, 0:TILE, :] = sums[...]
+    for group in range(sent.shape[0] // 8):
         rows = part[group * 8 * own_rows : (group + 1) * 8 * own_rows, :]
         rows = jnp.concatenate([rows[:, h * DH : (h + 1) * DH] for h in range(HK)], axis=0)
         moved = dot(select[...], rows, 1, 0).reshape(8, count, DH)
@@ -320,14 +327,16 @@
     )
     first = swap(first)
 
-    second, weight, table = plain(
-        functools.partial(fetch_kernel, own_rows),
+    (weight,) = plain(
+        functools.partial(weight_kernel, own_rows),
         [first, select],
-        [
-            shape((n_leaf, slots, DH), BF),
-            shape((n_leaf * own_rows, width), BF),
-            shape(((SLOTS - 1) * n_leaf,), jnp.int32),
-        ],
+        [shape((n_leaf * own_rows, width), BF)],
+    )
+    weight = lax.all_gather(weight, "grp", axis=0, tiled=True)
+    second, table = plain(
+        fetch_kernel,
+        [first],
+        [shape((n_leaf, slots, DH), BF), shape(((SLOTS - 1) * n_leaf,), jnp.int32)],
         [
             pltpu.VMEM((n_leaf, DH), jnp.int32),
             pltpu.SMEM((n_leaf, DH), jnp.int32),
@@ -335,7 +344,6 @@
         ],
         scalar_outs=1,
     )
-    weight = lax.all_gather(weight, "grp", axis=0, tiled=True)
     key_pieces = swap(second).reshape(blocks, HK, slots, DH)
     probs, value_terms, value_term_own = attention(
         probs_kernel,
@@ -381,12 +389,17 @@
 
     fifth = swap(key_terms.reshape(-1, slots, DH))
 
+    (key_sums,) = plain(
+        key_kernel, [table, fifth], [shape((n_leaf, TILE, DH), BF)], totals, scalars=1
+    )
+    weight_part, hidden_grad, key_sums = lax.optimization_barrier(
+        (weight_part, hidden_grad, key_sums)
+    )
+
     (sixth,) = plain(
-        functools.partial(key_kernel, own_rows),
-        [table, fifth, weight_part, select],
+        functools.partial(join_kernel, own_rows),
+        [key_sums, weight_part, select],
         [shape((n_leaf, TILE + tail, DH), BF)],
-        totals,
-        scalars=1,
     )
     sixth = swap(sixth)
     key_grad, weight_grad = plain(

time: 195 us -> 190 us (0.974)
  blocking collectives: 93.7 us -> 69.9 us
  local copies, waits for them, and re-layouts: 3.92 us -> 19.5 us
  Pallas kernels: 33.8 us -> 23.9 us
  waiting for transfers between devices: 28.1 us -> 34.9 us
  starting transfers between devices: 15.1 us -> 20.5 us
    all_to_all x4 -> x3, blocking collectives: 93.7 us -> 69.9 us  [swap(): return lax.all_to_all(array, 'leaf', 0, 0, tiled=True)]
    unnamed x15 -> x25, local copies, waits for them, and re-layouts: 1.87 us -> 15.3 us
    all_to_all x2 -> x3, waiting for transfers between devices: 24 us -> 33.3 us  [swap(): return lax.all_to_all(array, 'leaf', 0, 0, tiled=True)]
    all_to_all x2 -> x3, starting transfers between devices: 15 us -> 20.4 us  [swap(): return lax.all_to_all(array, 'leaf', 0, 0, tiled=True)]
    pallas_call x5 -> x7, Pallas kernels: 11.4 us -> 6.6 us  [plain(): pl.pallas_call(kernel, out_shape=outs, in_specs=[smem] * scalars + [vmem]...]
    pallas_call x2, Pallas kernels: 19.2 us -> 15.2 us  [attention(): pl.pallas_call(kernel, grid=(HK,), out_shape=outs, in_specs=[pl.BlockSpec...]
    reduce_scatter x1, waiting for transfers between devices: 4 us -> 1.53 us  [shards(): lax.psum_scatter(weight_part, 'grp', scatter_dimension=0, tiled=True)]
  transfers between devices with their start and end apart: 4 -> 5, of which waited for: 3 -> 4; matrix products, arithmetic and copies ran while one was open for 2% -> 4% of each run, Pallas kernels for 10% -> 9%
where the time goes in v3:
time: 190 us; the launch traced here: 189 us
  blocking collectives  69.9 us (37%)
  waiting for transfers between devices  34.9 us (18%)
  Pallas kernels  23.9 us (13%)
  starting transfers between devices  20.5 us (11%)
  local copies, waits for them, and re-layouts  19.5 us (10%)
  between operations  14.9 us (8%)
  matrix products  5.08 us (3%)
    all_to_all x3, blocking collectives, swap(): return lax.all_to_all(array, 'leaf', 0, 0, tiled=True)  69.9 us
    all_to_all x3, waiting for transfers between devices, swap(): return lax.all_to_all(array, 'leaf', 0, 0, tiled=True)  33.3 us
    all_to_all x3, starting transfers between devices, swap(): return lax.all_to_all(array, 'leaf', 0, 0, tiled=True)  20.4 us
    unnamed x25, local copies, waits for them, and re-layouts  15.3 us
    pallas_call x2, Pallas kernels, attention(): pl.pallas_call(kernel, grid=(HK,), out_shape=outs, in_specs=[pl.BlockSpec...  15.2 us
    pallas_call x7, Pallas kernels, plain(): pl.pallas_call(kernel, out_shape=outs, in_specs=[smem] * scalars + [vmem]...  6.6 us
    dot_general x2, matrix products, dot(): lax.dot_general(lhs, rhs, (((left,), (right,)), ((), ())), preferred_elem...  5.08 us
  transfers between devices with their start and end apart: 5, of which 4 were waited for; matrix products, arithmetic and copies ran while one was open for 4% of the time, Pallas kernels for 9%

profile of v3, /device:TPU:32, one launch (start us, length us, event | category | flops | bytes accessed | tf_op | source)
XLA Modules:
  0.0 188.7 jit_solution(10198226573670447923)
XLA Ops:
  7.2 0.0 all-gather.2.cloned.1.call-start
  7.9 0.0 copy-start.7
  7.9 0.9 copy-done.7
  8.8 0.7 copy-done.10
  9.5 28.3 %all_to_all.30.held = bf16[32,64,128]{2,1,0:T(8,128)(2,1)S(1)} all-to-all(bf16[32,64,128]{2,1,0:T(8,128)(2,1)S(1)} %shard_map.110), channel_id=1, replica_groups=mesh['leaf'=32,'grp'=8] {'leaf'}, dimensions={0} | all-to-all | bytes 1048576 | tf_op jit(solution)/shard_map/all_to_all | solution.py:302
  37.9 0.9 copy-done.5
  38.8 1.2 shard_map.113
  40.0 0.0 all-gather.2.cloned.1.call-update
  40.0 1.8 shard_map.111
  41.9 5.2 %all-to-all-start.1 = ((bf16[32,48,128]{2,1,0:T(8,128)(2,1)}), bf16[32,48,128]{2,1,0:T(8,128)(2,1)S(1)}, u32[]{:S(2)}, u32[]{:S(2)}) async-start(bf16[32,48,128]{2,1,0:T(8,128)(2,1)} %get-tuple-element.22), calls=%async_computation.1 | async-start | bytes 786432 | tf_op jit(solution)/shard_map/all_to_all | solution.py:302
  47.1 0.0 reduce-scatter.2.cloned.1.call-start
  47.2 0.3 copy.16
  47.5 0.0 copy-start.2
  47.5 0.0 copy-start.8
  47.5 0.2 reshape.46
  47.7 1.2 copy.17
  48.9 1.4 reshape.47.columns
  50.3 10.6 %all-to-all-done.1 = bf16[32,48,128]{2,1,0:T(8,128)(2,1)S(1)} async-done(((bf16[32,48,128]{2,1,0:T(8,128)(2,1)}), bf16[32,48,128]{2,1,0:T(8,128)(2,1)S(1)}, u32[]{:S(2)}, u32[]{:S(2)}) %all-to-all-start.1) | async-done | bytes 393248 | tf_op jit(solution)/shard_map/all_to_all | solution.py:302
  60.9 0.0 copy-done.8
  60.9 1.3 copy-done.3
  62.2 7.0 %shard_map.112 = (f32[4,512,1280]{2,1,0:T(8,128)S(1)}, bf16[8,4,48,128]{3,2,1,0:T(8,128)(2,1)S(1)}, bf16[128,512]{1,0:T(8,128)(2,1)S(1)}) custom-call(s32[64]{0:T(128)S(1)} %get-tuple-element.21.table, s32[1]{0:T(128)} %bitcast.3.own, bf16[128,5120]{1,0:T(8,128)(2,1)S(1)} %bitcast.33, bf16[128,5120]{1,0:T(8,128)(2,1)S(1)} %bitcast.35, ...), custom_call_target="tpu_custom_call" | custom-call | flops 1342177280 | bytes 14155776 | tf_op jit(solution)/shard_map/pallas_call | solution.py:251
  69.2 4.0 %copy-done = f32[4,512,1280]{2,1,0:T(8,128)} copy-done((f32[4,512,1280]{2,1,0:T(8,128)}, f32[4,512,1280]{2,1,0:T(8,128)S(1)}, u32[]{:S(2)}) %copy-start) | copy-done | bytes 10485784
  73.2 2.3 %fusion.value_own = bf16[128,512]{1,0:T(8,128)(2,1)S(1)} fusion(bf16[2560,512]{1,0:T(8,128)(2,1)} %all-gather.2.cloned.1.call-done, bf16[2560,128]{1,0:T(8,128)(2,1)S(1)} %reshape.47.columns), kind=kOutput, calls=%fused_computation.2 | convolution fusion | flops 335609856 | bytes 3407872 | tf_op jit(solution)/shard_map/dot_general | solution.py:189
  75.6 0.1 pad_maximum_fusion
  75.7 20.8 %all_to_all.31.held = bf16[32,64,128]{2,1,0:T(8,128)(2,1)S(1)} all-to-all(bf16[32,64,128]{2,1,0:T(8,128)(2,1)S(1)} %pad_maximum_fusion), channel_id=1, replica_groups=mesh['leaf'=32,'grp'=8] {'leaf'}, dimensions={0} | all-to-all | bytes 1048576 | tf_op jit(solution)/shard_map/all_to_all | solution.py:302
  96.5 0.8 shard_map.114
  97.3 20.8 %all_to_all.32 = bf16[32,64,128]{2,1,0:T(8,128)(2,1)S(1)} all-to-all(bf16[32,64,128]{2,1,0:T(8,128)(2,1)S(1)} %shard_map.114), channel_id=1, replica_groups=mesh['leaf'=32,'grp'=8] {'leaf'}, dimensions={0} | all-to-all | bytes 1048576 | tf_op jit(solution)/shard_map/all_to_all | solution.py:302
  118.1 2.2 %shard_map.116 = (bf16[128,512]{1,0:T(8,128)(2,1)S(1)}, bf16[2560,512]{1,0:T(8,128)(2,1)}) custom-call(bf16[8,4,64,128]{3,2,1,0:T(8,128)(2,1)S(1)} %bitcast.29, bf16[128,512]{1,0:T(8,128)(2,1)S(1)} %get-tuple-element.27.own, bf16[2560,128]{1,0:T(8,128)(2,1)S(1)} %reshape.47.columns), custom_call_target="tpu_custom_call" | custom-call | flops 335544320 | bytes 3276800 | tf_op jit(solution)/shard_map/pallas_call | solution.py:270
  120.2 0.0 reduce-scatter.2.cloned.1.call-update
  120.3 4.0 %copy-done.1 = f32[4,512,1280]{2,1,0:T(8,128)S(1)} copy-done((f32[4,512,1280]{2,1,0:T(8,128)S(1)}, f32[4,512,1280]{2,1,0:T(8,128)}, u32[]{:S(2)}) %copy-start.1) | copy-done | bytes 10485784
  124.2 1.3 copy-done.4
  125.5 8.2 %shard_map.115 = (bf16[128,5120]{1,0:T(8,128)(2,1)}, bf16[128,5120]{1,0:T(8,128)(2,1)}, bf16[8,4,48,128]{3,2,1,0:T(8,128)(2,1)}, bf16[128,512]{1,0:T(8,128)(2,1)S(1)}) custom-call(bf16[128,5120]{1,0:T(8,128)(2,1)S(1)} %bitcast.34, bf16[128,5120]{1,0:T(8,128)(2,1)S(1)} %bitcast.36, f32[4,512,1280]{2,1,0:T(8,128)S(1)} %copy-done.1, ...), custom_call_target="tpu_custom_call" | custom-call | flops 2684354560 | bytes 17432576 | tf_op jit(solution)/shard_map/pallas_call | solution.py:251
  133.8 5.1 %all-to-all-start.4 = ((bf16[32,48,128]{2,1,0:T(8,128)(2,1)}), bf16[32,48,128]{2,1,0:T(8,128)(2,1)S(1)}, u32[]{:S(2)}, u32[]{:S(2)}) async-start(bf16[32,48,128]{2,1,0:T(8,128)(2,1)} %bitcast.16), calls=%async_computation.5 | async-start | bytes 786432 | tf_op jit(solution)/shard_map/all_to_all | solution.py:302
  138.9 2.8 %convolution_convert_fusion = bf16[128,2560]{1,0:T(8,128)(2,1)S(1)} fusion(bf16[128,512]{1,0:T(8,128)(2,1)S(1)} %get-tuple-element.29, bf16[2560,512]{1,0:T(8,128)(2,1)} %all-gather.2.cloned.1.call-done), kind=kOutput, calls=%fused_computation | convolution fusion | flops 335872000 | bytes 3407872 | tf_op jit(solution)/shard_map/dot_general | solution.py:189
  141.6 0.3 copy.20
  142.0 0.0 copy-start.6
  142.0 0.2 reshape.51
  142.2 0.3 copy.21
  142.5 0.2 reshape.52
  142.8 9.3 %all-to-all-done.4.held = bf16[32,48,128]{2,1,0:T(8,128)(2,1)S(1)} async-done(((bf16[32,48,128]{2,1,0:T(8,128)(2,1)}), bf16[32,48,128]{2,1,0:T(8,128)(2,1)S(1)}, u32[]{:S(2)}, u32[]{:S(2)}) %all-to-all-start.4) | async-done | bytes 393248 | tf_op jit(solution)/shard_map/all_to_all | solution.py:302
  152.1 0.8 shard_map.117.sums
  152.9 1.5 reduce-scatter.2.cloned.1.call-done.part
  154.4 1.0 copy-done.9
  155.4 1.2 shard_map.118
  156.6 10.1 %all-to-all-start.5 = ((bf16[32,64,128]{2,1,0:T(8,128)(2,1)}), bf16[32,64,128]{2,1,0:T(8,128)(2,1)S(1)}, u32[]{:S(2)}, u32[]{:S(2)}) async-start(bf16[32,64,128]{2,1,0:T(8,128)(2,1)} %shard_map.118), calls=%async_computation.6 | async-start | bytes 1048576 | tf_op jit(solution)/shard_map/all_to_all | solution.py:302
  166.7 1.1 copy.22
  167.8 13.4 %all-to-all-done.5.held = bf16[32,64,128]{2,1,0:T(8,128)(2,1)S(1)} async-done(((bf16[32,64,128]{2,1,0:T(8,128)(2,1)}), bf16[32,64,128]{2,1,0:T(8,128)(2,1)S(1)}, u32[]{:S(2)}, u32[]{:S(2)}) %all-to-all-start.5) | async-done | bytes 524320 | tf_op jit(solution)/shard_map/all_to_all | solution.py:302
  181.2 0.7 shard_map.119
  (15 shorter events, 0.1 us)
Async XLA Ops:
  7.2 66.0 %all-gather.2.cloned.1.call-start = ((), (), s32[]{:S(2)}) async-start(), calls=%async_computation.7 | async-start | bytes 2949120 | tf_op jit(solution)/shard_map/all_gather | solution.py:335
  7.9 0.9 copy-start.7
  8.8 0.7 copy-start.10
  9.5 37.7 %copy-start.11 = (bf16[1,128,2560]{2,1,0:T(8,128)(2,1)S(1)}, bf16[1,128,2560]{2,1,0:T(8,128)(2,1)}, u32[]{:S(2)}) copy-start(bf16[1,128,2560]{2,1,0:T(8,128)(2,1)} %param.7) | copy-start | bytes 1966084
  37.9 0.9 copy-start.5
  41.9 19.0 %all-to-all-start.1 = ((bf16[32,48,128]{2,1,0:T(8,128)(2,1)}), bf16[32,48,128]{2,1,0:T(8,128)(2,1)S(1)}, u32[]{:S(2)}, u32[]{:S(2)}) async-start(bf16[32,48,128]{2,1,0:T(8,128)(2,1)} %get-tuple-element.22), calls=%async_computation.1 | async-start | bytes 786432 | tf_op jit(solution)/shard_map/all_to_all | solution.py:302
  47.1 107.3 %reduce-scatter.2.cloned.1.call-start = ((), (), s32[]{:S(2)}) async-start(), calls=%async_computation.8 | async-start | bytes 2949120 | tf_op jit(solution)/shard_map/reduce_scatter | solution.py:371
  47.5 13.4 %copy-start.2 = (bf16[1,128,5120]{2,1,0:T(8,128)(2,1)S(1)}, bf16[1,128,5120]{2,1,0:T(8,128)(2,1)}, u32[]{:S(2)}) copy-start(bf16[1,128,5120]{2,1,0:T(8,128)(2,1)} %param.8) | copy-start | bytes 3932164
  47.5 13.4 %copy-start.8 = (bf16[1,128,512]{2,1,0:T(8,128)(2,1)S(1)}, bf16[1,128,512]{2,1,0:T(8,128)(2,1)}, u32[]{:S(2)}) copy-start(bf16[1,128,512]{2,1,0:T(8,128)(2,1)} %param.9) | copy-start | bytes 393220
  60.9 1.3 copy-start.3
  69.2 4.0 %copy-start = (f32[4,512,1280]{2,1,0:T(8,128)}, f32[4,512,1280]{2,1,0:T(8,128)S(1)}, u32[]{:S(2)}) copy-start(f32[4,512,1280]{2,1,0:T(8,128)S(1)} %get-tuple-element.23.probs) | copy-start | bytes 31457284
  120.2 4.0 %copy-start.1 = (f32[4,512,1280]{2,1,0:T(8,128)S(1)}, f32[4,512,1280]{2,1,0:T(8,128)}, u32[]{:S(2)}) copy-start(f32[4,512,1280]{2,1,0:T(8,128)} %copy-done) | copy-start | bytes 31457284
  124.2 1.3 copy-start.4
  133.8 18.3 %all-to-all-start.4 = ((bf16[32,48,128]{2,1,0:T(8,128)(2,1)}), bf16[32,48,128]{2,1,0:T(8,128)(2,1)S(1)}, u32[]{:S(2)}, u32[]{:S(2)}) async-start(bf16[32,48,128]{2,1,0:T(8,128)(2,1)} %bitcast.16), calls=%async_computation.5 | async-start | bytes 786432 | tf_op jit(solution)/shard_map/all_to_all | solution.py:302
  142.0 12.4 %copy-start.6 = (bf16[320,320]{1,0:T(8,128)(2,1)S(1)}, bf16[320,320]{1,0:T(8,128)(2,1)}, u32[]{:S(2)}) copy-start(bf16[320,320]{1,0:T(8,128)(2,1)} %constant.8.clone.select) | copy-start | bytes 614404
  154.4 1.0 copy-start.9
  156.6 24.6 %all-to-all-start.5 = ((bf16[32,64,128]{2,1,0:T(8,128)(2,1)}), bf16[32,64,128]{2,1,0:T(8,128)(2,1)S(1)}, u32[]{:S(2)}, u32[]{:S(2)}) async-start(bf16[32,64,128]{2,1,0:T(8,128)(2,1)} %shard_map.118), calls=%async_computation.6 | async-start | bytes 1048576 | tf_op jit(solution)/shard_map/all_to_all | solution.py:302
Sparse Core Ops, SparseCore 0:
  40.2 25.3 all-gather.1
  120.4 34.0 reduce-scatter.1

commit v4 on v3

--- a/solution.py
+++ b/solution.py
@@ -2,7 +2,6 @@
 
 import jax
 import jax.numpy as jnp
-import numpy as np
 from jax import lax
 from jax.experimental import pallas as pl
 from jax.experimental.pallas import tpu as pltpu
@@ -18,12 +17,28 @@
 BF = jnp.bfloat16
 F32 = jnp.float32
 VMEM_LIMIT = 28 * 1024 * 1024
-
-
-def spread_rows(n_leaf, own_rows):
-    leaf, head, row = (x.ravel() for x in np.indices((8, HK, own_rows)))
-    source = (head * 8 + leaf) * own_rows + row
-    return (source[:, None] == np.arange(source.size)[None, :]).astype(np.float32)
+ATTENTION_LIMIT = 56 * 1024 * 1024
+
+
+def quotient(value, divisor, limit):
+    shift = next(
+        n
+        for n in range(8, 20)
+        if all(x * ((1 << n) // divisor + 1) >> n == x // divisor for x in range(limit))
+    )
+    return (value * ((1 << shift) // divisor + 1)) >> shift
+
+
+def spread_rows(own_rows):
+    count = HK * own_rows
+    size = 8 * count
+    target = lax.broadcasted_iota(jnp.int32, (size, size), 0)
+    leaf = quotient(target, count, size)
+    rest = target - leaf * count
+    head = quotient(rest, own_rows, count)
+    source = (head * 8 + leaf) * own_rows + (rest - head * own_rows)
+    found = source == lax.broadcasted_iota(jnp.int32, (size, size), 1)
+    return jnp.where(found, 1.0, 0.0).astype(BF)
 
 
 def pack_kernel(own_rows, parent, keys, weight, sent, rows):
@@ -40,12 +55,13 @@
         sent[piece, TILE:, :] = common
 
 
-def weight_kernel(own_rows, held, select, weight):
+def weight_kernel(own_rows, held, weight):
+    select = spread_rows(own_rows)
     count = HK * own_rows
     for group in range(held.shape[0] // 8):
         part = held[group * 8 : (group + 1) * 8, TILE:, :].astype(F32)[:, :count, :]
         part = part.reshape(8 * count, DH).astype(BF)
-        moved = dot(select[...], part, 0, 0).astype(BF)
+        moved = dot(select, part, 0, 0).astype(BF)
         for head in range(HK):
             weight[
                 group * 8 * own_rows : (group + 1) * 8 * own_rows, head * DH : (head + 1) * DH
@@ -104,13 +120,14 @@
         sums[node] = (totals[0][node] + totals[1][node]).astype(BF)
 
 
-def join_kernel(own_rows, sums, part, select, sent):
+def join_kernel(own_rows, sums, part, sent):
+    select = spread_rows(own_rows)
     count = HK * own_rows
     sent[:, 0:TILE, :] = sums[...]
     for group in range(sent.shape[0] // 8):
         rows = part[group * 8 * own_rows : (group + 1) * 8 * own_rows, :]
         rows = jnp.concatenate([rows[:, h * DH : (h + 1) * DH] for h in range(HK)], axis=0)
-        moved = dot(select[...], rows, 1, 0).reshape(8, count, DH)
+        moved = dot(select, rows, 1, 0).reshape(8, count, DH)
         fill = jnp.zeros((8, sent.shape[1] - TILE - count, DH), F32)
         sent[group * 8 : (group + 1) * 8, TILE:, :] = jnp.concatenate(
             [moved, fill], axis=1
@@ -177,6 +194,10 @@
     )
 
 
+def heads_of(block):
+    return jnp.concatenate([block[:, i * DH : (i + 1) * DH] for i in range(GROUPS)], axis=0)
+
+
 def put_pair(block, index, rows):
     seg = block.shape[0]
     for i in range(2):
@@ -189,49 +210,68 @@
     return lax.dot_general(lhs, rhs, (((left,), (right,)), ((), ())), preferred_element_type=F32)
 
 
-def probs_kernel(table, own, query, grad, key_pieces, key_own, probs, value_pieces, value_own, bias):
-    seg = query.shape[0]
+def masks_of(table, own, bias):
+    seg = bias.shape[0]
 
     @pl.when(pl.program_id(0) == 0)
     def _():
-        key_ids = lax.broadcasted_iota(jnp.int32, (seg, 2 * seg), 0)
-        query_ids = lax.broadcasted_iota(jnp.int32, (seg, 2 * seg), 1) % seg
+        key_ids = lax.broadcasted_iota(jnp.int32, bias.shape, 0)
+        query_ids = lax.broadcasted_iota(jnp.int32, bias.shape, 1) % seg
         bias[...] = jnp.where(key_ids <= query_ids, 0.0, -1e30)
 
     nodes = table.shape[0] // (SLOTS - 1)
     present = [own[0] > 0] + [table[slot * nodes + own[0]] >= 0 for slot in range(SLOTS - 1)]
-    levels = [jnp.where(here, 0.0, -1e30).astype(F32) for here in present]
-    keys = rows_of(key_pieces, key_own)
-    total = jnp.zeros((keys.shape[0], DH), F32)
-    for index in range(GROUPS // 2):
-        scores = dot(keys, pair(query, index), 1, 1) * (LOG2E / DH**0.5)
-        scores = jnp.concatenate(
-            [scores[slot * seg : (slot + 1) * seg, :] + levels[slot] for slot in range(SLOTS)]
-            + [scores[SLOTS * seg :, :] + bias[...]],
-            axis=0,
-        )
-        weight = jnp.exp2(scores - jnp.max(scores, axis=0, keepdims=True))
-        prob = weight * (1.0 / jnp.sum(weight, axis=0, keepdims=True))
-        probs[0, :, index * 2 * seg : (index + 1) * 2 * seg] = prob
-        total += dot(prob.astype(BF), pair(grad, index), 1, 0)
-    put_rows(value_pieces, value_own, total)
-
-
-def grads_kernel(
-    query, grad, probs, key_pieces, key_own, value_pieces, value_own,
-    output, query_grad, grad_pieces, grad_own,
+    return [jnp.where(here, 0.0, -1e30).astype(F32) for here in present]
+
+
+def scores_of(keys, queries, levels, bias):
+    seg = bias.shape[0]
+    scores = dot(keys, queries, 1, 1) * (LOG2E / DH**0.5)
+    return jnp.concatenate(
+        [scores[slot * seg : (slot + 1) * seg, :] + levels[slot] for slot in range(SLOTS)]
+        + [scores[SLOTS * seg :, :] + bias[...]],
+        axis=0,
+    )
+
+
+def probs_kernel(
+    table, own, query, grad, key_pieces, key_own, stats, value_pieces, value_own, bias, low
 ):
     seg = query.shape[0]
+    levels = masks_of(table, own, bias)
+    keys = rows_of(key_pieces, key_own)
+    for index in range(GROUPS // 2):
+        at = slice(index * 2 * seg, (index + 1) * 2 * seg)
+        scores = scores_of(keys, pair(query, index), levels, bias)
+        top = jnp.max(scores, axis=0, keepdims=True)
+        weight = jnp.exp2(scores - top)
+        norm = 1.0 / jnp.sum(weight, axis=0, keepdims=True)
+        stats[0, 0:1, at] = top
+        stats[0, 1:2, at] = norm
+        low[:, at] = (weight * norm).astype(BF)
+    total = dot(low[...], heads_of(grad), 1, 0)
+    put_rows(value_pieces, value_own, total)
+
+
+def grads_kernel(
+    table, own, query, grad, stats, key_pieces, key_own, value_pieces, value_own,
+    output, query_grad, grad_pieces, grad_own, bias,
+):
+    seg = query.shape[0]
+    levels = masks_of(table, own, bias)
     keys = rows_of(key_pieces, key_own)
     values = rows_of(value_pieces, value_own)
     keys_t, values_t = keys.T, values.T
     total = jnp.zeros((keys.shape[0], DH), F32)
     for index in range(GROUPS // 2):
-        prob = probs[0, :, index * 2 * seg : (index + 1) * 2 * seg]
+        at = slice(index * 2 * seg, (index + 1) * 2 * seg)
+        queries = pair(query, index)
+        scores = scores_of(keys, queries, levels, bias)
+        prob = jnp.exp2(scores - stats[0, 0:1, at]) * stats[0, 1:2, at]
         dprob = dot(values, pair(grad, index), 1, 1)
         delta = jnp.sum(prob * dprob, axis=0, keepdims=True)
         dscore = (prob * (dprob - delta)).astype(BF)
-        total += dot(dscore, pair(query, index), 1, 0)
+        total += dot(dscore, queries, 1, 0)
         put_pair(output, index, dot(values_t, prob.astype(BF), 1, 0).astype(BF).T)
         put_pair(query_grad, index, (dot(keys_t, dscore, 1, 0) * (1.0 / DH**0.5)).astype(BF).T)
     put_rows(grad_pieces, grad_own, total * (1.0 / DH**0.5))
@@ -256,7 +296,7 @@
         + [spec(a.shape) for a in arrays],
         out_specs=[spec(o.shape) for o in outs],
         scratch_shapes=scratch,
-        compiler_params=pltpu.CompilerParams(vmem_limit_bytes=VMEM_LIMIT),
+        compiler_params=pltpu.CompilerParams(vmem_limit_bytes=ATTENTION_LIMIT),
         cost_estimate=pl.CostEstimate(
             flops=flops, bytes_accessed=moved, transcendentals=transcendentals
         ),
@@ -311,7 +351,6 @@
     tail = -(-(HK * own_rows + TILE // 2) // TILE) * TILE
     shape = jax.ShapeDtypeStruct
     flops = 2 * seg * 4 * seg * DH * HQ
-    select = jnp.asarray(spread_rows(n_leaf, own_rows), BF)
     totals = [pltpu.VMEM((n_leaf, TILE, DH), F32)] * (SLOTS - 1)
     slots = SLOTS * TILE
 
@@ -329,7 +368,7 @@
 
     (weight,) = plain(
         functools.partial(weight_kernel, own_rows),
-        [first, select],
+        [first],
         [shape((n_leaf * own_rows, width), BF)],
     )
     weight = lax.all_gather(weight, "grp", axis=0, tiled=True)
@@ -345,16 +384,17 @@
         scalar_outs=1,
     )
     key_pieces = swap(second).reshape(blocks, HK, slots, DH)
-    probs, value_terms, value_term_own = attention(
+    place = [table, lax.axis_index("leaf").astype(jnp.int32).reshape(1)]
+    stats, value_terms, value_term_own = attention(
         probs_kernel,
-        [table, lax.axis_index("leaf").astype(jnp.int32).reshape(1)],
+        place,
         [query, grad, key_pieces, keys],
         [
-            shape((HK, 4 * seg, GROUPS * seg), F32),
+            shape((HK, 8, GROUPS * seg), F32),
             shape((blocks, HK, slots, DH), BF),
             shape((seg, width), BF),
         ],
-        [pltpu.VMEM((seg, 2 * seg), F32)],
+        [pltpu.VMEM((seg, 2 * seg), F32), pltpu.VMEM((4 * seg, GROUPS * seg), BF)],
         2 * flops,
         HQ * seg * 4 * seg,
     )
@@ -371,17 +411,17 @@
     weight_part = lax.psum_scatter(weight_part, "grp", scatter_dimension=0, tiled=True)
     output, query_grad, key_terms, key_term_own = attention(
         grads_kernel,
-        [],
-        [query, grad, probs, key_pieces, keys, fourth, values],
+        place,
+        [query, grad, stats, key_pieces, keys, fourth, values],
         [
             shape((seg, HQ * DH), BF),
             shape((seg, HQ * DH), BF),
             shape((blocks, HK, slots, DH), BF),
             shape((seg, width), BF),
         ],
-        [],
-        4 * flops,
-        0,
+        [pltpu.VMEM((seg, 2 * seg), F32)],
+        5 * flops,
+        HQ * seg * 4 * seg,
     )
     hidden_grad = dot(value_grad, weight, 1, 1).astype(BF)
     hidden_grad = hidden_grad.reshape(seg, n_grp, n_leaf, own_rows).transpose(0, 2, 1, 3)
@@ -398,7 +438,7 @@
 
     (sixth,) = plain(
         functools.partial(join_kernel, own_rows),
-        [key_sums, weight_part, select],
+        [key_sums, weight_part],
         [shape((n_leaf, TILE + tail, DH), BF)],
     )
     sixth = swap(sixth)

time: 190 us -> 188 us (0.989)
  local copies, waits for them, and re-layouts: 19.5 us -> 7.02 us
  Pallas kernels: 23.9 us -> 28.4 us
  blocking collectives: 69.9 us -> 73.4 us
  waiting for transfers between devices: 34.9 us -> 37.1 us
    unnamed x25 -> x27, local copies, waits for them, and re-layouts: 15.3 us -> 4.98 us
    pallas_call x2, Pallas kernels: 15.2 us -> 19.5 us  [attention(): pl.pallas_call(kernel, grid=(HK,), out_shape=outs, in_specs=[pl.BlockSpec...]
    all_to_all x3, blocking collectives: 69.9 us -> 73.4 us  [swap(): return lax.all_to_all(array, 'leaf', 0, 0, tiled=True)]
    all_to_all x3, waiting for transfers between devices: 33.3 us -> 35.9 us  [swap(): return lax.all_to_all(array, 'leaf', 0, 0, tiled=True)]
  transfers between devices with their start and end apart: 5 -> 5, of which waited for: 4 -> 4; matrix products, arithmetic and copies ran while one was open for 4% -> 3% of each run, Pallas kernels for 9% -> 12%
where the time goes in v4:
time: 188 us; the launch traced here: 186 us
  blocking collectives  73.4 us (39%)
  waiting for transfers between devices  37.1 us (20%)
  Pallas kernels  28.4 us (15%)
  starting transfers between devices  20.4 us (11%)
  between operations  14.9 us (8%)
  local copies, waits for them, and re-layouts  7.02 us (4%)
  matrix products  5.11 us (3%)
    all_to_all x3, blocking collectives, swap(): return lax.all_to_all(array, 'leaf', 0, 0, tiled=True)  73.4 us
    all_to_all x3, waiting for transfers between devices, swap(): return lax.all_to_all(array, 'leaf', 0, 0, tiled=True)  35.9 us
    all_to_all x3, starting transfers between devices, swap(): return lax.all_to_all(array, 'leaf', 0, 0, tiled=True)  20.4 us
    pallas_call x2, Pallas kernels, attention(): pl.pallas_call(kernel, grid=(HK,), out_shape=outs, in_specs=[pl.BlockSpec...  19.5 us
    pallas_call x7, Pallas kernels, plain(): pl.pallas_call(kernel, out_shape=outs, in_specs=[smem] * scalars + [vmem]...  6.68 us
    dot_general x2, matrix products, dot(): lax.dot_general(lhs, rhs, (((left,), (right,)), ((), ())), preferred_elem...  5.11 us
    unnamed x27, local copies, waits for them, and re-layouts  4.98 us
  transfers between devices with their start and end apart: 5, of which 4 were waited for; matrix products, arithmetic and copies ran while one was open for 3% of the time, Pallas kernels for 12%

profile of v4, /device:TPU:32, one launch (start us, length us, event | category | flops | bytes accessed | tf_op | source)
XLA Modules:
  0.0 186.4 jit_solution(17931006595990853606)
XLA Ops:
  7.2 0.0 all-gather.2.cloned.1.call-start
  7.9 0.0 copy-start.4
  7.9 0.9 copy-done.4
  8.8 0.7 copy-done.5
  9.5 28.3 %all_to_all.30.held = bf16[32,64,128]{2,1,0:T(8,128)(2,1)S(1)} all-to-all(bf16[32,64,128]{2,1,0:T(8,128)(2,1)S(1)} %shard_map.101), channel_id=1, replica_groups=mesh['leaf'=32,'grp'=8] {'leaf'}, dimensions={0} | all-to-all | bytes 1048576 | tf_op jit(solution)/shard_map/all_to_all | solution.py:342
  37.9 1.2 shard_map.104
  39.1 0.0 all-gather.2.cloned.1.call-update
  39.1 1.8 shard_map.102
  41.0 0.0 copy-start.6
  41.0 0.5 copy-done.6
  41.5 5.2 %all-to-all-start.1 = ((bf16[32,48,128]{2,1,0:T(8,128)(2,1)}), bf16[32,48,128]{2,1,0:T(8,128)(2,1)S(1)}, u32[]{:S(2)}, u32[]{:S(2)}) async-start(bf16[32,48,128]{2,1,0:T(8,128)(2,1)} %get-tuple-element.22), calls=%async_computation.1 | async-start | bytes 786432 | tf_op jit(solution)/shard_map/all_to_all | solution.py:342
  46.7 0.0 reduce-scatter.2.cloned.1.call-start
  46.7 0.0 copy-done.9
  46.7 0.3 copy.15
  47.1 0.2 reshape.46
  47.3 0.2 copy.16
  47.5 0.2 reshape.47.columns
  47.7 12.8 %all-to-all-done.1 = bf16[32,48,128]{2,1,0:T(8,128)(2,1)S(1)} async-done(((bf16[32,48,128]{2,1,0:T(8,128)(2,1)}), bf16[32,48,128]{2,1,0:T(8,128)(2,1)S(1)}, u32[]{:S(2)}, u32[]{:S(2)}) %all-to-all-start.1) | async-done | bytes 393248 | tf_op jit(solution)/shard_map/all_to_all | solution.py:342
  60.5 0.8 copy-done.10
  61.2 7.1 %shard_map.103 = (f32[4,8,1280]{2,1,0:T(8,128)}, bf16[8,4,48,128]{3,2,1,0:T(8,128)(2,1)}, bf16[128,512]{1,0:T(8,128)(2,1)}) custom-call(s32[64]{0:T(128)} %copy-done.6, s32[1]{0:T(128)} %bitcast.1.own, bf16[128,5120]{1,0:T(8,128)(2,1)} %bitcast.44, bf16[128,5120]{1,0:T(8,128)(2,1)} %bitcast.46, bf16[8,4,48,128]{3,2,1,0:T(8,128)(2,1)} %bitcast.40, ...), custom_call_target="tpu_custom_call" | custom-call | flops 1342177280 | bytes 3833856 | tf_op jit(solution)/shard_map/pallas_call | solution.py:291
  68.4 0.0 all-gather.2.cloned.1.call-done
  68.4 2.4 %fusion.value_own = bf16[128,512]{1,0:T(8,128)(2,1)S(1)} fusion(bf16[2560,512]{1,0:T(8,128)(2,1)} %all-gather.2.cloned.1.call-done, bf16[2560,128]{1,0:T(8,128)(2,1)S(1)} %reshape.47.columns), kind=kOutput, calls=%fused_computation.2 | convolution fusion | flops 335609856 | bytes 3407872 | tf_op jit(solution)/shard_map/dot_general | solution.py:210
  70.7 0.0 copy-start.12
  70.8 0.0 copy-start.3
  70.8 0.1 pad_maximum_fusion
  70.9 23.6 %all_to_all.31.held = bf16[32,64,128]{2,1,0:T(8,128)(2,1)S(1)} all-to-all(bf16[32,64,128]{2,1,0:T(8,128)(2,1)S(1)} %pad_maximum_fusion), channel_id=1, replica_groups=mesh['leaf'=32,'grp'=8] {'leaf'}, dimensions={0} | all-to-all | bytes 1048576 | tf_op jit(solution)/shard_map/all_to_all | solution.py:342
  94.5 0.8 shard_map.105
  95.4 21.5 %all_to_all.32 = bf16[32,64,128]{2,1,0:T(8,128)(2,1)S(1)} all-to-all(bf16[32,64,128]{2,1,0:T(8,128)(2,1)S(1)} %shard_map.105), channel_id=1, replica_groups=mesh['leaf'=32,'grp'=8] {'leaf'}, dimensions={0} | all-to-all | bytes 1048576 | tf_op jit(solution)/shard_map/all_to_all | solution.py:342
  116.8 2.1 %shard_map.107 = (bf16[128,512]{1,0:T(8,128)(2,1)S(1)}, bf16[2560,512]{1,0:T(8,128)(2,1)}) custom-call(bf16[8,4,64,128]{3,2,1,0:T(8,128)(2,1)S(1)} %bitcast.29, bf16[128,512]{1,0:T(8,128)(2,1)S(1)} %copy-done.3, bf16[2560,128]{1,0:T(8,128)(2,1)S(1)} %reshape.47.columns), custom_call_target="tpu_custom_call" | custom-call | flops 335544320 | bytes 3276800 | tf_op jit(solution)/shard_map/pallas_call | solution.py:310
  119.0 0.0 reduce-scatter.2.cloned.1.call-update
  119.0 12.4 %shard_map.106 = (bf16[128,5120]{1,0:T(8,128)(2,1)}, bf16[128,5120]{1,0:T(8,128)(2,1)}, bf16[8,4,48,128]{3,2,1,0:T(8,128)(2,1)}, bf16[128,512]{1,0:T(8,128)(2,1)}) custom-call(s32[64]{0:T(128)} %copy-done.6, s32[1]{0:T(128)} %bitcast.1.own, bf16[128,5120]{1,0:T(8,128)(2,1)} %bitcast.45, bf16[128,5120]{1,0:T(8,128)(2,1)} %bitcast.47, ...), custom_call_target="tpu_custom_call" | custom-call | flops 3355443200 | bytes 7110656 | tf_op jit(solution)/shard_map/pallas_call | solution.py:291
  131.4 5.1 %all-to-all-start.4 = ((bf16[32,48,128]{2,1,0:T(8,128)(2,1)}), bf16[32,48,128]{2,1,0:T(8,128)(2,1)S(1)}, u32[]{:S(2)}, u32[]{:S(2)}) async-start(bf16[32,48,128]{2,1,0:T(8,128)(2,1)} %bitcast.42), calls=%async_computation.5 | async-start | bytes 786432 | tf_op jit(solution)/shard_map/all_to_all | solution.py:342
  136.5 2.8 %convolution_convert_fusion = bf16[128,2560]{1,0:T(8,128)(2,1)S(1)} fusion(bf16[128,512]{1,0:T(8,128)(2,1)S(1)} %get-tuple-element.29, bf16[2560,512]{1,0:T(8,128)(2,1)} %all-gather.2.cloned.1.call-done), kind=kOutput, calls=%fused_computation | convolution fusion | flops 335872000 | bytes 3407872 | tf_op jit(solution)/shard_map/dot_general | solution.py:210
  139.3 0.3 copy.19
  139.6 0.0 copy-start.8
  139.7 0.2 reshape.51
  139.9 0.3 copy.20
  140.2 0.0 copy-start.2
  140.2 0.2 reshape.52
  140.4 9.9 %all-to-all-done.4.held = bf16[32,48,128]{2,1,0:T(8,128)(2,1)S(1)} async-done(((bf16[32,48,128]{2,1,0:T(8,128)(2,1)}), bf16[32,48,128]{2,1,0:T(8,128)(2,1)S(1)}, u32[]{:S(2)}, u32[]{:S(2)}) %all-to-all-start.4) | async-done | bytes 393248 | tf_op jit(solution)/shard_map/all_to_all | solution.py:342
  150.3 0.8 shard_map.108.sums
  151.1 1.1 reduce-scatter.2.cloned.1.call-done.part
  152.2 1.0 copy-done.1
  153.1 1.3 shard_map.109
  154.4 10.0 %all-to-all-start.5 = ((bf16[32,64,128]{2,1,0:T(8,128)(2,1)}), bf16[32,64,128]{2,1,0:T(8,128)(2,1)S(1)}, u32[]{:S(2)}, u32[]{:S(2)}) async-start(bf16[32,64,128]{2,1,0:T(8,128)(2,1)} %shard_map.109), calls=%async_computation.6 | async-start | bytes 1048576 | tf_op jit(solution)/shard_map/all_to_all | solution.py:342
  164.4 1.1 copy.21
  165.5 13.3 %all-to-all-done.5.held = bf16[32,64,128]{2,1,0:T(8,128)(2,1)S(1)} async-done(((bf16[32,64,128]{2,1,0:T(8,128)(2,1)}), bf16[32,64,128]{2,1,0:T(8,128)(2,1)S(1)}, u32[]{:S(2)}, u32[]{:S(2)}) %all-to-all-start.5) | async-done | bytes 524320 | tf_op jit(solution)/shard_map/all_to_all | solution.py:342
  178.8 0.7 shard_map.110
  (17 shorter events, 0.1 us)
Async XLA Ops:
  7.2 61.2 %all-gather.2.cloned.1.call-start = ((), (), s32[]{:S(2)}) async-start(), calls=%async_computation.7 | async-start | bytes 2949120 | tf_op jit(solution)/shard_map/all_gather | solution.py:374
  7.9 0.9 copy-start.4
  8.8 0.7 copy-start.5
  9.5 37.3 %copy-start.9 = (bf16[1,128,2560]{2,1,0:T(8,128)(2,1)S(1)}, bf16[1,128,2560]{2,1,0:T(8,128)(2,1)}, u32[]{:S(2)}) copy-start(bf16[1,128,2560]{2,1,0:T(8,128)(2,1)} %param.6) | copy-start | bytes 1966084
  41.0 0.5 copy-start.6
  41.5 19.0 %all-to-all-start.1 = ((bf16[32,48,128]{2,1,0:T(8,128)(2,1)}), bf16[32,48,128]{2,1,0:T(8,128)(2,1)S(1)}, u32[]{:S(2)}, u32[]{:S(2)}) async-start(bf16[32,48,128]{2,1,0:T(8,128)(2,1)} %get-tuple-element.22), calls=%async_computation.1 | async-start | bytes 786432 | tf_op jit(solution)/shard_map/all_to_all | solution.py:342
  46.7 105.5 %reduce-scatter.2.cloned.1.call-start = ((), (), s32[]{:S(2)}) async-start(), calls=%async_computation.8 | async-start | bytes 2949120 | tf_op jit(solution)/shard_map/reduce_scatter | solution.py:411
  60.5 0.8 copy-start.10
  68.3 2.5 %copy-start.11 = (bf16[8,4,48,128]{3,2,1,0:T(8,128)(2,1)S(1)}, bf16[8,4,48,128]{3,2,1,0:T(8,128)(2,1)}, u32[]{:S(2)}) copy-start(bf16[8,4,48,128]{3,2,1,0:T(8,128)(2,1)} %get-tuple-element.24) | copy-start | bytes 1179652
  68.3 26.2 %copy-start.7 = (s32[64]{0:T(128)S(1)}, s32[64]{0:T(128)}, u32[]{:S(2)}) copy-start(s32[64]{0:T(128)} %copy-done.6) | copy-start | bytes 772
  70.7 48.2 %copy-start.12 = (bf16[128,512]{1,0:T(8,128)(2,1)}, bf16[128,512]{1,0:T(8,128)(2,1)S(1)}, u32[]{:S(2)}) copy-start(bf16[128,512]{1,0:T(8,128)(2,1)S(1)} %fusion.value_own) | copy-start | bytes 393220
  70.8 46.1 %copy-start.3 = (bf16[128,512]{1,0:T(8,128)(2,1)S(1)}, bf16[128,512]{1,0:T(8,128)(2,1)}, u32[]{:S(2)}) copy-start(bf16[128,512]{1,0:T(8,128)(2,1)} %get-tuple-element.27.own) | copy-start | bytes 393220
  116.8 2.2 %copy-start = (bf16[32,64,128]{2,1,0:T(8,128)(2,1)}, bf16[32,64,128]{2,1,0:T(8,128)(2,1)S(1)}, u32[]{:S(2)}) copy-start(bf16[32,64,128]{2,1,0:T(8,128)(2,1)S(1)} %all_to_all.32) | copy-start | bytes 1572868
  131.4 18.9 %all-to-all-start.4 = ((bf16[32,48,128]{2,1,0:T(8,128)(2,1)}), bf16[32,48,128]{2,1,0:T(8,128)(2,1)S(1)}, u32[]{:S(2)}, u32[]{:S(2)}) async-start(bf16[32,48,128]{2,1,0:T(8,128)(2,1)} %bitcast.42), calls=%async_computation.5 | async-start | bytes 786432 | tf_op jit(solution)/shard_map/all_to_all | solution.py:342
  139.6 10.7 %copy-start.8 = (s32[64]{0:T(128)S(1)}, s32[64]{0:T(128)}, u32[]{:S(2)}) copy-start(s32[64]{0:T(128)} %copy-done.6) | copy-start | bytes 772
  140.2 38.7 %copy-start.2 = (bf16[128,512]{1,0:T(8,128)(2,1)S(1)}, bf16[128,512]{1,0:T(8,128)(2,1)}, u32[]{:S(2)}) copy-start(bf16[128,512]{1,0:T(8,128)(2,1)} %get-tuple-element.33.key_own) | copy-start | bytes 393220
  152.2 1.0 copy-start.1
  154.4 24.4 %all-to-all-start.5 = ((bf16[32,64,128]{2,1,0:T(8,128)(2,1)}), bf16[32,64,128]{2,1,0:T(8,128)(2,1)S(1)}, u32[]{:S(2)}, u32[]{:S(2)}) async-start(bf16[32,64,128]{2,1,0:T(8,128)(2,1)} %shard_map.109), calls=%async_computation.6 | async-start | bytes 1048576 | tf_op jit(solution)/shard_map/all_to_all | solution.py:342
Sparse Core Ops, SparseCore 0:
  39.2 25.3 all-gather.1
  119.1 33.0 reduce-scatter.1

commit v5 on v4

--- a/solution.py
+++ b/solution.py
@@ -4,6 +4,7 @@
 import jax.numpy as jnp
 from jax import lax
 from jax.experimental import pallas as pl
+from jax.experimental.layout import Layout, with_layout_constraint
 from jax.experimental.pallas import tpu as pltpu
 from jax.sharding import PartitionSpec as P
 
@@ -210,7 +211,7 @@
     return lax.dot_general(lhs, rhs, (((left,), (right,)), ((), ())), preferred_element_type=F32)
 
 
-def masks_of(table, own, bias):
+def masks_of(present, bias):
     seg = bias.shape[0]
 
     @pl.when(pl.program_id(0) == 0)
@@ -219,9 +220,7 @@
         query_ids = lax.broadcasted_iota(jnp.int32, bias.shape, 1) % seg
         bias[...] = jnp.where(key_ids <= query_ids, 0.0, -1e30)
 
-    nodes = table.shape[0] // (SLOTS - 1)
-    present = [own[0] > 0] + [table[slot * nodes + own[0]] >= 0 for slot in range(SLOTS - 1)]
-    return [jnp.where(here, 0.0, -1e30).astype(F32) for here in present]
+    return [jnp.where(present[slot] > 0, 0.0, -1e30).astype(F32) for slot in range(SLOTS)]
 
 
 def scores_of(keys, queries, levels, bias):
@@ -235,10 +234,10 @@
 
 
 def probs_kernel(
-    table, own, query, grad, key_pieces, key_own, stats, value_pieces, value_own, bias, low
+    present, query, grad, key_pieces, key_own, stats, value_pieces, value_own, bias, low
 ):
     seg = query.shape[0]
-    levels = masks_of(table, own, bias)
+    levels = masks_of(present, bias)
     keys = rows_of(key_pieces, key_own)
     for index in range(GROUPS // 2):
         at = slice(index * 2 * seg, (index + 1) * 2 * seg)
@@ -254,11 +253,11 @@
 
 
 def grads_kernel(
-    table, own, query, grad, stats, key_pieces, key_own, value_pieces, value_own,
+    present, query, grad, stats, key_pieces, key_own, value_pieces, value_own,
     output, query_grad, grad_pieces, grad_own, bias,
 ):
     seg = query.shape[0]
-    levels = masks_of(table, own, bias)
+    levels = masks_of(present, bias)
     keys = rows_of(key_pieces, key_own)
     values = rows_of(value_pieces, value_own)
     keys_t, values_t = keys.T, values.T
@@ -384,10 +383,12 @@
         scalar_outs=1,
     )
     key_pieces = swap(second).reshape(blocks, HK, slots, DH)
-    place = [table, lax.axis_index("leaf").astype(jnp.int32).reshape(1)]
+    own = lax.axis_index("leaf")
+    here = (table.reshape(SLOTS - 1, n_leaf) >= 0) & (jnp.arange(n_leaf) == own)
+    present = jnp.concatenate([(own > 0)[None], jnp.any(here, axis=1)]).astype(jnp.int32)
     stats, value_terms, value_term_own = attention(
         probs_kernel,
-        place,
+        [present],
         [query, grad, key_pieces, keys],
         [
             shape((HK, 8, GROUPS * seg), F32),
@@ -411,7 +412,7 @@
     weight_part = lax.psum_scatter(weight_part, "grp", scatter_dimension=0, tiled=True)
     output, query_grad, key_terms, key_term_own = attention(
         grads_kernel,
-        place,
+        [present],
         [query, grad, stats, key_pieces, keys, fourth, values],
         [
             shape((seg, HQ * DH), BF),
@@ -425,7 +426,9 @@
     )
     hidden_grad = dot(value_grad, weight, 1, 1).astype(BF)
     hidden_grad = hidden_grad.reshape(seg, n_grp, n_leaf, own_rows).transpose(0, 2, 1, 3)
-    hidden_grad = hidden_grad.reshape(seg, depth)
+    hidden_grad = with_layout_constraint(
+        hidden_grad.reshape(1, seg, depth), Layout(major_to_minor=(0, 1, 2))
+    )
 
     fifth = swap(key_terms.reshape(-1, slots, DH))
 
@@ -448,7 +451,7 @@
         [shape((seg, width), BF), shape((own_rows, width), F32)],
         [pltpu.VMEM((tail, DH), F32)],
     )
-    return (output[None], query_grad[None], key_grad[None], hidden_grad[None], weight_grad)
+    return (output[None], query_grad[None], key_grad[None], hidden_grad, weight_grad)
 
 
 def solution(mesh):

time: 188 us -> 187 us (level)
  blocking collectives: 73.4 us -> 98.2 us
  waiting for transfers between devices: 37.1 us -> 21.8 us
  starting transfers between devices: 20.4 us -> 10.4 us
    all_to_all x3 -> x4, blocking collectives: 73.4 us -> 98.2 us  [swap(): return lax.all_to_all(array, 'leaf', 0, 0, tiled=True)]
    all_to_all x3 -> x2, waiting for transfers between devices: 35.9 us -> 20.7 us  [swap(): return lax.all_to_all(array, 'leaf', 0, 0, tiled=True)]
    all_to_all x3 -> x2, starting transfers between devices: 20.4 us -> 10.4 us  [swap(): return lax.all_to_all(array, 'leaf', 0, 0, tiled=True)]
    unnamed x27 -> x20, local copies, waits for them, and re-layouts: 4.98 us -> 3.38 us
  transfers between devices with their start and end apart: 5 -> 4, of which waited for: 4 -> 3; matrix products, arithmetic and copies ran while one was open for 3% -> 4% of each run, Pallas kernels for 12% -> 12%
where the time goes in v5:
time: 187 us; the launch traced here: 185 us
  blocking collectives  98.2 us (53%)
  Pallas kernels  27.5 us (15%)
  waiting for transfers between devices  21.8 us (12%)
  between operations  14.9 us (8%)
  starting transfers between devices  10.4 us (6%)
  local copies, waits for them, and re-layouts  6.62 us (4%)
  matrix products  5.13 us (3%)
    all_to_all x4, blocking collectives, swap(): return lax.all_to_all(array, 'leaf', 0, 0, tiled=True)  98.2 us
    all_to_all x2, waiting for transfers between devices, swap(): return lax.all_to_all(array, 'leaf', 0, 0, tiled=True)  20.7 us
    pallas_call x2, Pallas kernels, attention(): pl.pallas_call(kernel, grid=(HK,), out_shape=outs, in_specs=[pl.BlockSpec...  19.5 us
    all_to_all x2, starting transfers between devices, swap(): return lax.all_to_all(array, 'leaf', 0, 0, tiled=True)  10.4 us
    pallas_call x7, Pallas kernels, plain(): pl.pallas_call(kernel, out_shape=outs, in_specs=[smem] * scalars + [vmem]...  5.86 us
    dot_general x2, matrix products, dot(): lax.dot_general(lhs, rhs, (((left,), (right,)), ((), ())), preferred_elem...  5.13 us
  transfers between devices with their start and end apart: 4, of which 3 were waited for; matrix products, arithmetic and copies ran while one was open for 4% of the time, Pallas kernels for 12%

profile of v5, /device:TPU:32, one launch (start us, length us, event | category | flops | bytes accessed | tf_op | source)
XLA Modules:
  0.0 185.4 jit_solution(3078579540637593514)
XLA Ops:
  7.2 0.0 all-gather.2.cloned.1.call-start
  7.9 0.0 copy-start.4
  7.9 0.9 copy-done.4
  8.8 0.7 copy-done.5
  9.5 28.3 %all_to_all.30.held = bf16[32,64,128]{2,1,0:T(8,128)(2,1)S(1)} all-to-all(bf16[32,64,128]{2,1,0:T(8,128)(2,1)S(1)} %shard_map.101), channel_id=1, replica_groups=mesh['leaf'=32,'grp'=8] {'leaf'}, dimensions={0} | all-to-all | bytes 1048576 | tf_op jit(solution)/shard_map/all_to_all | solution.py:341
  37.9 1.2 shard_map.104
  39.1 0.0 all-gather.2.cloned.1.call-update
  39.1 1.8 shard_map.102
  41.0 5.2 %all-to-all-start.1 = ((bf16[32,48,128]{2,1,0:T(8,128)(2,1)}), bf16[32,48,128]{2,1,0:T(8,128)(2,1)S(1)}, u32[]{:S(2)}, u32[]{:S(2)}) async-start(bf16[32,48,128]{2,1,0:T(8,128)(2,1)} %get-tuple-element.22), calls=%async_computation.1 | async-start | bytes 786432 | tf_op jit(solution)/shard_map/all_to_all | solution.py:341
  46.2 0.0 reduce-scatter.2.cloned.1.call-start
  46.2 0.0 copy-done.6
  46.2 0.3 copy.15
  46.6 0.2 reshape.49
  46.8 0.2 copy.16
  47.0 0.2 reshape.50.columns
  47.3 0.1 ge.11
  47.3 0.1 and_reduce_fusion
  47.5 0.6 add_convert_fusion.present
  48.1 11.9 %all-to-all-done.1 = bf16[32,48,128]{2,1,0:T(8,128)(2,1)S(1)} async-done(((bf16[32,48,128]{2,1,0:T(8,128)(2,1)}), bf16[32,48,128]{2,1,0:T(8,128)(2,1)S(1)}, u32[]{:S(2)}, u32[]{:S(2)}) %all-to-all-start.1) | async-done | bytes 393248 | tf_op jit(solution)/shard_map/all_to_all | solution.py:341
  60.0 0.8 copy-done.7
  60.7 7.1 %shard_map.103 = (f32[4,8,1280]{2,1,0:T(8,128)}, bf16[8,4,48,128]{3,2,1,0:T(8,128)(2,1)}, bf16[128,512]{1,0:T(8,128)(2,1)}) custom-call(s32[3]{0:T(128)} %add_convert_fusion.present, bf16[128,5120]{1,0:T(8,128)(2,1)} %bitcast.42, bf16[128,5120]{1,0:T(8,128)(2,1)} %bitcast.44, bf16[8,4,48,128]{3,2,1,0:T(8,128)(2,1)} %bitcast.38, bf16[128,512]{1,0:T(8,128)(2,1)} %bitcast.30), custom_call_target="tpu_custom_call" | custom-call | flops 1342177280 | bytes 3833856 | tf_op jit(solution)/shard_map/pallas_call | solution.py:290
  67.8 0.0 all-gather.2.cloned.1.call-done
  67.9 2.4 %fusion.value_own = bf16[128,512]{1,0:T(8,128)(2,1)S(1)} fusion(bf16[2560,512]{1,0:T(8,128)(2,1)} %all-gather.2.cloned.1.call-done, bf16[2560,128]{1,0:T(8,128)(2,1)S(1)} %reshape.50.columns), kind=kOutput, calls=%fused_computation.2 | convolution fusion | flops 335609856 | bytes 3407872 | tf_op jit(solution)/shard_map/dot_general | solution.py:211
  70.3 0.0 copy-start.9
  70.3 0.0 copy-start.3
  70.3 0.0 copy-done.8
  70.4 0.1 pad_maximum_fusion
  70.4 24.1 %all_to_all.31.held = bf16[32,64,128]{2,1,0:T(8,128)(2,1)S(1)} all-to-all(bf16[32,64,128]{2,1,0:T(8,128)(2,1)S(1)} %pad_maximum_fusion), channel_id=1, replica_groups=mesh['leaf'=32,'grp'=8] {'leaf'}, dimensions={0} | all-to-all | bytes 1048576 | tf_op jit(solution)/shard_map/all_to_all | solution.py:341
  94.6 0.8 shard_map.105
  95.4 21.4 %all_to_all.32 = bf16[32,64,128]{2,1,0:T(8,128)(2,1)S(1)} all-to-all(bf16[32,64,128]{2,1,0:T(8,128)(2,1)S(1)} %shard_map.105), channel_id=1, replica_groups=mesh['leaf'=32,'grp'=8] {'leaf'}, dimensions={0} | all-to-all | bytes 1048576 | tf_op jit(solution)/shard_map/all_to_all | solution.py:341
  116.8 2.1 %shard_map.107 = (bf16[128,512]{1,0:T(8,128)(2,1)S(1)}, bf16[2560,512]{1,0:T(8,128)(2,1)}) custom-call(bf16[8,4,64,128]{3,2,1,0:T(8,128)(2,1)S(1)} %bitcast.28, bf16[128,512]{1,0:T(8,128)(2,1)S(1)} %copy-done.3, bf16[2560,128]{1,0:T(8,128)(2,1)S(1)} %reshape.50.columns), custom_call_target="tpu_custom_call" | custom-call | flops 335544320 | bytes 3276800 | tf_op jit(solution)/shard_map/pallas_call | solution.py:309
  118.9 0.0 reduce-scatter.2.cloned.1.call-update
  119.0 12.4 %shard_map.106 = (bf16[128,5120]{1,0:T(8,128)(2,1)}, bf16[128,5120]{1,0:T(8,128)(2,1)}, bf16[8,4,48,128]{3,2,1,0:T(8,128)(2,1)}, bf16[128,512]{1,0:T(8,128)(2,1)}) custom-call(s32[3]{0:T(128)} %add_convert_fusion.present, bf16[128,5120]{1,0:T(8,128)(2,1)} %bitcast.43, bf16[128,5120]{1,0:T(8,128)(2,1)} %bitcast.45, f32[4,8,1280]{2,1,0:T(8,128)} %get-tuple-element.23.stats, ...), custom_call_target="tpu_custom_call" | custom-call | flops 3355443200 | bytes 7110656 | tf_op jit(solution)/shard_map/pallas_call | solution.py:290
  131.4 5.1 %all-to-all-start.4 = ((bf16[32,48,128]{2,1,0:T(8,128)(2,1)}), bf16[32,48,128]{2,1,0:T(8,128)(2,1)S(1)}, u32[]{:S(2)}, u32[]{:S(2)}) async-start(bf16[32,48,128]{2,1,0:T(8,128)(2,1)} %bitcast.40), calls=%async_computation.5 | async-start | bytes 786432 | tf_op jit(solution)/shard_map/all_to_all | solution.py:341
  136.6 2.7 %convolution_convert_fusion = bf16[128,2560]{1,0:T(8,128)(2,1)S(1)} fusion(bf16[128,512]{1,0:T(8,128)(2,1)S(1)} %get-tuple-element.29, bf16[2560,512]{1,0:T(8,128)(2,1)} %all-gather.2.cloned.1.call-done), kind=kOutput, calls=%fused_computation | convolution fusion | flops 335872000 | bytes 3407872 | tf_op jit(solution)/shard_map/dot_general | solution.py:211
  139.3 0.3 copy.19
  139.6 0.2 reshape.54
  139.9 0.3 copy.20
  140.2 0.0 copy-start.2
  140.2 0.2 reshape.55
  140.4 1.1 copy.21
  141.5 8.8 %all-to-all-done.4.held = bf16[32,48,128]{2,1,0:T(8,128)(2,1)S(1)} async-done(((bf16[32,48,128]{2,1,0:T(8,128)(2,1)}), bf16[32,48,128]{2,1,0:T(8,128)(2,1)S(1)}, u32[]{:S(2)}, u32[]{:S(2)}) %all-to-all-start.4) | async-done | bytes 393248 | tf_op jit(solution)/shard_map/all_to_all | solution.py:341
  150.3 0.8 shard_map.108.sums
  151.1 1.1 reduce-scatter.2.cloned.1.call-done.part
  152.2 1.0 copy-done.1
  153.1 0.5 shard_map.109
  153.6 24.2 %all_to_all.33.held = bf16[32,64,128]{2,1,0:T(8,128)(2,1)S(1)} all-to-all(bf16[32,64,128]{2,1,0:T(8,128)(2,1)S(1)} %shard_map.109), channel_id=1, replica_groups=mesh['leaf'=32,'grp'=8] {'leaf'}, dimensions={0} | all-to-all | bytes 1048576 | tf_op jit(solution)/shard_map/all_to_all | solution.py:341
  177.8 0.7 shard_map.110
  (15 shorter events, 0.1 us)
Async XLA Ops:
  7.2 60.7 %all-gather.2.cloned.1.call-start = ((), (), s32[]{:S(2)}) async-start(), calls=%async_computation.7 | async-start | bytes 2949120 | tf_op jit(solution)/shard_map/all_gather | solution.py:373
  7.9 0.9 copy-start.4
  8.8 0.7 copy-start.5
  9.5 36.8 %copy-start.6 = (bf16[1,128,2560]{2,1,0:T(8,128)(2,1)S(1)}, bf16[1,128,2560]{2,1,0:T(8,128)(2,1)}, u32[]{:S(2)}) copy-start(bf16[1,128,2560]{2,1,0:T(8,128)(2,1)} %param.6) | copy-start | bytes 1966084
  41.0 19.0 %all-to-all-start.1 = ((bf16[32,48,128]{2,1,0:T(8,128)(2,1)}), bf16[32,48,128]{2,1,0:T(8,128)(2,1)S(1)}, u32[]{:S(2)}, u32[]{:S(2)}) async-start(bf16[32,48,128]{2,1,0:T(8,128)(2,1)} %get-tuple-element.22), calls=%async_computation.1 | async-start | bytes 786432 | tf_op jit(solution)/shard_map/all_to_all | solution.py:341
  46.2 106.0 %reduce-scatter.2.cloned.1.call-start = ((), (), s32[]{:S(2)}) async-start(), calls=%async_computation.8 | async-start | bytes 2949120 | tf_op jit(solution)/shard_map/reduce_scatter | solution.py:412
  60.0 0.8 copy-start.7
  67.8 2.5 %copy-start.8 = (bf16[8,4,48,128]{3,2,1,0:T(8,128)(2,1)S(1)}, bf16[8,4,48,128]{3,2,1,0:T(8,128)(2,1)}, u32[]{:S(2)}) copy-start(bf16[8,4,48,128]{3,2,1,0:T(8,128)(2,1)} %get-tuple-element.24) | copy-start | bytes 1179652
  70.3 48.7 %copy-start.9 = (bf16[128,512]{1,0:T(8,128)(2,1)}, bf16[128,512]{1,0:T(8,128)(2,1)S(1)}, u32[]{:S(2)}) copy-start(bf16[128,512]{1,0:T(8,128)(2,1)S(1)} %fusion.value_own) | copy-start | bytes 393220
  70.3 46.6 %copy-start.3 = (bf16[128,512]{1,0:T(8,128)(2,1)S(1)}, bf16[128,512]{1,0:T(8,128)(2,1)}, u32[]{:S(2)}) copy-start(bf16[128,512]{1,0:T(8,128)(2,1)} %get-tuple-element.27.own) | copy-start | bytes 393220
  116.8 2.1 %copy-start = (bf16[32,64,128]{2,1,0:T(8,128)(2,1)}, bf16[32,64,128]{2,1,0:T(8,128)(2,1)S(1)}, u32[]{:S(2)}) copy-start(bf16[32,64,128]{2,1,0:T(8,128)(2,1)S(1)} %all_to_all.32) | copy-start | bytes 1572868
  131.4 18.9 %all-to-all-start.4 = ((bf16[32,48,128]{2,1,0:T(8,128)(2,1)}), bf16[32,48,128]{2,1,0:T(8,128)(2,1)S(1)}, u32[]{:S(2)}, u32[]{:S(2)}) async-start(bf16[32,48,128]{2,1,0:T(8,128)(2,1)} %bitcast.40), calls=%async_computation.5 | async-start | bytes 786432 | tf_op jit(solution)/shard_map/all_to_all | solution.py:341
  140.2 37.7 %copy-start.2 = (bf16[128,512]{1,0:T(8,128)(2,1)S(1)}, bf16[128,512]{1,0:T(8,128)(2,1)}, u32[]{:S(2)}) copy-start(bf16[128,512]{1,0:T(8,128)(2,1)} %get-tuple-element.33.key_own) | copy-start | bytes 393220
  152.2 1.0 copy-start.1
Sparse Core Ops, SparseCore 0:
  39.2 25.3 all-gather.1
  119.1 33.0 reduce-scatter.1

commit v6 on v5

--- a/solution.py
+++ b/solution.py
@@ -44,7 +44,7 @@
 
 def pack_kernel(own_rows, parent, keys, weight, sent, rows):
     count = HK * own_rows
-    rows[...] = jnp.full(rows.shape, parent[0, 0].astype(F32), F32)
+    rows[...] = jnp.broadcast_to(parent[...].astype(F32), rows.shape)
     for head in range(HK):
         rows[head * own_rows : (head + 1) * own_rows, :] = weight[
             :, head * DH : (head + 1) * DH
@@ -147,20 +147,7 @@
         ]
 
 
-def project_kernel(pieces, own, columns, value_grad, part):
-    @pl.when(pl.program_id(0) == 0)
-    def _():
-        for block in range(pieces.shape[0]):
-            for head in range(HK):
-                at = (slice(block * TILE, (block + 1) * TILE), slice(head * DH, (head + 1) * DH))
-                value_grad[at] = (
-                    pieces[block, head].astype(F32) + own[at].astype(F32)
-                ).astype(BF)
-
-    part[...] = dot(columns[...], value_grad[...], 1, 0).astype(BF)
-
-
-def plain(kernel, arrays, outs, scratch=(), scalars=0, scalar_outs=0, flops=0):
+def plain(kernel, arrays, outs, scratch=(), scalars=0, scalar_outs=0, limit=VMEM_LIMIT):
     smem, vmem = pl.BlockSpec(memory_space=pltpu.SMEM), pl.BlockSpec(memory_space=pltpu.VMEM)
     moved = sum(a.size * a.dtype.itemsize for a in list(arrays) + list(outs))
     return pl.pallas_call(
@@ -169,8 +156,8 @@
         in_specs=[smem] * scalars + [vmem] * (len(arrays) - scalars),
         out_specs=[vmem] * (len(outs) - scalar_outs) + [smem] * scalar_outs,
         scratch_shapes=list(scratch),
-        compiler_params=pltpu.CompilerParams(vmem_limit_bytes=VMEM_LIMIT),
-        cost_estimate=pl.CostEstimate(flops=flops, bytes_accessed=moved, transcendentals=0),
+        compiler_params=pltpu.CompilerParams(vmem_limit_bytes=limit),
+        cost_estimate=pl.CostEstimate(flops=0, bytes_accessed=moved, transcendentals=0),
     )(*arrays)
 
 
@@ -234,7 +221,7 @@
 
 
 def probs_kernel(
-    present, query, grad, key_pieces, key_own, stats, value_pieces, value_own, bias, low
+    present, query, grad, key_pieces, key_own, probs, value_pieces, value_own, bias, low
 ):
     seg = query.shape[0]
     levels = masks_of(present, bias)
@@ -242,37 +229,31 @@
     for index in range(GROUPS // 2):
         at = slice(index * 2 * seg, (index + 1) * 2 * seg)
         scores = scores_of(keys, pair(query, index), levels, bias)
-        top = jnp.max(scores, axis=0, keepdims=True)
-        weight = jnp.exp2(scores - top)
-        norm = 1.0 / jnp.sum(weight, axis=0, keepdims=True)
-        stats[0, 0:1, at] = top
-        stats[0, 1:2, at] = norm
-        low[:, at] = (weight * norm).astype(BF)
-    total = dot(low[...], heads_of(grad), 1, 0)
-    put_rows(value_pieces, value_own, total)
+        weight = jnp.exp2(scores - jnp.max(scores, axis=0, keepdims=True))
+        prob = weight * (1.0 / jnp.sum(weight, axis=0, keepdims=True))
+        probs[0, :, at] = prob
+        low[:, at] = prob.astype(BF)
+    put_rows(value_pieces, value_own, dot(low[...], heads_of(grad), 1, 0))
 
 
 def grads_kernel(
-    present, query, grad, stats, key_pieces, key_own, value_pieces, value_own,
-    output, query_grad, grad_pieces, grad_own, bias,
+    query, grad, probs, key_pieces, key_own, value_pieces, value_own,
+    output, query_grad, grad_pieces, grad_own, low,
 ):
     seg = query.shape[0]
-    levels = masks_of(present, bias)
     keys = rows_of(key_pieces, key_own)
     values = rows_of(value_pieces, value_own)
     keys_t, values_t = keys.T, values.T
-    total = jnp.zeros((keys.shape[0], DH), F32)
     for index in range(GROUPS // 2):
         at = slice(index * 2 * seg, (index + 1) * 2 * seg)
-        queries = pair(query, index)
-        scores = scores_of(keys, queries, levels, bias)
-        prob = jnp.exp2(scores - stats[0, 0:1, at]) * stats[0, 1:2, at]
+        prob = probs[0, :, at]
         dprob = dot(values, pair(grad, index), 1, 1)
         delta = jnp.sum(prob * dprob, axis=0, keepdims=True)
         dscore = (prob * (dprob - delta)).astype(BF)
-        total += dot(dscore, queries, 1, 0)
+        low[:, at] = dscore
         put_pair(output, index, dot(values_t, prob.astype(BF), 1, 0).astype(BF).T)
         put_pair(query_grad, index, (dot(keys_t, dscore, 1, 0) * (1.0 / DH**0.5)).astype(BF).T)
+    total = dot(low[...], heads_of(query), 1, 0)
     put_rows(grad_pieces, grad_own, total * (1.0 / DH**0.5))
 
 
@@ -302,33 +283,50 @@
     )(*lead, *arrays)
 
 
-def project(pieces, own, columns, steps=2):
-    blocks = pieces.shape[0]
-    seg, width = own.shape
-    depth = columns.shape[0]
+def share_kernel(which, pieces, own, columns, value_grad, part):
+    @pl.when(pl.program_id(0) == 0)
+    def _():
+        for block in range(pieces.shape[0]):
+            for head in range(HK):
+                at = (slice(block * TILE, (block + 1) * TILE), slice(head * DH, (head + 1) * DH))
+                value_grad[at] = (
+                    pieces[block, head].astype(F32) + own[at].astype(F32)
+                ).astype(BF)
+
+    part[...] = dot(columns[...], value_grad[...], 1, 0).astype(BF)
+
+
+def combine_kernel(which, value_grad, columns, arrived, part):
+    own = dot(columns[...], value_grad[...], 1, 0)
+    part[...] = (own + arrived[...].astype(F32)).astype(BF)
+
+
+def share(kernel, which, first, columns, rest, outs, n_grp):
+    rows = columns.shape[0] // n_grp
+
+    def spec(shape):
+        if len(shape) == 4:
+            return pl.BlockSpec(shape[:2] + (TILE, DH), lambda i, which: (0, 0, SLOTS, 0))
+        if shape[0] == columns.shape[1]:
+            return pl.BlockSpec(shape, lambda i, which: (0, 0))
+        return pl.BlockSpec((rows, shape[1]), lambda i, which: (i, 0))
+
     return pl.pallas_call(
-        project_kernel,
-        grid=(steps,),
-        out_shape=[
-            jax.ShapeDtypeStruct((seg, width), BF),
-            jax.ShapeDtypeStruct((depth, width), BF),
-        ],
-        in_specs=[
-            pl.BlockSpec((blocks, HK, TILE, DH), lambda i: (0, 0, SLOTS, 0)),
-            pl.BlockSpec((seg, width), lambda i: (0, 0)),
-            pl.BlockSpec((depth // steps, seg), lambda i: (i, 0)),
-        ],
-        out_specs=[
-            pl.BlockSpec((seg, width), lambda i: (0, 0)),
-            pl.BlockSpec((depth // steps, width), lambda i: (i, 0)),
-        ],
+        kernel,
+        out_shape=outs,
+        grid_spec=pltpu.PrefetchScalarGridSpec(
+            num_scalar_prefetch=1,
+            grid=(n_grp // 2,),
+            in_specs=[spec(a.shape) for a in first]
+            + [pl.BlockSpec((rows, columns.shape[1]), lambda i, which: (2 * i + which[0], 0))]
+            + [spec(a.shape) for a in rest],
+            out_specs=[spec(o.shape) for o in outs],
+        ),
         compiler_params=pltpu.CompilerParams(vmem_limit_bytes=VMEM_LIMIT),
         cost_estimate=pl.CostEstimate(
-            flops=2 * seg * width * depth,
-            bytes_accessed=2 * depth * (width + seg),
-            transcendentals=0,
+            flops=columns.size * 512, bytes_accessed=columns.size * 5, transcendentals=0
         ),
-    )(pieces, own, columns)
+    )(which, *first, columns, *rest)
 
 
 def to_pieces(rows):
@@ -355,13 +353,14 @@
 
     columns = hidden.T.reshape(n_leaf, n_grp, own_rows, seg).transpose(1, 0, 2, 3)
     columns = columns.reshape(depth, seg)
+    core = lax.axis_index("grp").astype(jnp.int32).reshape(1) % 2
 
     (first,) = plain(
         functools.partial(pack_kernel, own_rows),
         [parent_links, keys, value_weight],
         [shape((n_leaf, TILE + tail, DH), BF)],
         [pltpu.VMEM((tail, DH), F32)],
-        scalars=1,
+        limit=ATTENTION_LIMIT,
     )
     first = swap(first)
 
@@ -386,12 +385,12 @@
     own = lax.axis_index("leaf")
     here = (table.reshape(SLOTS - 1, n_leaf) >= 0) & (jnp.arange(n_leaf) == own)
     present = jnp.concatenate([(own > 0)[None], jnp.any(here, axis=1)]).astype(jnp.int32)
-    stats, value_terms, value_term_own = attention(
+    probs, value_terms, value_term_own = attention(
         probs_kernel,
         [present],
         [query, grad, key_pieces, keys],
         [
-            shape((HK, 8, GROUPS * seg), F32),
+            shape((HK, 4 * seg, GROUPS * seg), F32),
             shape((blocks, HK, slots, DH), BF),
             shape((seg, width), BF),
         ],
@@ -408,21 +407,40 @@
         value_kernel, [table, third], [shape((n_leaf, slots + TILE, DH), BF)], totals, scalars=1
     )
     fourth = swap(fourth).reshape(blocks, HK, slots + TILE, DH)
-    value_grad, weight_part = project(fourth, value_term_own, columns)
-    weight_part = lax.psum_scatter(weight_part, "grp", scatter_dimension=0, tiled=True)
+    half = shape((depth // 2, width), BF)
+    value_grad, weight_part = share(
+        share_kernel,
+        1 - core,
+        [fourth, value_term_own],
+        columns,
+        [],
+        [shape((seg, width), BF), half],
+        n_grp,
+    )
+    weight_part = lax.ppermute(weight_part, "grp", [(i, i ^ 1) for i in range(n_grp)])
+    (weight_part,) = share(
+        combine_kernel, core, [value_grad], columns, [weight_part], [half], n_grp
+    )
+    weight_part = lax.psum_scatter(
+        weight_part,
+        "grp",
+        scatter_dimension=0,
+        axis_index_groups=[list(range(c, n_grp, 2)) for c in range(2)],
+        tiled=True,
+    )
     output, query_grad, key_terms, key_term_own = attention(
         grads_kernel,
-        [present],
-        [query, grad, stats, key_pieces, keys, fourth, values],
+        [],
+        [query, grad, probs, key_pieces, keys, fourth, values],
         [
             shape((seg, HQ * DH), BF),
             shape((seg, HQ * DH), BF),
             shape((blocks, HK, slots, DH), BF),
             shape((seg, width), BF),
         ],
-        [pltpu.VMEM((seg, 2 * seg), F32)],
-        5 * flops,
-        HQ * seg * 4 * seg,
+        [pltpu.VMEM((4 * seg, GROUPS * seg), BF)],
+        4 * flops,
+        0,
     )
     hidden_grad = dot(value_grad, weight, 1, 1).astype(BF)
     hidden_grad = hidden_grad.reshape(seg, n_grp, n_leaf, own_rows).transpose(0, 2, 1, 3)

time: 187 us -> 187 us (level)
  blocking collectives: 98.2 us -> 72.5 us
  waiting for transfers between devices: 21.8 us -> 41.5 us
  starting transfers between devices: 10.4 us -> 15.5 us
  Pallas kernels: 27.5 us -> 30.3 us
    all_to_all x4 -> x3, blocking collectives: 98.2 us -> 72.5 us  [swap(): return lax.all_to_all(array, 'leaf', 0, 0, tiled=True)]
    all_to_all x2 -> x3, waiting for transfers between devices: 20.7 us -> 38.4 us  [swap(): return lax.all_to_all(array, 'leaf', 0, 0, tiled=True)]
    all_to_all x2 -> x3, starting transfers between devices: 10.4 us -> 15.3 us  [swap(): return lax.all_to_all(array, 'leaf', 0, 0, tiled=True)]
    ppermute x0 -> x1, waiting for transfers between devices: none -> 3.02 us  [shards(): lax.ppermute(weight_part, 'grp', [(i, i ^ 1) for i in range(n_grp)])]
    pallas_call x7, Pallas kernels: 5.86 us -> 8.4 us  [plain(): pl.pallas_call(kernel, out_shape=outs, in_specs=[smem] * scalars + [vmem]...]
  transfers between devices with their start and end apart: 4 -> 6, of which waited for: 3 -> 4; matrix products, arithmetic and copies ran while one was open for 4% -> 4% of each run, Pallas kernels for 12% -> 11%
where the time goes in v6:
time: 187 us; the launch traced here: 186 us
  blocking collectives  72.5 us (39%)
  waiting for transfers between devices  41.5 us (22%)
  Pallas kernels  30.3 us (16%)
  starting transfers between devices  15.5 us (8%)
  between operations  15 us (8%)
  matrix products  5.11 us (3%)
  local copies, waits for them, and re-layouts  4.99 us (3%)
    all_to_all x3, blocking collectives, swap(): return lax.all_to_all(array, 'leaf', 0, 0, tiled=True)  72.5 us
    all_to_all x3, waiting for transfers between devices, swap(): return lax.all_to_all(array, 'leaf', 0, 0, tiled=True)  38.4 us
    pallas_call x2, Pallas kernels, attention(): pl.pallas_call(kernel, grid=(HK,), out_shape=outs, in_specs=[pl.BlockSpec...  18.7 us
    all_to_all x3, starting transfers between devices, swap(): return lax.all_to_all(array, 'leaf', 0, 0, tiled=True)  15.3 us
    pallas_call x7, Pallas kernels, plain(): pl.pallas_call(kernel, out_shape=outs, in_specs=[smem] * scalars + [vmem]...  8.4 us
    dot_general x2, matrix products, dot(): lax.dot_general(lhs, rhs, (((left,), (right,)), ((), ())), preferred_elem...  5.11 us
  transfers between devices with their start and end apart: 6, of which 4 were waited for; matrix products, arithmetic and copies ran while one was open for 4% of the time, Pallas kernels for 11%

profile of v6, /device:TPU:32, one launch (start us, length us, event | category | flops | bytes accessed | tf_op | source)
XLA Modules:
  0.0 185.7 jit_solution(3773228017347750903)
XLA Ops:
  7.2 0.0 all-gather.2.cloned.1.call-start
  7.9 1.8 shard_map.101
  9.7 28.4 %all_to_all.30.held = bf16[32,64,128]{2,1,0:T(8,128)(2,1)S(1)} all-to-all(bf16[32,64,128]{2,1,0:T(8,128)(2,1)} %shard_map.101), channel_id=1, replica_groups=mesh['leaf'=32,'grp'=8] {'leaf'}, dimensions={0} | all-to-all | bytes 1048576 | tf_op jit(solution)/shard_map/all_to_all | solution.py:339
  38.1 1.2 shard_map.104
  39.4 0.0 all-gather.2.cloned.1.call-update
  39.4 1.8 shard_map.102
  41.2 5.2 %all-to-all-start.1 = ((bf16[32,48,128]{2,1,0:T(8,128)(2,1)}), bf16[32,48,128]{2,1,0:T(8,128)(2,1)S(1)}, u32[]{:S(2)}, u32[]{:S(2)}) async-start(bf16[32,48,128]{2,1,0:T(8,128)(2,1)} %get-tuple-element.22), calls=%async_computation.1 | async-start | bytes 786432 | tf_op jit(solution)/shard_map/all_to_all | solution.py:339
  46.5 0.3 copy.15
  46.8 0.2 reshape.54
  47.0 0.2 copy.16
  47.2 0.2 reshape.55.columns
  47.5 0.1 ge.11
  47.5 0.1 and_reduce_fusion
  47.7 0.6 add_convert_fusion.present
  48.3 12.0 %all-to-all-done.1 = bf16[32,48,128]{2,1,0:T(8,128)(2,1)S(1)} async-done(((bf16[32,48,128]{2,1,0:T(8,128)(2,1)}), bf16[32,48,128]{2,1,0:T(8,128)(2,1)S(1)}, u32[]{:S(2)}, u32[]{:S(2)}) %all-to-all-start.1) | async-done | bytes 393248 | tf_op jit(solution)/shard_map/all_to_all | solution.py:339
  60.2 0.8 copy-done.4
  61.0 8.4 %shard_map.103 = (f32[4,512,1280]{2,1,0:T(8,128)}, bf16[8,4,48,128]{3,2,1,0:T(8,128)(2,1)}, bf16[128,512]{1,0:T(8,128)(2,1)}) custom-call(s32[3]{0:T(128)} %add_convert_fusion.present, bf16[128,5120]{1,0:T(8,128)(2,1)} %bitcast.35, bf16[128,5120]{1,0:T(8,128)(2,1)} %bitcast.37, bf16[8,4,48,128]{3,2,1,0:T(8,128)(2,1)} %bitcast.33, bf16[128,512]{1,0:T(8,128)(2,1)} %bitcast.41), custom_call_target="tpu_custom_call" | custom-call | flops 1342177280 | bytes 14155776 | tf_op jit(solution)/shard_map/pallas_call | solution.py:271
  69.4 0.0 all-gather.2.cloned.1.call-done
  69.4 2.4 %fusion.value_own = bf16[128,512]{1,0:T(8,128)(2,1)S(1)} fusion(bf16[2560,512]{1,0:T(8,128)(2,1)} %all-gather.2.cloned.1.call-done, bf16[2560,128]{1,0:T(8,128)(2,1)S(1)} %reshape.55.columns), kind=kOutput, calls=%fused_computation.2 | convolution fusion | flops 335609856 | bytes 3407872 | tf_op jit(solution)/shard_map/dot_general | solution.py:198
  71.8 0.0 copy-start.2
  71.9 0.1 pad_maximum_fusion
  71.9 22.9 %all_to_all.31.held = bf16[32,64,128]{2,1,0:T(8,128)(2,1)S(1)} all-to-all(bf16[32,64,128]{2,1,0:T(8,128)(2,1)S(1)} %pad_maximum_fusion), channel_id=1, replica_groups=mesh['leaf'=32,'grp'=8] {'leaf'}, dimensions={0} | all-to-all | bytes 1048576 | tf_op jit(solution)/shard_map/all_to_all | solution.py:339
  94.8 1.6 shard_map.105
  96.4 5.2 %all-to-all-start.3 = ((bf16[32,64,128]{2,1,0:T(8,128)(2,1)}), bf16[32,64,128]{2,1,0:T(8,128)(2,1)S(1)}, u32[]{:S(2)}, u32[]{:S(2)}) async-start(bf16[32,64,128]{2,1,0:T(8,128)(2,1)} %shard_map.105), calls=%async_computation.3 | async-start | bytes 1048576 | tf_op jit(solution)/shard_map/all_to_all | solution.py:339
  101.6 0.0 reduce-scatter.2.cloned.1.call-start
  101.7 16.4 %all-to-all-done.3 = bf16[32,64,128]{2,1,0:T(8,128)(2,1)S(1)} async-done(((bf16[32,64,128]{2,1,0:T(8,128)(2,1)}), bf16[32,64,128]{2,1,0:T(8,128)(2,1)S(1)}, u32[]{:S(2)}, u32[]{:S(2)}) %all-to-all-start.3) | async-done | bytes 524320 | tf_op jit(solution)/shard_map/all_to_all | solution.py:339
  118.1 0.0 copy-done.2
  118.1 1.1 shard_map.107
  119.1 0.1 collective-permute-start
  119.2 3.0 %collective-permute-done.arrived = bf16[1280,512]{1,0:T(8,128)(2,1)S(1)} collective-permute-done((bf16[1280,512]{1,0:T(8,128)(2,1)S(1)}, bf16[1280,512]{1,0:T(8,128)(2,1)S(1)}, u32[]{:S(2)}, u32[]{:S(2)}) %collective-permute-start) | collective-permute-done | bytes 1310752 | tf_op jit(solution)/shard_map/ppermute | solution.py:420
  122.3 2.2 %shard_map.108 = bf16[1280,512]{1,0:T(8,128)(2,1)} custom-call(s32[1]{0:T(128)S(6)} %select_n.7.which, bf16[128,512]{1,0:T(8,128)(2,1)S(1)} %get-tuple-element.28.value_grad, bf16[2560,128]{1,0:T(8,128)(2,1)S(1)} %reshape.55.columns, bf16[1280,512]{1,0:T(8,128)(2,1)S(1)} %collective-permute-done.arrived), custom_call_target="tpu_custom_call" | custom-call | flops 167772160 | bytes 1638400 | tf_op jit(solution)/shard_map/pallas_call | solution.py:314
  124.4 0.0 reduce-scatter.2.cloned.1.call-update
  124.5 10.3 %shard_map.106 = (bf16[128,5120]{1,0:T(8,128)(2,1)}, bf16[128,5120]{1,0:T(8,128)(2,1)}, bf16[8,4,48,128]{3,2,1,0:T(8,128)(2,1)}, bf16[128,512]{1,0:T(8,128)(2,1)}) custom-call(bf16[128,5120]{1,0:T(8,128)(2,1)} %bitcast.36, bf16[128,5120]{1,0:T(8,128)(2,1)} %bitcast.38, f32[4,512,1280]{2,1,0:T(8,128)} %get-tuple-element.23.probs, ...), custom_call_target="tpu_custom_call" | custom-call | flops 2684354560 | bytes 17432576 | tf_op jit(solution)/shard_map/pallas_call | solution.py:271
  134.8 4.9 %all-to-all-start.4 = ((bf16[32,48,128]{2,1,0:T(8,128)(2,1)}), bf16[32,48,128]{2,1,0:T(8,128)(2,1)S(1)}, u32[]{:S(2)}, u32[]{:S(2)}) async-start(bf16[32,48,128]{2,1,0:T(8,128)(2,1)} %bitcast.45), calls=%async_computation.5 | async-start | bytes 786432 | tf_op jit(solution)/shard_map/all_to_all | solution.py:339
  139.7 2.7 %convolution_convert_fusion = bf16[128,2560]{1,0:T(8,128)(2,1)S(1)} fusion(bf16[128,512]{1,0:T(8,128)(2,1)S(1)} %get-tuple-element.28.value_grad, bf16[2560,512]{1,0:T(8,128)(2,1)} %all-gather.2.cloned.1.call-done), kind=kOutput, calls=%fused_computation | convolution fusion | flops 335872000 | bytes 3407872 | tf_op jit(solution)/shard_map/dot_general | solution.py:198
  142.5 0.3 copy.19
  142.8 0.2 reshape.60
  143.0 0.3 copy.20
  143.3 0.0 copy-start.3
  143.3 0.2 reshape.61
  143.5 1.1 copy.21
  144.7 10.1 %all-to-all-done.4.held = bf16[32,48,128]{2,1,0:T(8,128)(2,1)S(1)} async-done(((bf16[32,48,128]{2,1,0:T(8,128)(2,1)}), bf16[32,48,128]{2,1,0:T(8,128)(2,1)S(1)}, u32[]{:S(2)}, u32[]{:S(2)}) %all-to-all-start.4) | async-done | bytes 393248 | tf_op jit(solution)/shard_map/all_to_all | solution.py:339
  154.7 0.8 shard_map.109.sums
  155.5 0.0 reduce-scatter.2.cloned.1.call-done.part
  155.5 1.0 copy-done.1
  156.5 0.5 shard_map.110
  156.9 21.3 %all_to_all.32.held = bf16[32,64,128]{2,1,0:T(8,128)(2,1)S(1)} all-to-all(bf16[32,64,128]{2,1,0:T(8,128)(2,1)S(1)} %shard_map.110), channel_id=1, replica_groups=mesh['leaf'=32,'grp'=8] {'leaf'}, dimensions={0} | all-to-all | bytes 1048576 | tf_op jit(solution)/shard_map/all_to_all | solution.py:339
  178.2 0.7 shard_map.111
  (15 shorter events, 0.1 us)
Async XLA Ops:
  7.2 39.3 %copy-start.5 = (bf16[1,128,2560]{2,1,0:T(8,128)(2,1)S(1)}, bf16[1,128,2560]{2,1,0:T(8,128)(2,1)}, u32[]{:S(2)}) copy-start(bf16[1,128,2560]{2,1,0:T(8,128)(2,1)} %param.6) | copy-start | bytes 1966084
  7.2 62.2 %all-gather.2.cloned.1.call-start = ((), (), s32[]{:S(2)}) async-start(), calls=%async_computation.7 | async-start | bytes 2949120 | tf_op jit(solution)/shard_map/all_gather | solution.py:372
  41.2 19.0 %all-to-all-start.1 = ((bf16[32,48,128]{2,1,0:T(8,128)(2,1)}), bf16[32,48,128]{2,1,0:T(8,128)(2,1)S(1)}, u32[]{:S(2)}, u32[]{:S(2)}) async-start(bf16[32,48,128]{2,1,0:T(8,128)(2,1)} %get-tuple-element.22), calls=%async_computation.1 | async-start | bytes 786432 | tf_op jit(solution)/shard_map/all_to_all | solution.py:339
  60.2 0.8 copy-start.4
  69.4 2.5 %copy-start.7 = (bf16[8,4,48,128]{3,2,1,0:T(8,128)(2,1)S(1)}, bf16[8,4,48,128]{3,2,1,0:T(8,128)(2,1)}, u32[]{:S(2)}) copy-start(bf16[8,4,48,128]{3,2,1,0:T(8,128)(2,1)} %get-tuple-element.24) | copy-start | bytes 1179652
  71.8 47.4 %copy-start.6 = (bf16[128,512]{1,0:T(8,128)(2,1)}, bf16[128,512]{1,0:T(8,128)(2,1)S(1)}, u32[]{:S(2)}) copy-start(bf16[128,512]{1,0:T(8,128)(2,1)S(1)} %fusion.value_own) | copy-start | bytes 393220
  71.8 46.3 %copy-start.2 = (bf16[128,512]{1,0:T(8,128)(2,1)S(1)}, bf16[128,512]{1,0:T(8,128)(2,1)}, u32[]{:S(2)}) copy-start(bf16[128,512]{1,0:T(8,128)(2,1)} %get-tuple-element.27.own) | copy-start | bytes 393220
  96.4 21.6 %all-to-all-start.3 = ((bf16[32,64,128]{2,1,0:T(8,128)(2,1)}), bf16[32,64,128]{2,1,0:T(8,128)(2,1)S(1)}, u32[]{:S(2)}, u32[]{:S(2)}) async-start(bf16[32,64,128]{2,1,0:T(8,128)(2,1)} %shard_map.105), calls=%async_computation.3 | async-start | bytes 1048576 | tf_op jit(solution)/shard_map/all_to_all | solution.py:339
  101.6 53.9 %reduce-scatter.2.cloned.1.call-start = ((), (), s32[]{:S(2)}) async-start(), calls=%async_computation.8 | async-start | bytes 1638400 | tf_op jit(solution)/shard_map/reduce_scatter | solution.py:424
  118.1 6.4 %copy-start = (bf16[32,64,128]{2,1,0:T(8,128)(2,1)}, bf16[32,64,128]{2,1,0:T(8,128)(2,1)S(1)}, u32[]{:S(2)}) copy-start(bf16[32,64,128]{2,1,0:T(8,128)(2,1)S(1)} %all-to-all-done.3) | copy-start | bytes 1572868
  119.1 3.1 %collective-permute-start = (bf16[1280,512]{1,0:T(8,128)(2,1)S(1)}, bf16[1280,512]{1,0:T(8,128)(2,1)S(1)}, u32[]{:S(2)}, u32[]{:S(2)}) collective-permute-start(bf16[1280,512]{1,0:T(8,128)(2,1)S(1)} %get-tuple-element.29), channel_id=1, source_target_pairs={{0,1},{1,0},{2,3},{3,2},{4,5},{5,4},{6,7},{7,6},{8,9},{9,8},{10,11... | collective-permute-start | bytes 3932168 | tf_op jit(solution)/shard_map/ppermute | solution.py:420
  134.8 19.9 %all-to-all-start.4 = ((bf16[32,48,128]{2,1,0:T(8,128)(2,1)}), bf16[32,48,128]{2,1,0:T(8,128)(2,1)S(1)}, u32[]{:S(2)}, u32[]{:S(2)}) async-start(bf16[32,48,128]{2,1,0:T(8,128)(2,1)} %bitcast.45), calls=%async_computation.5 | async-start | bytes 786432 | tf_op jit(solution)/shard_map/all_to_all | solution.py:339
  143.3 34.9 %copy-start.3 = (bf16[128,512]{1,0:T(8,128)(2,1)S(1)}, bf16[128,512]{1,0:T(8,128)(2,1)}, u32[]{:S(2)}) copy-start(bf16[128,512]{1,0:T(8,128)(2,1)} %get-tuple-element.33.key_own) | copy-start | bytes 393220
  155.5 1.0 copy-start.1
Sparse Core Ops, SparseCore 0:
  39.5 25.3 all-gather.1
  124.6 22.6 reduce-scatter.1

commit v7 on v6

--- a/solution.py
+++ b/solution.py
@@ -257,30 +257,41 @@
     put_rows(grad_pieces, grad_own, total * (1.0 / DH**0.5))
 
 
-def attention(kernel, lead, arrays, outs, scratch, flops, transcendentals):
+def attention(
+    kernel, lead, arrays, outs, scratch, flops, transcendentals, start=0, stop=HK, into=()
+):
     def spec(shape):
         if len(shape) == 4:
-            return pl.BlockSpec((shape[0], 1) + shape[2:], lambda h: (0, h, 0, 0))
+            return pl.BlockSpec((shape[0], 1) + shape[2:], lambda h: (0, h + start, 0, 0))
         if len(shape) == 3:
-            return pl.BlockSpec((1,) + shape[1:], lambda h: (h, 0, 0))
-        return pl.BlockSpec((shape[0], shape[1] // HK), lambda h: (0, h))
+            return pl.BlockSpec((1,) + shape[1:], lambda h: (h + start, 0, 0))
+        return pl.BlockSpec((shape[0], shape[1] // HK), lambda h: (0, h + start))
+
+    given = len(lead) + len(arrays)
+
+    def run(*refs):
+        kernel(*refs[:given], *refs[given + len(into) :])
 
     moved = sum(a.size * a.dtype.itemsize for a in arrays) + sum(
         o.size * o.dtype.itemsize for o in outs
     )
     return pl.pallas_call(
-        kernel,
-        grid=(HK,),
+        run,
+        grid=(stop - start,),
         out_shape=outs,
         in_specs=[pl.BlockSpec(memory_space=pltpu.SMEM)] * len(lead)
-        + [spec(a.shape) for a in arrays],
+        + [spec(a.shape) for a in arrays]
+        + [pl.BlockSpec(memory_space=pl.ANY)] * len(into),
+        input_output_aliases={given + i: i for i in range(len(into))},
         out_specs=[spec(o.shape) for o in outs],
         scratch_shapes=scratch,
         compiler_params=pltpu.CompilerParams(vmem_limit_bytes=ATTENTION_LIMIT),
         cost_estimate=pl.CostEstimate(
-            flops=flops, bytes_accessed=moved, transcendentals=transcendentals
+            flops=flops * (stop - start) // HK,
+            bytes_accessed=moved * (stop - start) // HK,
+            transcendentals=transcendentals * (stop - start) // HK,
         ),
-    )(*lead, *arrays)
+    )(*lead, *arrays, *into)
 
 
 def share_kernel(which, pieces, own, columns, value_grad, part):
@@ -418,17 +429,8 @@
         n_grp,
     )
     weight_part = lax.ppermute(weight_part, "grp", [(i, i ^ 1) for i in range(n_grp)])
-    (weight_part,) = share(
-        combine_kernel, core, [value_grad], columns, [weight_part], [half], n_grp
-    )
-    weight_part = lax.psum_scatter(
-        weight_part,
-        "grp",
-        scatter_dimension=0,
-        axis_index_groups=[list(range(c, n_grp, 2)) for c in range(2)],
-        tiled=True,
-    )
-    output, query_grad, key_terms, key_term_own = attention(
+    backward = functools.partial(
+        attention,
         grads_kernel,
         [],
         [query, grad, probs, key_pieces, keys, fourth, values],
@@ -442,6 +444,18 @@
         4 * flops,
         0,
     )
+    weight_part, *grads = lax.optimization_barrier((weight_part, *backward(stop=HK // 2)))
+    (weight_part,) = share(
+        combine_kernel, core, [value_grad], columns, [weight_part], [half], n_grp
+    )
+    weight_part = lax.psum_scatter(
+        weight_part,
+        "grp",
+        scatter_dimension=0,
+        axis_index_groups=[list(range(c, n_grp, 2)) for c in range(2)],
+        tiled=True,
+    )
+    output, query_grad, key_terms, key_term_own = backward(start=HK // 2, into=grads)
     hidden_grad = dot(value_grad, weight, 1, 1).astype(BF)
     hidden_grad = hidden_grad.reshape(seg, n_grp, n_leaf, own_rows).transpose(0, 2, 1, 3)
     hidden_grad = with_layout_constraint(

time: 187 us -> 186 us (level)
  waiting for transfers between devices: 41.5 us -> 38.5 us
  Pallas kernels: 30.3 us -> 32.5 us
    ppermute x1, waiting for transfers between devices: 3.02 us -> 0.01 us  [shards(): lax.ppermute(weight_part, 'grp', [(i, i ^ 1) for i in range(n_grp)])]
    pallas_call x2 -> x3, Pallas kernels: 18.7 us -> 20.8 us  [attention(): pl.pallas_call(run, grid=(stop - start,), out_shape=outs, in_specs=[pl.Bl...]
  transfers between devices with their start and end apart: 6 -> 6, of which waited for: 4 -> 3; matrix products, arithmetic and copies ran while one was open for 4% -> 4% of each run, Pallas kernels for 11% -> 13%
where the time goes in v7:
time: 186 us; the launch traced here: 185 us
  blocking collectives  72.6 us (39%)
  waiting for transfers between devices  38.5 us (21%)
  Pallas kernels  32.5 us (17%)
  starting transfers between devices  15.7 us (8%)
  between operations  15 us (8%)
  local copies, waits for them, and re-layouts  6.09 us (3%)
  matrix products  4.2 us (2%)
    all_to_all x3, blocking collectives, swap(): return lax.all_to_all(array, 'leaf', 0, 0, tiled=True)  72.6 us
    all_to_all x3, waiting for transfers between devices, swap(): return lax.all_to_all(array, 'leaf', 0, 0, tiled=True)  38.5 us
    pallas_call x3, Pallas kernels, attention(): pl.pallas_call(run, grid=(stop - start,), out_shape=outs, in_specs=[pl.Bl...  20.8 us
    all_to_all x3, starting transfers between devices, swap(): return lax.all_to_all(array, 'leaf', 0, 0, tiled=True)  15.6 us
    pallas_call x7, Pallas kernels, plain(): pl.pallas_call(kernel, out_shape=outs, in_specs=[smem] * scalars + [vmem]...  8.45 us
    dot_general x2, matrix products, dot(): lax.dot_general(lhs, rhs, (((left,), (right,)), ((), ())), preferred_elem...  4.2 us
  transfers between devices with their start and end apart: 6, of which 3 were waited for; matrix products, arithmetic and copies ran while one was open for 4% of the time, Pallas kernels for 13%

profile of v7, /device:TPU:32, one launch (start us, length us, event | category | flops | bytes accessed | tf_op | source)
XLA Modules:
  0.0 185.3 jit_solution(11719471491694465442)
XLA Ops:
  7.2 0.0 all-gather.2.cloned.1.call-start
  7.9 1.8 shard_map.101
  9.7 28.4 %all_to_all.30.held = bf16[32,64,128]{2,1,0:T(8,128)(2,1)S(1)} all-to-all(bf16[32,64,128]{2,1,0:T(8,128)(2,1)} %shard_map.101), channel_id=1, replica_groups=mesh['leaf'=32,'grp'=8] {'leaf'}, dimensions={0} | all-to-all | bytes 1048576 | tf_op jit(solution)/shard_map/all_to_all | solution.py:350
  38.1 1.2 shard_map.104
  39.3 0.0 all-gather.2.cloned.1.call-update
  39.3 1.8 shard_map.102
  41.2 5.2 %all-to-all-start.1 = ((bf16[32,48,128]{2,1,0:T(8,128)(2,1)}), bf16[32,48,128]{2,1,0:T(8,128)(2,1)S(1)}, u32[]{:S(2)}, u32[]{:S(2)}) async-start(bf16[32,48,128]{2,1,0:T(8,128)(2,1)} %get-tuple-element.31), calls=%async_computation.1 | async-start | bytes 786432 | tf_op jit(solution)/shard_map/all_to_all | solution.py:350
  46.4 0.0 copy-done.7
  46.4 0.3 copy.19
  46.7 0.2 reshape.54
  46.9 0.2 copy.20
  47.1 0.2 reshape.55.columns
  47.4 0.1 ge.11
  47.5 0.1 and_reduce_fusion
  47.6 0.6 add_convert_fusion.refs_0_
  48.2 12.0 %all-to-all-done.1 = bf16[32,48,128]{2,1,0:T(8,128)(2,1)S(1)} async-done(((bf16[32,48,128]{2,1,0:T(8,128)(2,1)}), bf16[32,48,128]{2,1,0:T(8,128)(2,1)S(1)}, u32[]{:S(2)}, u32[]{:S(2)}) %all-to-all-start.1) | async-done | bytes 393248 | tf_op jit(solution)/shard_map/all_to_all | solution.py:350
  60.2 0.8 copy-done.4
  60.9 8.4 %shard_map.103 = (f32[4,512,1280]{2,1,0:T(8,128)}, bf16[8,4,48,128]{3,2,1,0:T(8,128)(2,1)}, bf16[128,512]{1,0:T(8,128)(2,1)}) custom-call(s32[3]{0:T(128)} %add_convert_fusion.refs_0_, bf16[128,5120]{1,0:T(8,128)(2,1)} %bitcast.32, bf16[128,5120]{1,0:T(8,128)(2,1)} %bitcast.35, bf16[8,4,48,128]{3,2,1,0:T(8,128)(2,1)} %bitcast.40, bf16[128,512]{1,0:T(8,128)(2,1)} %bitcast.47), custom_call_target="tpu_custom_call" | custom-call | flops 1342177280 | bytes 14155776 | tf_op jit(solution)/shard_map/pallas_call | solution.py:278
  69.3 0.0 all-gather.2.cloned.1.call-done
  69.4 2.4 %fusion.refs_6_ = bf16[128,512]{1,0:T(8,128)(2,1)S(1)} fusion(bf16[2560,512]{1,0:T(8,128)(2,1)} %all-gather.2.cloned.1.call-done, bf16[2560,128]{1,0:T(8,128)(2,1)S(1)} %reshape.55.columns), kind=kOutput, calls=%fused_computation.2 | convolution fusion | flops 335609856 | bytes 3407872 | tf_op jit(solution)/shard_map/dot_general | solution.py:198
  71.8 0.0 copy-done.8
  71.8 0.1 pad_maximum_fusion
  71.9 22.9 %all_to_all.31.held = bf16[32,64,128]{2,1,0:T(8,128)(2,1)S(1)} all-to-all(bf16[32,64,128]{2,1,0:T(8,128)(2,1)S(1)} %pad_maximum_fusion), channel_id=1, replica_groups=mesh['leaf'=32,'grp'=8] {'leaf'}, dimensions={0} | all-to-all | bytes 1048576 | tf_op jit(solution)/shard_map/all_to_all | solution.py:350
  94.8 1.6 shard_map.105
  96.4 5.2 %all-to-all-start.3 = ((bf16[32,64,128]{2,1,0:T(8,128)(2,1)}), bf16[32,64,128]{2,1,0:T(8,128)(2,1)S(1)}, u32[]{:S(2)}, u32[]{:S(2)}) async-start(bf16[32,64,128]{2,1,0:T(8,128)(2,1)} %shard_map.105), calls=%async_computation.3 | async-start | bytes 1048576 | tf_op jit(solution)/shard_map/all_to_all | solution.py:350
  101.6 0.0 reduce-scatter.2.cloned.1.call-start
  101.6 16.4 %all-to-all-done.3 = bf16[32,64,128]{2,1,0:T(8,128)(2,1)S(1)} async-done(((bf16[32,64,128]{2,1,0:T(8,128)(2,1)}), bf16[32,64,128]{2,1,0:T(8,128)(2,1)S(1)}, u32[]{:S(2)}, u32[]{:S(2)}) %all-to-all-start.3) | async-done | bytes 524320 | tf_op jit(solution)/shard_map/all_to_all | solution.py:350
  118.0 1.1 shard_map.106
  119.1 0.1 collective-permute-start
  119.2 6.1 %shard_map.107 = (bf16[128,5120]{1,0:T(8,128)(2,1)}, bf16[128,5120]{1,0:T(8,128)(2,1)}, bf16[8,4,48,128]{3,2,1,0:T(8,128)(2,1)}, bf16[128,512]{1,0:T(8,128)(2,1)}) custom-call(bf16[128,5120]{1,0:T(8,128)(2,1)} %bitcast.33, bf16[128,5120]{1,0:T(8,128)(2,1)} %bitcast.36, f32[4,512,1280]{2,1,0:T(8,128)} %get-tuple-element.32.refs_2_, ...), custom_call_target="tpu_custom_call" | custom-call | flops 1342177280 | bytes 8716288 | tf_op jit(solution)/shard_map/pallas_call | solution.py:278
  125.3 0.0 collective-permute-done.arrived
  125.3 2.2 %shard_map.109 = bf16[1280,512]{1,0:T(8,128)(2,1)} custom-call(s32[1]{0:T(128)S(6)} %select_n.7.which, bf16[128,512]{1,0:T(8,128)(2,1)S(1)} %get-tuple-element.46.value_grad, bf16[2560,128]{1,0:T(8,128)(2,1)S(1)} %reshape.55.columns, bf16[1280,512]{1,0:T(8,128)(2,1)S(1)} %collective-permute-done.arrived), custom_call_target="tpu_custom_call" | custom-call | flops 167772160 | bytes 1638400 | tf_op jit(solution)/shard_map/pallas_call | solution.py:325
  127.5 0.0 reduce-scatter.2.cloned.1.call-update
  127.5 6.3 %shard_map.108 = (bf16[128,5120]{1,0:T(8,128)(2,1)}, bf16[128,5120]{1,0:T(8,128)(2,1)}, bf16[8,4,48,128]{3,2,1,0:T(8,128)(2,1)}, bf16[128,512]{1,0:T(8,128)(2,1)}) custom-call(bf16[128,5120]{1,0:T(8,128)(2,1)} %bitcast.34, bf16[128,5120]{1,0:T(8,128)(2,1)} %bitcast.37, ...), custom_call_target="tpu_custom_call", output_to_operand_aliasing={{0}: (7, {}), {1}: (8, {}), {2}: (9, {}), {3}: (10, {})} | custom-call | flops 1342177280 | bytes 8716288 | tf_op jit(solution)/shard_map/pallas_call | solution.py:278
  133.8 5.1 %all-to-all-start.4 = ((bf16[32,48,128]{2,1,0:T(8,128)(2,1)}), bf16[32,48,128]{2,1,0:T(8,128)(2,1)S(1)}, u32[]{:S(2)}, u32[]{:S(2)}) async-start(bf16[32,48,128]{2,1,0:T(8,128)(2,1)} %bitcast.43), calls=%async_computation.5 | async-start | bytes 786432 | tf_op jit(solution)/shard_map/all_to_all | solution.py:350
  139.0 1.8 convolution_convert_fusion
  140.8 1.4 copy.23
  142.2 0.2 reshape.60
  142.4 0.3 copy.24
  142.7 0.2 reshape.61
  143.0 1.1 copy.25
  144.1 10.1 %all-to-all-done.4.held = bf16[32,48,128]{2,1,0:T(8,128)(2,1)S(1)} async-done(((bf16[32,48,128]{2,1,0:T(8,128)(2,1)}), bf16[32,48,128]{2,1,0:T(8,128)(2,1)S(1)}, u32[]{:S(2)}, u32[]{:S(2)}) %all-to-all-start.4) | async-done | bytes 393248 | tf_op jit(solution)/shard_map/all_to_all | solution.py:350
  154.2 0.8 shard_map.110.sums
  155.0 0.0 reduce-scatter.2.cloned.1.call-done.part
  155.0 1.0 copy-done.2
  156.0 0.5 shard_map.111
  156.5 21.3 %all_to_all.32.held = bf16[32,64,128]{2,1,0:T(8,128)(2,1)S(1)} all-to-all(bf16[32,64,128]{2,1,0:T(8,128)(2,1)S(1)} %shard_map.111), channel_id=1, replica_groups=mesh['leaf'=32,'grp'=8] {'leaf'}, dimensions={0} | all-to-all | bytes 1048576 | tf_op jit(solution)/shard_map/all_to_all | solution.py:350
  177.8 0.7 shard_map.112
  (18 shorter events, 0.1 us)
Async XLA Ops:
  7.2 62.2 %all-gather.2.cloned.1.call-start = ((), (), s32[]{:S(2)}) async-start(), calls=%async_computation.7 | async-start | bytes 2949120 | tf_op jit(solution)/shard_map/all_gather | solution.py:383
  38.0 8.3 %copy-start.7 = (bf16[1,128,2560]{2,1,0:T(8,128)(2,1)S(1)}, bf16[1,128,2560]{2,1,0:T(8,128)(2,1)}, u32[]{:S(2)}) copy-start(bf16[1,128,2560]{2,1,0:T(8,128)(2,1)} %param.6) | copy-start | bytes 1966084
  41.2 19.0 %all-to-all-start.1 = ((bf16[32,48,128]{2,1,0:T(8,128)(2,1)}), bf16[32,48,128]{2,1,0:T(8,128)(2,1)S(1)}, u32[]{:S(2)}, u32[]{:S(2)}) async-start(bf16[32,48,128]{2,1,0:T(8,128)(2,1)} %get-tuple-element.31), calls=%async_computation.1 | async-start | bytes 786432 | tf_op jit(solution)/shard_map/all_to_all | solution.py:350
  60.2 0.8 copy-start.4
  69.3 2.5 %copy-start.8 = (bf16[8,4,48,128]{3,2,1,0:T(8,128)(2,1)S(1)}, bf16[8,4,48,128]{3,2,1,0:T(8,128)(2,1)}, u32[]{:S(2)}) copy-start(bf16[8,4,48,128]{3,2,1,0:T(8,128)(2,1)} %get-tuple-element.33) | copy-start | bytes 1179652
  71.7 23.0 %copy-start.6 = (bf16[128,512]{1,0:T(8,128)(2,1)}, bf16[128,512]{1,0:T(8,128)(2,1)S(1)}, u32[]{:S(2)}) copy-start(bf16[128,512]{1,0:T(8,128)(2,1)S(1)} %fusion.refs_6_) | copy-start | bytes 393220
  94.8 23.3 %copy-start.3 = (bf16[128,512]{1,0:T(8,128)(2,1)S(1)}, bf16[128,512]{1,0:T(8,128)(2,1)}, u32[]{:S(2)}) copy-start(bf16[128,512]{1,0:T(8,128)(2,1)} %get-tuple-element.34.own) | copy-start | bytes 393220
  96.4 21.6 %all-to-all-start.3 = ((bf16[32,64,128]{2,1,0:T(8,128)(2,1)}), bf16[32,64,128]{2,1,0:T(8,128)(2,1)S(1)}, u32[]{:S(2)}, u32[]{:S(2)}) async-start(bf16[32,64,128]{2,1,0:T(8,128)(2,1)} %shard_map.105), calls=%async_computation.3 | async-start | bytes 1048576 | tf_op jit(solution)/shard_map/all_to_all | solution.py:350
  101.6 53.4 %reduce-scatter.2.cloned.1.call-start = ((), (), s32[]{:S(2)}) async-start(), calls=%async_computation.8 | async-start | bytes 1638400 | tf_op jit(solution)/shard_map/reduce_scatter | solution.py:451
  118.0 1.2 copy-start
  119.1 6.3 %collective-permute-start = (bf16[1280,512]{1,0:T(8,128)(2,1)S(1)}, bf16[1280,512]{1,0:T(8,128)(2,1)S(1)}, u32[]{:S(2)}, u32[]{:S(2)}) collective-permute-start(bf16[1280,512]{1,0:T(8,128)(2,1)S(1)} %get-tuple-element.35), channel_id=1, source_target_pairs={{0,1},{1,0},{2,3},{3,2},{4,5},{5,4},{6,7},{7,6},{8,9},{9,8},{10,11... | collective-permute-start | bytes 3932168 | tf_op jit(solution)/shard_map/ppermute | solution.py:431
  127.5 11.4 %copy-start.5 = (bf16[2560,512]{1,0:T(8,128)(2,1)S(1)}, bf16[2560,512]{1,0:T(8,128)(2,1)}, u32[]{:S(2)}) copy-start(bf16[2560,512]{1,0:T(8,128)(2,1)} %all-gather.2.cloned.1.call-done) | copy-start | bytes 7864324
  133.8 20.4 %all-to-all-start.4 = ((bf16[32,48,128]{2,1,0:T(8,128)(2,1)}), bf16[32,48,128]{2,1,0:T(8,128)(2,1)S(1)}, u32[]{:S(2)}, u32[]{:S(2)}) async-start(bf16[32,48,128]{2,1,0:T(8,128)(2,1)} %bitcast.43), calls=%async_computation.5 | async-start | bytes 786432 | tf_op jit(solution)/shard_map/all_to_all | solution.py:350
  144.1 33.7 %copy-start.1 = (bf16[128,512]{1,0:T(8,128)(2,1)S(1)}, bf16[128,512]{1,0:T(8,128)(2,1)}, u32[]{:S(2)}) copy-start(bf16[128,512]{1,0:T(8,128)(2,1)} %get-tuple-element.51.key_own) | copy-start | bytes 393220
  155.0 1.0 copy-start.2
Sparse Core Ops, SparseCore 0:
  39.4 25.3 all-gather.1
  127.7 22.6 reduce-scatter.1

commit v8 on v7

--- a/solution.py
+++ b/solution.py
@@ -221,7 +221,7 @@
 
 
 def probs_kernel(
-    present, query, grad, key_pieces, key_own, probs, value_pieces, value_own, bias, low
+    present, query, grad, key_pieces, key_own, probs, value_pieces, value_own, bias
 ):
     seg = query.shape[0]
     levels = masks_of(present, bias)
@@ -231,9 +231,8 @@
         scores = scores_of(keys, pair(query, index), levels, bias)
         weight = jnp.exp2(scores - jnp.max(scores, axis=0, keepdims=True))
         prob = weight * (1.0 / jnp.sum(weight, axis=0, keepdims=True))
-        probs[0, :, at] = prob
-        low[:, at] = prob.astype(BF)
-    put_rows(value_pieces, value_own, dot(low[...], heads_of(grad), 1, 0))
+        probs[0, :, at] = prob.astype(BF)
+    put_rows(value_pieces, value_own, dot(probs[0], heads_of(grad), 1, 0))
 
 
 def grads_kernel(
@@ -246,12 +245,13 @@
     keys_t, values_t = keys.T, values.T
     for index in range(GROUPS // 2):
         at = slice(index * 2 * seg, (index + 1) * 2 * seg)
-        prob = probs[0, :, at]
+        prob_low = probs[0, :, at]
+        prob = prob_low.astype(F32)
         dprob = dot(values, pair(grad, index), 1, 1)
-        delta = jnp.sum(prob * dprob, axis=0, keepdims=True)
+        delta = jnp.sum(prob * dprob, axis=0, keepdims=True) / jnp.sum(prob, axis=0, keepdims=True)
         dscore = (prob * (dprob - delta)).astype(BF)
         low[:, at] = dscore
-        put_pair(output, index, dot(values_t, prob.astype(BF), 1, 0).astype(BF).T)
+        put_pair(output, index, dot(values_t, prob_low, 1, 0).astype(BF).T)
         put_pair(query_grad, index, (dot(keys_t, dscore, 1, 0) * (1.0 / DH**0.5)).astype(BF).T)
     total = dot(low[...], heads_of(query), 1, 0)
     put_rows(grad_pieces, grad_own, total * (1.0 / DH**0.5))
@@ -401,11 +401,11 @@
         [present],
         [query, grad, key_pieces, keys],
         [
-            shape((HK, 4 * seg, GROUPS * seg), F32),
+            shape((HK, 4 * seg, GROUPS * seg), BF),
             shape((blocks, HK, slots, DH), BF),
             shape((seg, width), BF),
         ],
-        [pltpu.VMEM((seg, 2 * seg), F32), pltpu.VMEM((4 * seg, GROUPS * seg), BF)],
+        [pltpu.VMEM((seg, 2 * seg), F32)],
         2 * flops,
         HQ * seg * 4 * seg,
     )

time: 186 us -> 186 us (level)
  transfers between devices with their start and end apart: 6 -> 6, of which waited for: 3 -> 3; matrix products, arithmetic and copies ran while one was open for 4% -> 4% of each run, Pallas kernels for 13% -> 12%
where the time goes in v8:
time: 186 us; the launch traced here: 185 us
  blocking collectives  73.6 us (40%)
  waiting for transfers between devices  38.5 us (21%)
  Pallas kernels  31.3 us (17%)
  starting transfers between devices  15.7 us (8%)
  between operations  15 us (8%)
  local copies, waits for them, and re-layouts  6.06 us (3%)
  matrix products  4.2 us (2%)
    all_to_all x3, blocking collectives, swap(): return lax.all_to_all(array, 'leaf', 0, 0, tiled=True)  73.6 us
    all_to_all x3, waiting for transfers between devices, swap(): return lax.all_to_all(array, 'leaf', 0, 0, tiled=True)  38.5 us
    pallas_call x3, Pallas kernels, attention(): pl.pallas_call(run, grid=(stop - start,), out_shape=outs, in_specs=[pl.Bl...  19.5 us
    all_to_all x3, starting transfers between devices, swap(): return lax.all_to_all(array, 'leaf', 0, 0, tiled=True)  15.5 us
    pallas_call x7, Pallas kernels, plain(): pl.pallas_call(kernel, out_shape=outs, in_specs=[smem] * scalars + [vmem]...  8.45 us
    dot_general x2, matrix products, dot(): lax.dot_general(lhs, rhs, (((left,), (right,)), ((), ())), preferred_elem...  4.2 us
  transfers between devices with their start and end apart: 6, of which 3 were waited for; matrix products, arithmetic and copies ran while one was open for 4% of the time, Pallas kernels for 12%

profile of v8, /device:TPU:32, one launch (start us, length us, event | category | flops | bytes accessed | tf_op | source)
XLA Modules:
  0.0 185.0 jit_solution(16932518642586351660)
XLA Ops:
  7.2 0.0 all-gather.2.cloned.1.call-start
  7.9 1.8 shard_map.101
  9.7 28.4 %all_to_all.30.held = bf16[32,64,128]{2,1,0:T(8,128)(2,1)S(1)} all-to-all(bf16[32,64,128]{2,1,0:T(8,128)(2,1)} %shard_map.101), channel_id=1, replica_groups=mesh['leaf'=32,'grp'=8] {'leaf'}, dimensions={0} | all-to-all | bytes 1048576 | tf_op jit(solution)/shard_map/all_to_all | solution.py:350
  38.1 1.2 shard_map.104
  39.3 0.0 all-gather.2.cloned.1.call-update
  39.3 1.8 shard_map.102
  41.2 5.2 %all-to-all-start.1 = ((bf16[32,48,128]{2,1,0:T(8,128)(2,1)}), bf16[32,48,128]{2,1,0:T(8,128)(2,1)S(1)}, u32[]{:S(2)}, u32[]{:S(2)}) async-start(bf16[32,48,128]{2,1,0:T(8,128)(2,1)} %get-tuple-element.31), calls=%async_computation.1 | async-start | bytes 786432 | tf_op jit(solution)/shard_map/all_to_all | solution.py:350
  46.4 0.0 copy-done.7
  46.4 0.3 copy.19
  46.7 0.2 reshape.54
  46.9 0.2 copy.20
  47.1 0.2 reshape.55.columns
  47.4 0.1 ge.11
  47.5 0.1 and_reduce_fusion
  47.6 0.6 add_convert_fusion.refs_0_
  48.2 12.0 %all-to-all-done.1 = bf16[32,48,128]{2,1,0:T(8,128)(2,1)S(1)} async-done(((bf16[32,48,128]{2,1,0:T(8,128)(2,1)}), bf16[32,48,128]{2,1,0:T(8,128)(2,1)S(1)}, u32[]{:S(2)}, u32[]{:S(2)}) %all-to-all-start.1) | async-done | bytes 393248 | tf_op jit(solution)/shard_map/all_to_all | solution.py:350
  60.2 0.7 copy-done.4
  60.9 7.8 %shard_map.103 = (bf16[4,512,1280]{2,1,0:T(8,128)(2,1)}, bf16[8,4,48,128]{3,2,1,0:T(8,128)(2,1)}, bf16[128,512]{1,0:T(8,128)(2,1)}) custom-call(s32[3]{0:T(128)} %add_convert_fusion.refs_0_, bf16[128,5120]{1,0:T(8,128)(2,1)} %bitcast.32, bf16[128,5120]{1,0:T(8,128)(2,1)} %bitcast.35, bf16[8,4,48,128]{3,2,1,0:T(8,128)(2,1)} %bitcast.40, bf16[128,512]{1,0:T(8,128)(2,1)} %bitcast.47), custom_call_target="tpu_custom_call" | custom-call | flops 1342177280 | bytes 8912896 | tf_op jit(solution)/shard_map/pallas_call | solution.py:278
  68.8 0.0 all-gather.2.cloned.1.call-done
  68.8 2.4 %fusion.refs_6_ = bf16[128,512]{1,0:T(8,128)(2,1)S(1)} fusion(bf16[2560,512]{1,0:T(8,128)(2,1)} %all-gather.2.cloned.1.call-done, bf16[2560,128]{1,0:T(8,128)(2,1)S(1)} %reshape.55.columns), kind=kOutput, calls=%fused_computation.2 | convolution fusion | flops 335609856 | bytes 3407872 | tf_op jit(solution)/shard_map/dot_general | solution.py:198
  71.2 0.0 copy-start.6
  71.3 0.1 pad_maximum_fusion
  71.3 23.4 %all_to_all.31.held = bf16[32,64,128]{2,1,0:T(8,128)(2,1)S(1)} all-to-all(bf16[32,64,128]{2,1,0:T(8,128)(2,1)S(1)} %pad_maximum_fusion), channel_id=1, replica_groups=mesh['leaf'=32,'grp'=8] {'leaf'}, dimensions={0} | all-to-all | bytes 1048576 | tf_op jit(solution)/shard_map/all_to_all | solution.py:350
  94.8 1.6 shard_map.105
  96.4 5.2 %all-to-all-start.3 = ((bf16[32,64,128]{2,1,0:T(8,128)(2,1)}), bf16[32,64,128]{2,1,0:T(8,128)(2,1)S(1)}, u32[]{:S(2)}, u32[]{:S(2)}) async-start(bf16[32,64,128]{2,1,0:T(8,128)(2,1)} %shard_map.105), calls=%async_computation.3 | async-start | bytes 1048576 | tf_op jit(solution)/shard_map/all_to_all | solution.py:350
  101.6 0.0 reduce-scatter.2.cloned.1.call-start
  101.6 16.4 %all-to-all-done.3 = bf16[32,64,128]{2,1,0:T(8,128)(2,1)S(1)} async-done(((bf16[32,64,128]{2,1,0:T(8,128)(2,1)}), bf16[32,64,128]{2,1,0:T(8,128)(2,1)S(1)}, u32[]{:S(2)}, u32[]{:S(2)}) %all-to-all-start.3) | async-done | bytes 524320 | tf_op jit(solution)/shard_map/all_to_all | solution.py:350
  118.0 1.1 shard_map.106
  119.1 0.1 collective-permute-start
  119.2 5.8 %shard_map.107 = (bf16[128,5120]{1,0:T(8,128)(2,1)}, bf16[128,5120]{1,0:T(8,128)(2,1)}, bf16[8,4,48,128]{3,2,1,0:T(8,128)(2,1)}, bf16[128,512]{1,0:T(8,128)(2,1)}) custom-call(bf16[128,5120]{1,0:T(8,128)(2,1)} %bitcast.33, bf16[128,5120]{1,0:T(8,128)(2,1)} %bitcast.36, bf16[4,512,1280]{2,1,0:T(8,128)(2,1)} %get-tuple-element.32.refs_2_, ...), custom_call_target="tpu_custom_call" | custom-call | flops 1342177280 | bytes 6094848 | tf_op jit(solution)/shard_map/pallas_call | solution.py:278
  124.9 0.0 collective-permute-done.arrived
  124.9 2.3 %shard_map.109 = bf16[1280,512]{1,0:T(8,128)(2,1)} custom-call(s32[1]{0:T(128)S(6)} %select_n.7.which, bf16[128,512]{1,0:T(8,128)(2,1)S(1)} %get-tuple-element.46.value_grad, bf16[2560,128]{1,0:T(8,128)(2,1)S(1)} %reshape.55.columns, bf16[1280,512]{1,0:T(8,128)(2,1)S(1)} %collective-permute-done.arrived), custom_call_target="tpu_custom_call" | custom-call | flops 167772160 | bytes 1638400 | tf_op jit(solution)/shard_map/pallas_call | solution.py:325
  127.2 0.0 reduce-scatter.2.cloned.1.call-update
  127.3 5.9 %shard_map.108 = (bf16[128,5120]{1,0:T(8,128)(2,1)}, bf16[128,5120]{1,0:T(8,128)(2,1)}, bf16[8,4,48,128]{3,2,1,0:T(8,128)(2,1)}, bf16[128,512]{1,0:T(8,128)(2,1)}) custom-call(bf16[128,5120]{1,0:T(8,128)(2,1)} %bitcast.34, bf16[128,5120]{1,0:T(8,128)(2,1)} %bitcast.37, ...), custom_call_target="tpu_custom_call", output_to_operand_aliasing={{0}: (7, {}), {1}: (8, {}), {2}: (9, {}), {3}: (10, {})} | custom-call | flops 1342177280 | bytes 6094848 | tf_op jit(solution)/shard_map/pallas_call | solution.py:278
  133.1 5.1 %all-to-all-start.4 = ((bf16[32,48,128]{2,1,0:T(8,128)(2,1)}), bf16[32,48,128]{2,1,0:T(8,128)(2,1)S(1)}, u32[]{:S(2)}, u32[]{:S(2)}) async-start(bf16[32,48,128]{2,1,0:T(8,128)(2,1)} %bitcast.43), calls=%async_computation.5 | async-start | bytes 786432 | tf_op jit(solution)/shard_map/all_to_all | solution.py:350
  138.3 1.8 convolution_convert_fusion
  140.1 1.4 copy.23
  141.5 0.2 reshape.60
  141.7 0.3 copy.24
  142.0 0.2 reshape.61
  142.3 1.1 copy.25
  143.4 10.1 %all-to-all-done.4.held = bf16[32,48,128]{2,1,0:T(8,128)(2,1)S(1)} async-done(((bf16[32,48,128]{2,1,0:T(8,128)(2,1)}), bf16[32,48,128]{2,1,0:T(8,128)(2,1)S(1)}, u32[]{:S(2)}, u32[]{:S(2)}) %all-to-all-start.4) | async-done | bytes 393248 | tf_op jit(solution)/shard_map/all_to_all | solution.py:350
  153.5 0.8 shard_map.110.sums
  154.3 0.0 reduce-scatter.2.cloned.1.call-done.part
  154.3 1.0 copy-done.2
  155.3 0.5 shard_map.111
  155.8 21.7 %all_to_all.32.held = bf16[32,64,128]{2,1,0:T(8,128)(2,1)S(1)} all-to-all(bf16[32,64,128]{2,1,0:T(8,128)(2,1)S(1)} %shard_map.111), channel_id=1, replica_groups=mesh['leaf'=32,'grp'=8] {'leaf'}, dimensions={0} | all-to-all | bytes 1048576 | tf_op jit(solution)/shard_map/all_to_all | solution.py:350
  177.5 0.7 shard_map.112
  (18 shorter events, 0.1 us)
Async XLA Ops:
  7.2 61.6 %all-gather.2.cloned.1.call-start = ((), (), s32[]{:S(2)}) async-start(), calls=%async_computation.7 | async-start | bytes 2949120 | tf_op jit(solution)/shard_map/all_gather | solution.py:383
  38.0 8.3 %copy-start.7 = (bf16[1,128,2560]{2,1,0:T(8,128)(2,1)S(1)}, bf16[1,128,2560]{2,1,0:T(8,128)(2,1)}, u32[]{:S(2)}) copy-start(bf16[1,128,2560]{2,1,0:T(8,128)(2,1)} %param.6) | copy-start | bytes 1966084
  41.2 19.0 %all-to-all-start.1 = ((bf16[32,48,128]{2,1,0:T(8,128)(2,1)}), bf16[32,48,128]{2,1,0:T(8,128)(2,1)S(1)}, u32[]{:S(2)}, u32[]{:S(2)}) async-start(bf16[32,48,128]{2,1,0:T(8,128)(2,1)} %get-tuple-element.31), calls=%async_computation.1 | async-start | bytes 786432 | tf_op jit(solution)/shard_map/all_to_all | solution.py:350
  60.2 0.7 copy-start.4
  68.8 2.5 %copy-start.8 = (bf16[8,4,48,128]{3,2,1,0:T(8,128)(2,1)S(1)}, bf16[8,4,48,128]{3,2,1,0:T(8,128)(2,1)}, u32[]{:S(2)}) copy-start(bf16[8,4,48,128]{3,2,1,0:T(8,128)(2,1)} %get-tuple-element.33) | copy-start | bytes 1179652
  71.2 23.6 %copy-start.6 = (bf16[128,512]{1,0:T(8,128)(2,1)}, bf16[128,512]{1,0:T(8,128)(2,1)S(1)}, u32[]{:S(2)}) copy-start(bf16[128,512]{1,0:T(8,128)(2,1)S(1)} %fusion.refs_6_) | copy-start | bytes 393220
  94.8 23.3 %copy-start.3 = (bf16[128,512]{1,0:T(8,128)(2,1)S(1)}, bf16[128,512]{1,0:T(8,128)(2,1)}, u32[]{:S(2)}) copy-start(bf16[128,512]{1,0:T(8,128)(2,1)} %get-tuple-element.34.own) | copy-start | bytes 393220
  96.4 21.6 %all-to-all-start.3 = ((bf16[32,64,128]{2,1,0:T(8,128)(2,1)}), bf16[32,64,128]{2,1,0:T(8,128)(2,1)S(1)}, u32[]{:S(2)}, u32[]{:S(2)}) async-start(bf16[32,64,128]{2,1,0:T(8,128)(2,1)} %shard_map.105), calls=%async_computation.3 | async-start | bytes 1048576 | tf_op jit(solution)/shard_map/all_to_all | solution.py:350
  101.6 52.7 %reduce-scatter.2.cloned.1.call-start = ((), (), s32[]{:S(2)}) async-start(), calls=%async_computation.8 | async-start | bytes 1638400 | tf_op jit(solution)/shard_map/reduce_scatter | solution.py:451
  118.0 1.2 copy-start
  119.1 5.9 %collective-permute-start = (bf16[1280,512]{1,0:T(8,128)(2,1)S(1)}, bf16[1280,512]{1,0:T(8,128)(2,1)S(1)}, u32[]{:S(2)}, u32[]{:S(2)}) collective-permute-start(bf16[1280,512]{1,0:T(8,128)(2,1)S(1)} %get-tuple-element.35), channel_id=1, source_target_pairs={{0,1},{1,0},{2,3},{3,2},{4,5},{5,4},{6,7},{7,6},{8,9},{9,8},{10,11... | collective-permute-start | bytes 3932168 | tf_op jit(solution)/shard_map/ppermute | solution.py:431
  127.2 11.0 %copy-start.5 = (bf16[2560,512]{1,0:T(8,128)(2,1)S(1)}, bf16[2560,512]{1,0:T(8,128)(2,1)}, u32[]{:S(2)}) copy-start(bf16[2560,512]{1,0:T(8,128)(2,1)} %all-gather.2.cloned.1.call-done) | copy-start | bytes 7864324
  133.1 20.4 %all-to-all-start.4 = ((bf16[32,48,128]{2,1,0:T(8,128)(2,1)}), bf16[32,48,128]{2,1,0:T(8,128)(2,1)S(1)}, u32[]{:S(2)}, u32[]{:S(2)}) async-start(bf16[32,48,128]{2,1,0:T(8,128)(2,1)} %bitcast.43), calls=%async_computation.5 | async-start | bytes 786432 | tf_op jit(solution)/shard_map/all_to_all | solution.py:350
  143.4 34.1 %copy-start.1 = (bf16[128,512]{1,0:T(8,128)(2,1)S(1)}, bf16[128,512]{1,0:T(8,128)(2,1)}, u32[]{:S(2)}) copy-start(bf16[128,512]{1,0:T(8,128)(2,1)} %get-tuple-element.51.key_own) | copy-start | bytes 393220
  154.3 1.0 copy-start.2
Sparse Core Ops, SparseCore 0:
  39.4 25.3 all-gather.1
  127.4 22.7 reduce-scatter.1
